TPU v7x, 32 devices: a whole 2x2x4 slice. The times are simulated.
32 devices in a mesh: grp: 2 (over x), tm: 16 (over z, y, core).
Axes of the slice: x: 2, y: 2, z: 4, core: 2. Of those that a mesh axis runs over, the one named last changes fastest.
Arguments:
- upsampled: bfloat16 [2, 12288, 512], P(None, ('grp', 'tm')), parts along dimension 1, may hold values from -6 to 6
- taps: bfloat16 [3, 7, 512, 512], replicated, may hold values from -0.09375 to 0.09375
- bias_wide: float32 [3, 512], replicated, may hold values from -1.8 to 1.8
- pointwise: bfloat16 [3, 512, 512], replicated, may hold values from -0.25 to 0.25
- bias_point: float32 [3, 512], replicated, may hold values from -1.8 to 1.8
- alpha_in: float32 [3, 512], replicated, may hold values from 0.5 to 4
- beta_in: float32 [3, 512], replicated, may hold values from 0.5 to 4
- alpha_mid: float32 [3, 512], replicated, may hold values from 0.5 to 4
- beta_mid: float32 [3, 512], replicated, may hold values from 0.5 to 4
Outputs:
- decoded: bfloat16 [12288, 512], P(('grp', 'tm')), parts along dimension 0
There are 2 independent parts, one for each index of `grp`. A program takes and returns all parts, laid end to end along the dimension named above; an argument that names none is the same for every part. Nothing has to cross between parts.
All inputs are finite; a program needn't handle non-finite values.
Results may differ from a plain program's by a relative error of at most 0.027.
The roundings to bfloat16 on the way count: a program that leaves them out, or rounds other values in their place, can miss the bound.
Values may be sent and summed in bfloat16 or wider, within the bound.
No kernel may reach another device: no remote copies, remote signals or barrier semaphores. Data moves between devices by JAX's collectives and lax.ppermute only.
A program may use at most 128 MiB of HBM per device.

v0:
```python
import jax
import jax.numpy as jnp
from jax import lax
from jax.sharding import PartitionSpec as P

KERNEL = 7
STRIDE = 8
UNITS = 3


def passed_along(value, axis, steps):
    count = lax.axis_size(axis)
    first, last = (max(0, -steps), min(count, count - steps))
    return lax.ppermute(value, axis, [(source, source + steps) for source in range(first, last)])


def with_halo(block, sides, width):
    for axis, dim in sides:
        count = lax.axis_size(axis)
        forward = [(i, i + 1) for i in range(count - 1)]
        backward = [(target, source) for source, target in forward]
        low = lax.ppermute(
            lax.slice_in_dim(block, block.shape[dim] - width, None, axis=dim), axis, forward
        )
        high = lax.ppermute(lax.slice_in_dim(block, 0, width, axis=dim), axis, backward)
        block = jnp.concatenate([low, block, high], axis=dim)
    return block


def snake(values, alpha, beta):
    return values + jnp.square(jnp.sin(alpha * values)) / beta


def residual_unit(
    inputs, dilation, taps, bias_wide, pointwise, bias_point, alpha_in, beta_in, alpha_mid, beta_mid
):
    length = inputs.shape[0] - 6 * dilation
    widened = snake(inputs.astype(jnp.float32), alpha_in, beta_in).astype(jnp.bfloat16)
    stacked = jnp.concatenate(
        [widened[k * dilation : k * dilation + length] for k in range(KERNEL)], axis=1
    )
    kernel = taps.reshape(KERNEL * taps.shape[1], taps.shape[2])
    middle = jnp.dot(stacked, kernel, preferred_element_type=jnp.float32) + bias_wide
    gated = snake(middle, alpha_mid, beta_mid).astype(jnp.bfloat16)
    update = jnp.dot(gated, pointwise, preferred_element_type=jnp.float32) + bias_point
    kept = inputs[3 * dilation : 3 * dilation + length].astype(jnp.float32)
    return (kept + update).astype(jnp.bfloat16)


def per_device(
    upsampled, taps, bias_wide, pointwise, bias_point, alpha_in, beta_in, alpha_mid, beta_mid
):
    frames = upsampled.shape[1]
    dilations = (1, 3, 9)
    carried = passed_along(upsampled[1, frames - STRIDE :], "tm", 1)
    later = jnp.concatenate([carried, upsampled[1, : frames - STRIDE]], axis=0)
    current = (upsampled[0].astype(jnp.float32) + later.astype(jnp.float32)).astype(jnp.bfloat16)
    for index in range(UNITS):
        padded = with_halo(current, (("tm", 0),), 3 * dilations[index])
        current = residual_unit(
            padded,
            dilations[index],
            taps[index],
            bias_wide[index],
            pointwise[index],
            bias_point[index],
            alpha_in[index],
            beta_in[index],
            alpha_mid[index],
            beta_mid[index],
        )
    return current


def solution(mesh):
    placed = (P(None, ("grp", "tm"), None), P(), P(), P(), P(), P(), P(), P(), P())
    return jax.shard_map(
        per_device, mesh=mesh, in_specs=placed, out_specs=P(("grp", "tm"), None), check_vma=False
    )
```

profile of v0, /device:TPU:5, one launch (start us, length us, event | category | flops | bytes accessed | tf_op | source)
XLA Modules:
  0.0 73.5 jit_solution(8115087615131059547)
XLA Ops:
  0.0 0.7 slice_bitcast_fusion.1
  0.7 3.7 %collective-permute-start = (bf16[8,512]{1,0:T(8,128)(2,1)S(1)}, bf16[8,512]{1,0:T(8,128)(2,1)S(1)}, u32[]{:S(2)}, u32[]{:S(2)}) collective-permute-start(bf16[8,512]{1,0:T(8,128)(2,1)S(1)} %slice_bitcast_fusion.1), channel_id=1, source_target_pairs={{0,1},{1,2},{2,3},{3,4},{4,5},{5,6},{6,7},{7,8},{8,9},{9,10},{10,1... | collective-permute-start | bytes 24584 | tf_op jit(solution)/shard_map/ppermute | solution.py:14
  4.4 1.0 %slice_bitcast_fusion = bf16[376,512]{1,0:T(8,128)(2,1)S(1)} fusion(bf16[2,384,512]{2,1,0:T(8,128)(2,1)} %param.9), kind=kLoop, calls=%fused_computation.71 | loop fusion | bytes 770048 | tf_op jit(solution)/shard_map/squeeze | solution.py:56
  5.4 1.4 %fusion.38 = (f32[1,512]{1,0:T(1,128)}, f32[1,512]{1,0:T(1,128)}, f32[1,512]{1,0:T(1,128)}) fusion(f32[3,512]{1,0:T(4,128)} %param.11), kind=kLoop, calls=%fused_computation.77 | loop fusion | bytes 12288 | tf_op jit(solution)/shard_map/slice | solution.py:64
  6.8 1.4 %fusion.41 = (f32[1,512]{1,0:T(1,128)}, f32[1,512]{1,0:T(1,128)}, f32[1,512]{1,0:T(1,128)}) fusion(f32[3,512]{1,0:T(4,128)} %param.13), kind=kLoop, calls=%fused_computation.80 | loop fusion | bytes 12288 | tf_op jit(solution)/shard_map/slice | solution.py:66
  8.2 0.8 %fusion.42 = (f32[1,512]{1,0:T(1,128)S(1)}, f32[1,512]{1,0:T(1,128)S(1)}, f32[1,512]{1,0:T(1,128)S(1)}) fusion(f32[3,512]{1,0:T(4,128)} %param.14), kind=kLoop, calls=%fused_computation.81 | loop fusion | bytes 12288 | tf_op jit(solution)/shard_map/slice | solution.py:67
  9.1 0.8 %fusion.43 = (f32[1,512]{1,0:T(1,128)S(1)}, f32[1,512]{1,0:T(1,128)S(1)}, f32[1,512]{1,0:T(1,128)S(1)}) fusion(f32[3,512]{1,0:T(4,128)} %param.15), kind=kLoop, calls=%fused_computation.82 | loop fusion | bytes 12288 | tf_op jit(solution)/shard_map/slice | solution.py:68
  9.9 7.4 %fusion.34 = (bf16[1,7,512,512]{3,2,1,0:T(8,128)(2,1)}, bf16[1,7,512,512]{3,2,1,0:T(8,128)(2,1)}, bf16[1,7,512,512]{3,2,1,0:T(8,128)(2,1)}) fusion(bf16[3,7,512,512]{3,2,1,0:T(8,128)(2,1)} %param.10), kind=kLoop, calls=%fused_computation.73 | loop fusion | bytes 22020096 | tf_op jit(solution)/shard_map/slice | solution.py:63
  17.3 0.6 fusion.39
  17.9 0.1 fusion.18
  18.0 1.9 %collective-permute-start.1 = (bf16[3,512]{1,0:T(4,128)(2,1)S(1)}, bf16[3,512]{1,0:T(4,128)(2,1)S(1)}, u32[]{:S(2)}, u32[]{:S(2)}) collective-permute-start(bf16[3,512]{1,0:T(4,128)(2,1)S(1)} %get-tuple-element.12), channel_id=1, source_target_pairs={{0,1},{1,2},{2,3},{3,4},{4,5},{5,6},{6,7},{7,8},{8,9},{9,10},{10,1... | collective-permute-start | bytes 9224 | tf_op jit(solution)/shard_map/ppermute | solution.py:22
  20.0 2.4 %collective-permute-start.2 = (bf16[3,512]{1,0:T(4,128)(2,1)S(1)}, bf16[3,512]{1,0:T(4,128)(2,1)S(1)}, u32[]{:S(2)}, u32[]{:S(2)}) collective-permute-start(bf16[3,512]{1,0:T(4,128)(2,1)S(1)} %get-tuple-element.13), channel_id=1, source_target_pairs={{1,0},{2,1},{3,2},{4,3},{5,4},{6,5},{7,6},{8,7},{9,8},{10,9},{11,1... | collective-permute-start | bytes 9224 | tf_op jit(solution)/shard_map/ppermute | solution.py:25
  22.4 0.6 fusion.40
  23.0 2.8 %collective-permute-done.2 = bf16[3,512]{1,0:T(4,128)(2,1)S(1)} collective-permute-done((bf16[3,512]{1,0:T(4,128)(2,1)S(1)}, bf16[3,512]{1,0:T(4,128)(2,1)S(1)}, u32[]{:S(2)}, u32[]{:S(2)}) %collective-permute-start.2) | collective-permute-done | bytes 3104 | tf_op jit(solution)/shard_map/ppermute | solution.py:25
  25.8 2.8 %fusion.17 = bf16[390,512]{1,0:T(8,128)(2,1)S(1)} fusion(bf16[3,512]{1,0:T(4,128)(2,1)S(1)} %collective-permute-done.2, bf16[384,512]{1,0:T(8,128)(2,1)S(1)} %fusion.18, bf16[3,512]{1,0:T(4,128)(2,1)S(1)} %collective-permute-done.1, f32[512]{0:T(512)S(1)} %bitcast.51, f32[512]{0:T(512)S(1)} %bitcast.50), kind=kLoop, calls=%fused_computation.29 | loop fusion | flops 2196480 | bytes 802816 | tf_op jit(solution)/shard_map/convert_element_type | solution.py:38
  28.7 0.1 slice_dynamic-update-slice_fusion.19
  28.8 0.1 slice_dynamic-update-slice_fusion.18
  28.9 0.1 slice_dynamic-update-slice_fusion.17
  29.0 0.1 slice_dynamic-update-slice_fusion.16
  29.1 0.1 slice_dynamic-update-slice_fusion.15
  29.2 0.1 slice_dynamic-update-slice_fusion.14
  29.3 6.5 %fusion.5 = bf16[384,512]{1,0:T(8,128)(2,1)S(1)} fusion(bf16[384,3584]{1,0:T(8,128)(2,1)S(1)} %slice_dynamic-update-slice_fusion.14, bf16[3584,512]{1,0:T(8,128)(2,1)} %bitcast.45, bf16[384,512]{1,0:T(8,128)(2,1)S(1)} %fusion.18, bf16[3,512,512]{2,1,0:T(8,128)(2,1)} %param.12, f32[512]{0:T(512)} %bitcast.61, f32[512]{0:T(512)} %bitcast.63, ...), kind=kOutput, calls=%fused_computation.11 | convolution fusion | flops 1612578816 | bytes 7741440 | tf_op jit(solution)/shard_map/dot_general | solution.py:45
  35.8 1.9 %collective-permute-start.3 = (bf16[9,512]{1,0:T(8,128)(2,1)S(1)}, bf16[9,512]{1,0:T(8,128)(2,1)S(1)}, u32[]{:S(2)}, u32[]{:S(2)}) collective-permute-start(bf16[9,512]{1,0:T(8,128)(2,1)S(1)} %get-tuple-element.10), channel_id=1, source_target_pairs={{0,1},{1,2},{2,3},{3,4},{4,5},{5,6},{6,7},{7,8},{8,9},{9,10},{10,1... | collective-permute-start | bytes 27656 | tf_op jit(solution)/shard_map/ppermute | solution.py:22
  37.7 2.6 %collective-permute-start.4 = (bf16[9,512]{1,0:T(8,128)(2,1)S(1)}, bf16[9,512]{1,0:T(8,128)(2,1)S(1)}, u32[]{:S(2)}, u32[]{:S(2)}) collective-permute-start(bf16[9,512]{1,0:T(8,128)(2,1)S(1)} %get-tuple-element.11), channel_id=1, source_target_pairs={{1,0},{2,1},{3,2},{4,3},{5,4},{6,5},{7,6},{8,7},{9,8},{10,9},{11,1... | collective-permute-start | bytes 27656 | tf_op jit(solution)/shard_map/ppermute | solution.py:25
  40.3 3.4 %collective-permute-done.4 = bf16[9,512]{1,0:T(8,128)(2,1)S(1)} collective-permute-done((bf16[9,512]{1,0:T(8,128)(2,1)S(1)}, bf16[9,512]{1,0:T(8,128)(2,1)S(1)}, u32[]{:S(2)}, u32[]{:S(2)}) %collective-permute-start.4) | collective-permute-done | bytes 9248 | tf_op jit(solution)/shard_map/ppermute | solution.py:25
  43.7 3.4 %fusion.13 = bf16[402,512]{1,0:T(8,128)(2,1)S(1)} fusion(bf16[9,512]{1,0:T(8,128)(2,1)S(1)} %collective-permute-done.4, bf16[384,512]{1,0:T(8,128)(2,1)S(1)} %fusion.5, bf16[9,512]{1,0:T(8,128)(2,1)S(1)} %collective-permute-done.3, f32[512]{0:T(512)S(1)} %bitcast.49, f32[512]{0:T(512)S(1)} %bitcast.48), kind=kLoop, calls=%fused_computation.25 | loop fusion | flops 2264064 | bytes 827392 | tf_op jit(solution)/shard_map/convert_element_type | solution.py:38
  47.8 6.5 %fusion.4 = bf16[384,512]{1,0:T(8,128)(2,1)S(1)} fusion(bf16[384,3584]{1,0:T(8,128)(2,1)S(1)} %slice_dynamic-update-slice_fusion.7, bf16[3584,512]{1,0:T(8,128)(2,1)} %bitcast.44, bf16[384,512]{1,0:T(8,128)(2,1)S(1)} %fusion.5, bf16[3,512,512]{2,1,0:T(8,128)(2,1)} %param.12, f32[512]{0:T(512)S(1)} %bitcast.57, f32[512]{0:T(512)} %bitcast.59, ...), kind=kOutput, calls=%fused_computation.10 | convolution fusion | flops 1612578816 | bytes 7741440 | tf_op jit(solution)/shard_map/dot_general | solution.py:45
  54.3 1.9 %collective-permute-start.5 = (bf16[27,512]{1,0:T(8,128)(2,1)S(1)}, bf16[27,512]{1,0:T(8,128)(2,1)S(1)}, u32[]{:S(2)}, u32[]{:S(2)}) collective-permute-start(bf16[27,512]{1,0:T(8,128)(2,1)S(1)} %get-tuple-element.8), channel_id=1, source_target_pairs={{0,1},{1,2},{2,3},{3,4},{4,5},{5,6},{6,7},{7,8},{8,9},{9,10},{10,1... | collective-permute-start | bytes 82952 | tf_op jit(solution)/shard_map/ppermute | solution.py:22
  56.3 2.4 %collective-permute-start.6 = (bf16[27,512]{1,0:T(8,128)(2,1)S(1)}, bf16[27,512]{1,0:T(8,128)(2,1)S(1)}, u32[]{:S(2)}, u32[]{:S(2)}) collective-permute-start(bf16[27,512]{1,0:T(8,128)(2,1)S(1)} %get-tuple-element.9), channel_id=1, source_target_pairs={{1,0},{2,1},{3,2},{4,3},{5,4},{6,5},{7,6},{8,7},{9,8},{10,9},{11,1... | collective-permute-start | bytes 82952 | tf_op jit(solution)/shard_map/ppermute | solution.py:25
  58.7 3.7 %collective-permute-done.6 = bf16[27,512]{1,0:T(8,128)(2,1)S(1)} collective-permute-done((bf16[27,512]{1,0:T(8,128)(2,1)S(1)}, bf16[27,512]{1,0:T(8,128)(2,1)S(1)}, u32[]{:S(2)}, u32[]{:S(2)}) %collective-permute-start.6) | collective-permute-done | bytes 27680 | tf_op jit(solution)/shard_map/ppermute | solution.py:25
  62.4 3.2 %fusion.9 = bf16[438,512]{1,0:T(8,128)(2,1)S(1)} fusion(bf16[27,512]{1,0:T(8,128)(2,1)S(1)} %collective-permute-done.6, bf16[384,512]{1,0:T(8,128)(2,1)S(1)} %fusion.4, bf16[27,512]{1,0:T(8,128)(2,1)S(1)} %collective-permute-done.5, f32[512]{0:T(512)S(1)} %bitcast.47, f32[512]{0:T(512)S(1)} %bitcast.46), kind=kLoop, calls=%fused_computation.21 | loop fusion | flops 2466816 | bytes 901120 | tf_op jit(solution)/shard_map/convert_element_type | solution.py:38
  66.3 7.2 %fusion.3 = bf16[384,512]{1,0:T(8,128)(2,1)} fusion(bf16[384,3584]{1,0:T(8,128)(2,1)S(1)} %slice_dynamic-update-slice_fusion, bf16[3584,512]{1,0:T(8,128)(2,1)} %bitcast.43, bf16[384,512]{1,0:T(8,128)(2,1)S(1)} %fusion.4, bf16[3,512,512]{2,1,0:T(8,128)(2,1)} %param.12, f32[512]{0:T(512)S(1)} %bitcast.53, f32[512]{0:T(512)S(1)} %bitcast.55, ...), kind=kOutput, calls=%fused_computation.9 | convolution fusion | flops 1612578816 | bytes 7741440 | tf_op jit(solution)/shard_map/dot_general | solution.py:45
  (40 shorter events, 1.3 us)
Async XLA Ops:
  0.7 17.2 %collective-permute-start = (bf16[8,512]{1,0:T(8,128)(2,1)S(1)}, bf16[8,512]{1,0:T(8,128)(2,1)S(1)}, u32[]{:S(2)}, u32[]{:S(2)}) collective-permute-start(bf16[8,512]{1,0:T(8,128)(2,1)S(1)} %slice_bitcast_fusion.1), channel_id=1, source_target_pairs={{0,1},{1,2},{2,3},{3,4},{4,5},{5,6},{6,7},{7,8},{8,9},{9,10},{10,1... | collective-permute-start | bytes 24584 | tf_op jit(solution)/shard_map/ppermute | solution.py:14
  9.9 7.4 %copy-start.1 = (f32[3,512]{1,0:T(4,128)S(1)}, f32[3,512]{1,0:T(4,128)}, u32[]{:S(2)}) copy-start(f32[3,512]{1,0:T(4,128)} %param.16) | copy-start | bytes 18436
  9.9 8.0 %copy-start = (bf16[2,384,512]{2,1,0:T(8,128)(2,1)S(1)}, bf16[2,384,512]{2,1,0:T(8,128)(2,1)}, u32[]{:S(2)}) copy-start(bf16[2,384,512]{2,1,0:T(8,128)(2,1)} %param.9) | copy-start | bytes 2359300
  9.9 12.5 %copy-start.2 = (f32[3,512]{1,0:T(4,128)S(1)}, f32[3,512]{1,0:T(4,128)}, u32[]{:S(2)}) copy-start(f32[3,512]{1,0:T(4,128)} %param.17) | copy-start | bytes 18436
  18.0 5.0 %collective-permute-start.1 = (bf16[3,512]{1,0:T(4,128)(2,1)S(1)}, bf16[3,512]{1,0:T(4,128)(2,1)S(1)}, u32[]{:S(2)}, u32[]{:S(2)}) collective-permute-start(bf16[3,512]{1,0:T(4,128)(2,1)S(1)} %get-tuple-element.12), channel_id=1, source_target_pairs={{0,1},{1,2},{2,3},{3,4},{4,5},{5,6},{6,7},{7,8},{8,9},{9,10},{10,1... | collective-permute-start | bytes 9224 | tf_op jit(solution)/shard_map/ppermute | solution.py:22
  20.0 5.8 %collective-permute-start.2 = (bf16[3,512]{1,0:T(4,128)(2,1)S(1)}, bf16[3,512]{1,0:T(4,128)(2,1)S(1)}, u32[]{:S(2)}, u32[]{:S(2)}) collective-permute-start(bf16[3,512]{1,0:T(4,128)(2,1)S(1)} %get-tuple-element.13), channel_id=1, source_target_pairs={{1,0},{2,1},{3,2},{4,3},{5,4},{6,5},{7,6},{8,7},{9,8},{10,9},{11,1... | collective-permute-start | bytes 9224 | tf_op jit(solution)/shard_map/ppermute | solution.py:25
  35.8 4.5 %collective-permute-start.3 = (bf16[9,512]{1,0:T(8,128)(2,1)S(1)}, bf16[9,512]{1,0:T(8,128)(2,1)S(1)}, u32[]{:S(2)}, u32[]{:S(2)}) collective-permute-start(bf16[9,512]{1,0:T(8,128)(2,1)S(1)} %get-tuple-element.10), channel_id=1, source_target_pairs={{0,1},{1,2},{2,3},{3,4},{4,5},{5,6},{6,7},{7,8},{8,9},{9,10},{10,1... | collective-permute-start | bytes 27656 | tf_op jit(solution)/shard_map/ppermute | solution.py:22
  37.7 6.0 %collective-permute-start.4 = (bf16[9,512]{1,0:T(8,128)(2,1)S(1)}, bf16[9,512]{1,0:T(8,128)(2,1)S(1)}, u32[]{:S(2)}, u32[]{:S(2)}) collective-permute-start(bf16[9,512]{1,0:T(8,128)(2,1)S(1)} %get-tuple-element.11), channel_id=1, source_target_pairs={{1,0},{2,1},{3,2},{4,3},{5,4},{6,5},{7,6},{8,7},{9,8},{10,9},{11,1... | collective-permute-start | bytes 27656 | tf_op jit(solution)/shard_map/ppermute | solution.py:25
  47.1 0.7 copy-start.7
  47.1 0.7 copy-start.8
  54.3 4.3 %collective-permute-start.5 = (bf16[27,512]{1,0:T(8,128)(2,1)S(1)}, bf16[27,512]{1,0:T(8,128)(2,1)S(1)}, u32[]{:S(2)}, u32[]{:S(2)}) collective-permute-start(bf16[27,512]{1,0:T(8,128)(2,1)S(1)} %get-tuple-element.8), channel_id=1, source_target_pairs={{0,1},{1,2},{2,3},{3,4},{4,5},{5,6},{6,7},{7,8},{8,9},{9,10},{10,1... | collective-permute-start | bytes 82952 | tf_op jit(solution)/shard_map/ppermute | solution.py:22
  56.3 6.1 %collective-permute-start.6 = (bf16[27,512]{1,0:T(8,128)(2,1)S(1)}, bf16[27,512]{1,0:T(8,128)(2,1)S(1)}, u32[]{:S(2)}, u32[]{:S(2)}) collective-permute-start(bf16[27,512]{1,0:T(8,128)(2,1)S(1)} %get-tuple-element.9), channel_id=1, source_target_pairs={{1,0},{2,1},{3,2},{4,3},{5,4},{6,5},{7,6},{8,7},{9,8},{10,9},{11,1... | collective-permute-start | bytes 82952 | tf_op jit(solution)/shard_map/ppermute | solution.py:25
  65.6 0.7 copy-start.3
  65.6 0.7 copy-start.4
  65.6 0.7 copy-start.5
  65.6 0.7 copy-start.6
where the time goes:
time: 74.1 us; the launch traced here: 73.5 us
  matrix products  20.1 us (27%)
  starting transfers between devices  16.9 us (23%)
  local copies, waits for them, and re-layouts  16.7 us (23%)
  waiting for transfers between devices  9.91 us (13%)
  other arithmetic  9.56 us (13%)
    dot_general x3, matrix products, residual_unit(): jnp.dot(gated, pointwise, preferred_element_type=jnp.float32) + bias_point  20.1 us
    ppermute x3, waiting for transfers between devices, with_halo(): lax.ppermute(lax.slice_in_dim(block, 0, width, axis=dim), axis, backward)  9.9 us
    convert_element_type x3, other arithmetic, residual_unit(): snake(inputs.astype(jnp.float32), alpha_in, beta_in).astype(jnp.bfloat16)  9.45 us
    slice x1, local copies, waits for them, and re-layouts, per_device(): taps[index]  7.41 us
    ppermute x3, starting transfers between devices, with_halo(): lax.ppermute(lax.slice_in_dim(block, 0, width, axis=dim), axis, backward)  7.36 us
    ppermute x3, starting transfers between devices, with_halo(): lax.ppermute(lax.slice_in_dim(block, block.shape[dim] - width, None, axis...  5.8 us
    ppermute x1, starting transfers between devices, passed_along(): lax.ppermute(value, axis, [(source, source + steps) for source in range(f...  3.7 us
    unnamed x36, local copies, waits for them, and re-layouts  1.59 us
  transfers between devices with their start and end apart: 7, of which 3 were waited for; matrix products, arithmetic and copies ran while one was open for 19% of the time, Pallas kernels for 0%

commit v1 on v0

v1 whole, which is shorter than its diff:
```python
import functools
import math

import jax
import jax.numpy as jnp
import numpy as np
from jax import lax
from jax.experimental import pallas as pl
from jax.experimental.pallas import tpu as pltpu
from jax.sharding import PartitionSpec as P

KERNEL = 7
STRIDE = 8
UNITS = 3
DILATIONS = (1, 3, 9)
LANES = 128
LEFT = 48
SENT = 48
HALO = 40
SEGMENTS = 16

SINE = (9.86952481, -32.46513948, 42.64342537, -29.42627071, 10.5812946)


def snake(values, frequency, inverse):
    turns = values * frequency
    rest = turns - jnp.round(turns)
    square = rest * rest
    sine = jnp.float32(SINE[4])
    for coefficient in SINE[3::-1]:
        sine = sine * square + jnp.float32(coefficient)
    return values + (sine * square) * inverse


def rounded(values):
    return values.astype(jnp.bfloat16).astype(jnp.float32)


def segment_plan(frames):
    plan = []
    for unit in range(UNITS):
        reach = 3 * sum(DILATIONS[unit + 1 :])
        first = -(-reach // 8) * 8
        length = -(-(frames + 2 * first) // SEGMENTS)
        if length % 8 == 0 and unit == UNITS - 1:
            length += 1
        plan.append((-first, length))
    return plan


def kernel(
    frames, tracks,
    up, from_chip, from_next, bias_wide, bias_point, alpha_in, beta_in, alpha_mid, beta_mid,
    point_hbm, taps_hbm,
    out,
    x_rows, s_rows, tiles, taps, point, sems,
):
    channels = out.shape[1]
    groups = channels // LANES
    copies = []
    for unit in range(UNITS):
        row = []
        for k in range(KERNEL):
            row.append(
                pltpu.make_async_copy(taps_hbm.at[unit, k], taps.at[unit, k], sems.at[unit, k])
            )
        row.append(pltpu.make_async_copy(point_hbm.at[unit], point.at[unit], sems.at[unit, KERNEL]))
        for copy in row:
            copy.start()
        copies.append(row)

    place = lax.axis_index("tm")
    odd = place % 2 == 1
    is_first = place == 0
    is_last = place == tracks - 1
    rows = frames + 2 * LEFT

    def lane(c):
        return slice(c * LANES, (c + 1) * LANES)

    def snake_in(unit, c):
        frequency = alpha_in[unit : unit + 1, lane(c)] * (1.0 / math.pi)
        inverse = 1.0 / beta_in[unit : unit + 1, lane(c)]
        return lambda v: snake(v, frequency, inverse)

    def clear_outside(c):
        low = s_rows[c, 0:LEFT, :]
        s_rows[c, 0:LEFT, :] = jnp.where(is_first, 0.0, low)
        high = s_rows[c, LEFT + frames :, :]
        s_rows[c, LEFT + frames :, :] = jnp.where(is_last, 0.0, high)

    for c in range(groups):
        chip = from_chip[:, lane(c)].astype(jnp.float32)
        other = from_next[:, lane(c)].astype(jnp.float32)
        low = jnp.where(odd, chip, other)
        high = jnp.where(odd, other, chip)
        carried = jnp.where(is_first, 0.0, low[HALO:SENT])
        own = up[0, :, lane(c)].astype(jnp.float32)
        later = up[1, :, lane(c)].astype(jnp.float32)
        middle = rounded(own + jnp.concatenate([carried, later[: frames - STRIDE]], axis=0))
        joint = rounded(high[:STRIDE] + later[frames - STRIDE :])
        current = jnp.concatenate([low[:HALO], middle, joint, high[STRIDE:HALO]], axis=0)
        edge = LEFT - HALO
        x_rows[c, edge : rows - edge, :] = current
        s_rows[c, edge : rows - edge, :] = snake_in(0, c)(current)
        clear_outside(c)

    for unit in range(UNITS):
        dilation = DILATIONS[unit]
        first, length = segment_plan(frames)[unit]
        base = LEFT + first
        for j in range(length + 6 * dilation):
            start = base - 3 * dilation + j
            for c in range(groups):
                low = s_rows[c, pl.ds(start, 8, stride=length), :]
                high = s_rows[c, pl.ds(start + 8 * length, 8, stride=length), :]
                tiles[j * SEGMENTS : (j + 1) * SEGMENTS, lane(c)] = jnp.concatenate(
                    [low, high], axis=0
                ).astype(jnp.bfloat16)
        cut = -(-length // 2)
        for begin, end in ((0, cut), (cut, length)):
            middle = None
            for k in range(KERNEL):
                if begin == 0:
                    copies[unit][k].wait()
                window = tiles[
                    (begin + k * dilation) * SEGMENTS : (end + k * dilation) * SEGMENTS, :
                ]
                product = jnp.dot(window, taps[unit, k], preferred_element_type=jnp.float32)
                middle = product if middle is None else middle + product
            frequency = alpha_mid[unit : unit + 1, :] * (1.0 / math.pi)
            inverse = 1.0 / beta_mid[unit : unit + 1, :]
            gated = snake(middle + bias_wide[unit : unit + 1, :], frequency, inverse)
            if begin == 0:
                copies[unit][KERNEL].wait()
            update = jnp.dot(
                gated.astype(jnp.bfloat16), point[unit], preferred_element_type=jnp.float32
            ) + bias_point[unit : unit + 1, :]
            for c in range(groups):
                for j in range(begin, end):
                    row = (j - begin) * SEGMENTS
                    for half in range(2):
                        where = pl.ds(base + j + half * 8 * length, 8, stride=length)
                        change = update[row + half * 8 : row + half * 8 + 8, lane(c)]
                        current = rounded(x_rows[c, where, :] + change)
                        x_rows[c, where, :] = current
                        if unit + 1 < UNITS:
                            s_rows[c, where, :] = snake_in(unit + 1, c)(current)
        if unit + 1 < UNITS:
            for c in range(groups):
                clear_outside(c)

    for c in range(groups):
        out[:, lane(c)] = x_rows[c, LEFT : LEFT + frames, :].astype(jnp.bfloat16)


def swaps(groups, count):
    near, far = [], []
    for group in range(groups):
        for place in range(count):
            me = group * count + place
            near.append((me, group * count + (place ^ 1)))
            if place == 0 or place == count - 1:
                partner = group ^ 1
                far.append((me, partner * count + place))
            else:
                far.append((me, me + 1 if place % 2 else me - 1))
    return near, far


def per_device(
    upsampled, taps, bias_wide, pointwise, bias_point, alpha_in, beta_in, alpha_mid, beta_mid
):
    frames, channels = upsampled.shape[1:]
    count = lax.axis_size("tm")
    near, far = swaps(lax.axis_size("grp"), count)

    def summed(own, later):
        return (own.astype(jnp.float32) + later.astype(jnp.float32)).astype(jnp.bfloat16)

    none = jnp.zeros((STRIDE, channels), upsampled.dtype)
    to_next = summed(
        jnp.concatenate([upsampled[0, frames - HALO :], none], axis=0),
        upsampled[1, frames - SENT :],
    )
    to_last = summed(
        upsampled[0, :SENT], jnp.concatenate([none, upsampled[1, : SENT - STRIDE]], axis=0)
    )
    even = lax.axis_index("tm") % 2 == 0
    from_next = lax.ppermute(jnp.where(even, to_last, to_next), ("grp", "tm"), far)
    from_chip = lax.ppermute(jnp.where(even, to_next, to_last), ("grp", "tm"), near)

    rows = frames + 2 * LEFT
    reach = max(
        length + 6 * dilation
        for (_, length), dilation in zip(segment_plan(frames), DILATIONS)
    )
    vmem = pl.BlockSpec(memory_space=pltpu.VMEM)
    hbm = pl.BlockSpec(memory_space=pl.ANY)
    return pl.pallas_call(
        functools.partial(kernel, frames, count),
        out_shape=jax.ShapeDtypeStruct((frames, channels), jnp.bfloat16),
        in_specs=[vmem] * 9 + [hbm] * 2,
        out_specs=vmem,
        scratch_shapes=[
            pltpu.VMEM((channels // LANES, rows, LANES), jnp.float32),
            pltpu.VMEM((channels // LANES, rows, LANES), jnp.float32),
            pltpu.VMEM((reach * SEGMENTS, channels), jnp.bfloat16),
            pltpu.VMEM(taps.shape, jnp.bfloat16),
            pltpu.VMEM(pointwise.shape, jnp.bfloat16),
            pltpu.SemaphoreType.DMA((UNITS, KERNEL + 1)),
        ],
        compiler_params=pltpu.CompilerParams(vmem_limit_bytes=40 * 2**20),
        name="units",
    )(
        upsampled, from_chip, from_next, bias_wide, bias_point,
        alpha_in, beta_in, alpha_mid, beta_mid, pointwise, taps,
    )


def solution(mesh):
    placed = (P(None, ("grp", "tm"), None), P(), P(), P(), P(), P(), P(), P(), P())
    return jax.shard_map(
        per_device, mesh=mesh, in_specs=placed, out_specs=P(("grp", "tm"), None), check_vma=False
    )
```

time: 74.1 us -> 31.4 us (0.42)
  the two profiles are of different devices: /device:TPU:5 before, /device:TPU:0 now
where the time goes in v1:
time: 31.4 us; the launch traced here: 30.8 us
  Pallas kernels  13.2 us (42%)
  local copies, waits for them, and re-layouts  11.7 us (37%)
  starting transfers between devices  3.15 us (10%)
  waiting for transfers between devices  1.93 us (6%)
  other arithmetic  0.85 us (3%)
    pallas_call x1, Pallas kernels, per_device(): pl.pallas_call(functools.partial(kernel, frames, count), out_shape=jax.Sh...  13.2 us
    unnamed x18, local copies, waits for them, and re-layouts  10.8 us
    ppermute x1, starting transfers between devices, per_device(): lax.ppermute(jnp.where(even, to_last, to_next), ('grp', 'tm'), far)  3 us
    ppermute x1, waiting for transfers between devices, per_device(): lax.ppermute(jnp.where(even, to_last, to_next), ('grp', 'tm'), far)  1.93 us
    select_n x1, other arithmetic, per_device(): jnp.where(even, to_last, to_next)  0.85 us
    squeeze x1, local copies, waits for them, and re-layouts, per_device(): upsampled[1, :SENT - STRIDE]  0.8 us
  transfers between devices with their start and end apart: 2, of which 1 were waited for; matrix products, arithmetic and copies ran while one was open for 0% of the time, Pallas kernels for 0%

profile of v1, /device:TPU:0, one launch (start us, length us, event | category | flops | bytes accessed | tf_op | source)
XLA Modules:
  0.0 30.8 jit_solution(8979189882999414836)
XLA Ops:
  0.0 0.8 %slice_bitcast_fusion = (bf16[40,512]{1,0:T(8,128)(2,1)S(1)}, bf16[40,512]{1,0:T(8,128)(2,1)S(1)}) fusion(bf16[2,384,512]{2,1,0:T(8,128)(2,1)} %up.1), kind=kLoop, calls=%fused_computation.6 | loop fusion | bytes 163840 | tf_op jit(solution)/shard_map/squeeze | solution.py:187
  0.8 0.9 %broadcast_select_fusion = (bf16[48,512]{1,0:T(8,128)(2,1)S(1)}, bf16[48,512]{1,0:T(8,128)(2,1)S(1)}) fusion(pred[]{:T(512)S(6)} %eq.5, bf16[2,384,512]{2,1,0:T(8,128)(2,1)} %up.1, bf16[40,512]{1,0:T(8,128)(2,1)S(1)} %get-tuple-element.8, bf16[40,512]{1,0:T(8,128)(2,1)S(1)} %get-tuple-element.7), kind=kLoop, calls=%fused_computation.4 | loop fusion | flops 245760 | bytes 278529 | tf_op jit(solution)/shard_map/jit(_where)/select_n | solution.py:190
  1.7 3.0 %collective-permute-start.1 = (bf16[48,512]{1,0:T(8,128)(2,1)S(1)}, bf16[48,512]{1,0:T(8,128)(2,1)S(1)}, u32[]{:S(2)}, u32[]{:S(2)}) collective-permute-start(bf16[48,512]{1,0:T(8,128)(2,1)S(1)} %get-tuple-element.5), channel_id=1, source_target_pairs={{0,16},{1,2},{2,1},{3,4},{4,3},{5,6},{6,5},{7,8},{8,7},{9,10},{10,... | collective-permute-start | bytes 147464 | tf_op jit(solution)/shard_map/ppermute | solution.py:190
  4.7 0.1 collective-permute-start
  4.8 1.9 %collective-permute-done.1.from_next = bf16[48,512]{1,0:T(8,128)(2,1)S(1)} collective-permute-done((bf16[48,512]{1,0:T(8,128)(2,1)S(1)}, bf16[48,512]{1,0:T(8,128)(2,1)S(1)}, u32[]{:S(2)}, u32[]{:S(2)}) %collective-permute-start.1) | collective-permute-done | bytes 49184 | tf_op jit(solution)/shard_map/ppermute | solution.py:190
  6.7 0.0 collective-permute-done.from_chip
  6.7 0.0 copy-start
  6.7 4.1 %copy-done = bf16[3,7,512,512]{3,2,1,0:T(8,128)(2,1)S(1)} copy-done((bf16[3,7,512,512]{3,2,1,0:T(8,128)(2,1)S(1)}, bf16[3,7,512,512]{3,2,1,0:T(8,128)(2,1)}, u32[]{:S(2)}) %copy-start) | copy-done | bytes 11010072
  10.9 0.0 copy-start.1
  10.9 1.4 %copy-done.1 = bf16[3,512,512]{2,1,0:T(8,128)(2,1)S(1)} copy-done((bf16[3,512,512]{2,1,0:T(8,128)(2,1)S(1)}, bf16[3,512,512]{2,1,0:T(8,128)(2,1)}, u32[]{:S(2)}) %copy-start.1) | copy-done | bytes 1572888
  12.3 0.0 copy-start.2
  12.3 1.1 %copy-done.2 = bf16[2,384,512]{2,1,0:T(8,128)(2,1)S(1)} copy-done((bf16[2,384,512]{2,1,0:T(8,128)(2,1)S(1)}, bf16[2,384,512]{2,1,0:T(8,128)(2,1)}, u32[]{:S(2)}) %copy-start.2) | copy-done | bytes 786456
  13.4 0.0 copy-start.3
  13.4 0.7 %copy-done.3 = f32[3,512]{1,0:T(4,128)S(1)} copy-done((f32[3,512]{1,0:T(4,128)S(1)}, f32[3,512]{1,0:T(4,128)}, u32[]{:S(2)}) %copy-start.3) | copy-done | bytes 6168
  14.1 0.0 copy-start.4
  14.1 0.7 %copy-done.4 = f32[3,512]{1,0:T(4,128)S(1)} copy-done((f32[3,512]{1,0:T(4,128)S(1)}, f32[3,512]{1,0:T(4,128)}, u32[]{:S(2)}) %copy-start.4) | copy-done | bytes 6168
  14.8 0.0 copy-start.5
  14.8 0.7 %copy-done.5 = f32[3,512]{1,0:T(4,128)S(1)} copy-done((f32[3,512]{1,0:T(4,128)S(1)}, f32[3,512]{1,0:T(4,128)}, u32[]{:S(2)}) %copy-start.5) | copy-done | bytes 6168
  15.5 0.0 copy-start.6
  15.5 0.7 %copy-done.6 = f32[3,512]{1,0:T(4,128)S(1)} copy-done((f32[3,512]{1,0:T(4,128)S(1)}, f32[3,512]{1,0:T(4,128)}, u32[]{:S(2)}) %copy-start.6) | copy-done | bytes 6168
  16.2 0.0 copy-start.7
  16.2 0.7 %copy-done.7 = f32[3,512]{1,0:T(4,128)S(1)} copy-done((f32[3,512]{1,0:T(4,128)S(1)}, f32[3,512]{1,0:T(4,128)}, u32[]{:S(2)}) %copy-start.7) | copy-done | bytes 6168
  16.9 0.0 copy-start.8
  16.9 0.7 %copy-done.8 = f32[3,512]{1,0:T(4,128)S(1)} copy-done((f32[3,512]{1,0:T(4,128)S(1)}, f32[3,512]{1,0:T(4,128)}, u32[]{:S(2)}) %copy-start.8) | copy-done | bytes 6168
  17.6 13.2 %units.1 = bf16[384,512]{1,0:T(8,128)(2,1)} custom-call(bf16[2,384,512]{2,1,0:T(8,128)(2,1)S(1)} %copy-done.2, bf16[48,512]{1,0:T(8,128)(2,1)S(1)} %collective-permute-done.from_chip, bf16[48,512]{1,0:T(8,128)(2,1)S(1)} %collective-permute-done.1.from_next, f32[3,512]{1,0:T(4,128)S(1)} %copy-done.3, f32[3,512]{1,0:T(4,128)S(1)} %copy-done.4, ...), custom_call_target="tpu_custom_call" | custom-call | tf_op jit(solution)/shard_map/units/pallas_call | solution.py:200
Async XLA Ops:
  1.7 5.1 %collective-permute-start.1 = (bf16[48,512]{1,0:T(8,128)(2,1)S(1)}, bf16[48,512]{1,0:T(8,128)(2,1)S(1)}, u32[]{:S(2)}, u32[]{:S(2)}) collective-permute-start(bf16[48,512]{1,0:T(8,128)(2,1)S(1)} %get-tuple-element.5), channel_id=1, source_target_pairs={{0,16},{1,2},{2,1},{3,4},{4,3},{5,6},{6,5},{7,8},{8,7},{9,10},{10,... | collective-permute-start | bytes 147464 | tf_op jit(solution)/shard_map/ppermute | solution.py:190
  4.7 2.1 %collective-permute-start = (bf16[48,512]{1,0:T(8,128)(2,1)S(1)}, bf16[48,512]{1,0:T(8,128)(2,1)S(1)}, u32[]{:S(2)}, u32[]{:S(2)}) collective-permute-start(bf16[48,512]{1,0:T(8,128)(2,1)S(1)} %get-tuple-element.6), channel_id=1, source_target_pairs={{0,1},{1,0},{2,3},{3,2},{4,5},{5,4},{6,7},{7,6},{8,9},{9,8},{10,11... | collective-permute-start | bytes 147464 | tf_op jit(solution)/shard_map/ppermute | solution.py:191
  6.7 4.1 %copy-start = (bf16[3,7,512,512]{3,2,1,0:T(8,128)(2,1)S(1)}, bf16[3,7,512,512]{3,2,1,0:T(8,128)(2,1)}, u32[]{:S(2)}) copy-start(bf16[3,7,512,512]{3,2,1,0:T(8,128)(2,1)} %taps_hbm.1) | copy-start | bytes 33030148
  10.9 1.4 %copy-start.1 = (bf16[3,512,512]{2,1,0:T(8,128)(2,1)S(1)}, bf16[3,512,512]{2,1,0:T(8,128)(2,1)}, u32[]{:S(2)}) copy-start(bf16[3,512,512]{2,1,0:T(8,128)(2,1)} %point_hbm.1) | copy-start | bytes 4718596
  12.3 1.1 %copy-start.2 = (bf16[2,384,512]{2,1,0:T(8,128)(2,1)S(1)}, bf16[2,384,512]{2,1,0:T(8,128)(2,1)}, u32[]{:S(2)}) copy-start(bf16[2,384,512]{2,1,0:T(8,128)(2,1)} %up.1) | copy-start | bytes 2359300
  13.4 0.7 %copy-start.3 = (f32[3,512]{1,0:T(4,128)S(1)}, f32[3,512]{1,0:T(4,128)}, u32[]{:S(2)}) copy-start(f32[3,512]{1,0:T(4,128)} %bias_wide.1) | copy-start | bytes 18436
  14.1 0.7 %copy-start.4 = (f32[3,512]{1,0:T(4,128)S(1)}, f32[3,512]{1,0:T(4,128)}, u32[]{:S(2)}) copy-start(f32[3,512]{1,0:T(4,128)} %bias_point.1) | copy-start | bytes 18436
  14.8 0.7 %copy-start.5 = (f32[3,512]{1,0:T(4,128)S(1)}, f32[3,512]{1,0:T(4,128)}, u32[]{:S(2)}) copy-start(f32[3,512]{1,0:T(4,128)} %alpha_in.1) | copy-start | bytes 18436
  15.5 0.7 %copy-start.6 = (f32[3,512]{1,0:T(4,128)S(1)}, f32[3,512]{1,0:T(4,128)}, u32[]{:S(2)}) copy-start(f32[3,512]{1,0:T(4,128)} %beta_in.1) | copy-start | bytes 18436
  16.2 0.7 %copy-start.7 = (f32[3,512]{1,0:T(4,128)S(1)}, f32[3,512]{1,0:T(4,128)}, u32[]{:S(2)}) copy-start(f32[3,512]{1,0:T(4,128)} %alpha_mid.1) | copy-start | bytes 18436
  16.9 0.7 %copy-start.8 = (f32[3,512]{1,0:T(4,128)S(1)}, f32[3,512]{1,0:T(4,128)}, u32[]{:S(2)}) copy-start(f32[3,512]{1,0:T(4,128)} %beta_mid.1) | copy-start | bytes 18436

commit v2 on v0

v2 whole, which is shorter than its diff:
```python
import functools
import math

import jax
import jax.numpy as jnp
from jax import lax
from jax.experimental import pallas as pl
from jax.experimental.pallas import tpu as pltpu
from jax.sharding import PartitionSpec as P

KERNEL = 7
STRIDE = 8
UNITS = 3
DILATIONS = (1, 3, 9)
LANES = 128
LEFT = 48
SENT = 48
HALO = 40
SEGMENTS = 16
SIDE = 3
TABLE = 8
IN_RATE, IN_SCALE, MID_RATE, MID_SCALE, WIDE, POINT = range(6)

SINE = (9.86952481, -32.46513948, 42.64342537, -29.42627071, 10.5812946)


def snake(values, rate, scale):
    turns = values * rate
    rest = turns - jnp.round(turns)
    square = rest * rest
    sine = jnp.float32(SINE[4])
    for coefficient in SINE[3::-1]:
        sine = sine * square + jnp.float32(coefficient)
    return values + (sine * square) * scale


def rounded(values):
    return values.astype(jnp.bfloat16).astype(jnp.float32)


def lane(c):
    return slice(c * LANES, (c + 1) * LANES)


def entry(table, unit, which, lanes=slice(None)):
    row = unit * TABLE + which
    return table[row : row + 1, lanes]


def gather(s_rows, tiles, at, start, length, count):
    for j in range(count):
        for c in range(s_rows.shape[0]):
            low = s_rows[c, pl.ds(start + j, 8, stride=length), :]
            high = s_rows[c, pl.ds(start + j + 8 * length, 8, stride=length), :]
            row = (at + j) * SEGMENTS
            tiles[row : row + SEGMENTS, lane(c)] = jnp.concatenate([low, high], axis=0).astype(
                jnp.bfloat16
            )


def residual(unit, table, taps, point, windows):
    middle = None
    for k in range(KERNEL):
        product = jnp.dot(windows(k), taps[unit, k], preferred_element_type=jnp.float32)
        middle = product if middle is None else middle + product
    gated = snake(
        middle + entry(table, unit, WIDE),
        entry(table, unit, MID_RATE),
        entry(table, unit, MID_SCALE),
    )
    update = jnp.dot(
        gated.astype(jnp.bfloat16), point[unit], preferred_element_type=jnp.float32
    )
    return update + entry(table, unit, POINT)


def scatter(update, x_rows, out_rows, base, length, begin, end, after=None):
    for c in range(x_rows.shape[0]):
        for j in range(begin, end):
            for half in range(2):
                row = (j - begin) * SEGMENTS + half * 8
                where = pl.ds(base + j + half * 8 * length, 8, stride=length)
                current = rounded(x_rows[c, where, :] + update[row : row + 8, lane(c)])
                out_rows[c, where, :] = current
                if after is not None:
                    after(c, where, current)


def halves(length, parts=2):
    cuts = [length * part // parts for part in range(parts + 1)]
    return list(zip(cuts[:-1], cuts[1:]))


def place():
    return lax.axis_index("tm")


def edges_kernel(up_hbm, *refs):
    params, (x_own, to_far, to_near, table), (up, held, sems) = refs[:6], refs[6:10], refs[10:]
    frames = up.shape[1]
    copies = [pltpu.make_async_copy(up_hbm, up, sems.at[6])]
    for i, param in enumerate(params):
        copies.append(pltpu.make_async_copy(param, held.at[i], sems.at[i]))
    for copy in copies:
        copy.start()
    for copy in copies:
        copy.wait()
    later = up[1].astype(jnp.float32)
    none = jnp.zeros((STRIDE, later.shape[1]), jnp.float32)
    later = jnp.concatenate([none, later], axis=0)
    own = up[0].astype(jnp.float32)
    x_own[...] = (own + later[:frames]).astype(jnp.bfloat16)
    to_next = jnp.concatenate([own[frames - HALO :], none], axis=0) + later[frames - HALO :]
    to_last = own[:SENT] + later[:SENT]
    odd = place() % 2 == 1
    to_far[...] = jnp.where(odd, to_next, to_last).astype(jnp.bfloat16)
    to_near[...] = jnp.where(odd, to_last, to_next).astype(jnp.bfloat16)
    table[UNITS * TABLE :, :] = later[frames:]
    wide, point, alpha_in, beta_in, alpha_mid, beta_mid = (held[i] for i in range(6))
    rows = (alpha_in / math.pi, 1 / beta_in, alpha_mid / math.pi, 1 / beta_mid, wide, point)
    for which, value in enumerate(rows):
        for unit in range(UNITS):
            row = unit * TABLE + which
            table[row : row + 1, :] = value[unit : unit + 1, :]


def inner_plan(frames):
    return STRIDE, (frames - 2 * STRIDE) // SEGMENTS


def inner_kernel(x_own, table, taps, point, x_next, x_rows, s_rows, tiles):
    frames = x_own.shape[0]
    groups = x_rows.shape[0]
    first, length = inner_plan(frames)
    for c in range(groups):
        current = x_own[:, lane(c)].astype(jnp.float32)
        x_rows[c, LEFT : LEFT + frames, :] = current
        s_rows[c, LEFT : LEFT + frames, :] = snake(
            current, entry(table, 0, IN_RATE, lane(c)), entry(table, 0, IN_SCALE, lane(c))
        )
    base = LEFT + first
    gather(s_rows, tiles, 0, base - 3, length, length + 6)
    for begin, end in halves(length):
        update = residual(
            0, table, taps, point,
            lambda k: tiles[(begin + k) * SEGMENTS : (end + k) * SEGMENTS, :],
        )
        scatter(update, x_rows, x_next, base, length, begin, end)


def outer_plan(frames):
    plan = {}
    for unit in range(1, UNITS):
        reach = 3 * sum(DILATIONS[unit + 1 :])
        first = -(-reach // 8) * 8
        length = -(-(frames + 2 * first) // SEGMENTS)
        if length % 8 == 0:
            length += 1
        plan[unit] = (-first, length)
    return plan


def outer_kernel(
    tracks,
    x_own, x_inner, from_chip, from_far, table, taps, point,
    out,
    x_rows, s_rows, tiles,
):
    frames = x_own.shape[0]
    groups = x_rows.shape[0]
    end_row = LEFT + frames
    odd = place() % 2 == 1
    is_first = place() == 0
    is_last = place() == tracks - 1

    def snake_in(unit, c, values):
        return snake(
            values, entry(table, unit, IN_RATE, lane(c)), entry(table, unit, IN_SCALE, lane(c))
        )

    def clear_outside(c):
        s_rows[c, 0:LEFT, :] = jnp.where(is_first, 0.0, s_rows[c, 0:LEFT, :])
        s_rows[c, end_row:, :] = jnp.where(is_last, 0.0, s_rows[c, end_row:, :])

    inner_first, inner_length = inner_plan(frames)
    inner_end = LEFT + inner_first + inner_length * SEGMENTS
    low_end = LEFT + 2 * STRIDE
    for c in range(groups):
        chip = from_chip[:, lane(c)].astype(jnp.float32)
        far = from_far[:, lane(c)].astype(jnp.float32)
        before = jnp.where(odd, chip, far)
        behind = jnp.where(odd, far, chip)
        carried = jnp.where(is_first, 0.0, before[HALO:SENT])
        own_low = x_own[: 2 * STRIDE, lane(c)].astype(jnp.float32)
        own_high = x_own[frames - 2 * STRIDE :, lane(c)].astype(jnp.float32)
        low = jnp.concatenate(
            [before[:HALO], rounded(own_low[:STRIDE] + carried), own_low[STRIDE:]], axis=0
        )
        joint = rounded(behind[:STRIDE] + table[UNITS * TABLE :, lane(c)])
        high = jnp.concatenate([own_high, joint, behind[STRIDE:HALO]], axis=0)
        x_rows[c, LEFT - HALO : low_end, :] = low
        x_rows[c, end_row - 2 * STRIDE : end_row + HALO, :] = high
        s_rows[c, LEFT - HALO : low_end, :] = snake_in(0, c, low)
        s_rows[c, end_row - 2 * STRIDE : end_row + HALO, :] = snake_in(0, c, high)
        clear_outside(c)
    bases = (LEFT - 36, inner_end)
    side = SIDE + 6
    for at, base in enumerate(bases):
        gather(s_rows, tiles, at * side, base - 3, SIDE, side)

    def edge_windows(k):
        parts = [(at * side + k) * SEGMENTS for at in range(2)]
        return jnp.concatenate([tiles[p : p + SIDE * SEGMENTS, :] for p in parts], axis=0)

    update = residual(0, table, taps, point, edge_windows)
    for at, base in enumerate(bases):
        part = update[at * SIDE * SEGMENTS : (at + 1) * SIDE * SEGMENTS]
        scatter(part, x_rows, x_rows, base, SIDE, 0, SIDE)
    for c in range(groups):
        tile = slice(low_end - 8, low_end)
        row = lax.broadcasted_iota(jnp.int32, (8, LANES), 0)
        x_rows[c, tile, :] = jnp.where(row < 4, x_rows[c, tile, :], x_inner[c, tile, :])
        x_rows[c, low_end:inner_end, :] = x_inner[c, low_end:inner_end, :]
        rows = slice(LEFT - HALO, end_row + HALO)
        s_rows[c, rows, :] = snake_in(1, c, x_rows[c, rows, :])
        clear_outside(c)

    for unit, (first, length) in outer_plan(frames).items():
        dilation = DILATIONS[unit]
        base = LEFT + first
        gather(s_rows, tiles, 0, base - 3 * dilation, length, length + 6 * dilation)

        def after(c, where, current):
            s_rows[c, where, :] = snake_in(unit + 1, c, current)

        for begin, end in halves(length):
            update = residual(
                unit, table, taps, point,
                lambda k: tiles[
                    (begin + k * dilation) * SEGMENTS : (end + k * dilation) * SEGMENTS, :
                ],
            )
            scatter(
                update, x_rows, x_rows, base, length, begin, end,
                after if unit + 1 < UNITS else None,
            )
        if unit + 1 < UNITS:
            for c in range(groups):
                clear_outside(c)

    for c in range(groups):
        out[:, lane(c)] = x_rows[c, LEFT:end_row, :].astype(jnp.bfloat16)


def swaps(groups, count):
    near, far = [], []
    for group in range(groups):
        for index in range(count):
            me = group * count + index
            near.append((me, group * count + (index ^ 1)))
            if index == 0 or index == count - 1:
                far.append((me, (group ^ 1) * count + index))
            else:
                far.append((me, me + 1 if index % 2 else me - 1))
    return near, far


VMEM = pl.BlockSpec(memory_space=pltpu.VMEM)
HBM = pl.BlockSpec(memory_space=pltpu.HBM)


def in_hbm(value):
    return pltpu.with_memory_space_constraint(value, pltpu.HBM)


def per_device(
    upsampled, taps, bias_wide, pointwise, bias_point, alpha_in, beta_in, alpha_mid, beta_mid
):
    frames, channels = upsampled.shape[1:]
    count = lax.axis_size("tm")
    near, far = swaps(lax.axis_size("grp"), count)
    groups = channels // LANES
    rows = frames + 2 * LEFT
    half = jnp.bfloat16
    params = (bias_wide, bias_point, alpha_in, beta_in, alpha_mid, beta_mid)
    limit = pltpu.CompilerParams(vmem_limit_bytes=16 * 2**20)

    x_own, to_far, to_near, table = pl.pallas_call(
        edges_kernel,
        out_shape=(
            jax.ShapeDtypeStruct((frames, channels), half),
            jax.ShapeDtypeStruct((SENT, channels), half),
            jax.ShapeDtypeStruct((SENT, channels), half),
            jax.ShapeDtypeStruct((UNITS * TABLE + STRIDE, channels), jnp.float32),
        ),
        in_specs=[HBM] * 7,
        out_specs=(VMEM,) * 4,
        scratch_shapes=[
            pltpu.VMEM(upsampled.shape, half),
            pltpu.VMEM((6,) + bias_wide.shape, jnp.float32),
            pltpu.SemaphoreType.DMA((7,)),
        ],
        compiler_params=limit,
        cost_estimate=pl.CostEstimate(
            flops=6 * 10**9, bytes_accessed=upsampled.size * 2, transcendentals=0
        ),
        name="edges",
    )(in_hbm(upsampled), *(in_hbm(param) for param in params))

    from_far = lax.ppermute(to_far, ("grp", "tm"), far)
    from_chip = lax.ppermute(to_near, ("grp", "tm"), near)

    held = pltpu.VMEM((groups, rows, LANES), jnp.float32)
    inner_length = inner_plan(frames)[1]
    x_inner = pl.pallas_call(
        inner_kernel,
        out_shape=jax.ShapeDtypeStruct((groups, rows, LANES), jnp.float32),
        in_specs=[VMEM] * 4,
        out_specs=VMEM,
        scratch_shapes=[
            held,
            held,
            pltpu.VMEM(((inner_length + 6) * SEGMENTS, channels), half),
        ],
        compiler_params=limit,
        cost_estimate=pl.CostEstimate(
            flops=2 * (KERNEL + 1) * inner_length * SEGMENTS * channels**2,
            bytes_accessed=taps.size * 2,
            transcendentals=0,
        ),
        name="inner",
    )(x_own, table, taps, pointwise)

    reach = max(
        length + 6 * DILATIONS[unit] for unit, (_, length) in outer_plan(frames).items()
    )
    return pl.pallas_call(
        functools.partial(outer_kernel, count),
        out_shape=jax.ShapeDtypeStruct((frames, channels), half),
        in_specs=[VMEM] * 7,
        out_specs=VMEM,
        scratch_shapes=[held, held, pltpu.VMEM((reach * SEGMENTS, channels), half)],
        compiler_params=limit,
        name="outer",
    )(x_own, x_inner, from_chip, from_far, table, taps, pointwise)


def solution(mesh):
    placed = (P(None, ("grp", "tm"), None), P(), P(), P(), P(), P(), P(), P(), P())
    return jax.shard_map(
        per_device, mesh=mesh, in_specs=placed, out_specs=P(("grp", "tm"), None), check_vma=False
    )
```

time: 74.1 us -> 15.3 us (0.21)
  matrix products: 20.1 us -> 0 us
  local copies, waits for them, and re-layouts: 16.7 us -> 1.52 us
  starting transfers between devices: 16.9 us -> 1.94 us
  Pallas kernels: 0 us -> 11.7 us
  waiting for transfers between devices: 9.91 us -> 0.01 us
  other arithmetic: 9.56 us -> 0 us
    dot_general x3 -> x0, matrix products: 20.1 us -> none  [residual_unit(): jnp.dot(gated, pointwise, preferred_element_type=jnp.float32) + bias_point]
    ppermute x7 -> x2, starting transfers between devices: 16.9 us -> 1.94 us  [the longest x1 1.2 us: per_device(): from_far = lax.ppermute(to_far, ('grp', 'tm'), far)]
    slice x10 -> x0, local copies, waits for them, and re-layouts: 13.1 us -> none  [the longest x1 7.41 us: per_device(): taps[index]]
    pallas_call x0 -> x3, Pallas kernels: none -> 11.7 us  [the longest x1 7.6 us: per_device(): pl.pallas_call(functools.partial(outer_kernel, count), out_shape=jax.Shap...]
    ppermute x7 -> x2, waiting for transfers between devices: 9.91 us -> 0.01 us  [the longest x1 0.01 us: per_device(): from_chip = lax.ppermute(to_near, ('grp', 'tm'), near)]
    convert_element_type x4 -> x0, other arithmetic: 9.56 us -> none  [the longest x3 9.45 us: residual_unit(): snake(inputs.astype(jnp.float32), alpha_in, beta_in).astype(jnp.bfloat16)]
    squeeze x2 -> x0, local copies, waits for them, and re-layouts: 1.72 us -> none  [the longest x1 1.02 us: per_device(): later = jnp.concatenate([carried, upsampled[1, :frames - STRIDE]], axis=0)]
    unnamed x36 -> x4, local copies, waits for them, and re-layouts: 1.59 us -> 1.52 us
  transfers between devices with their start and end apart: 7 -> 2, of which waited for: 3 -> 0; matrix products, arithmetic and copies ran while one was open for 19% -> 0% of each run, Pallas kernels for 0% -> 17%
where the time goes in v2:
time: 15.3 us; the launch traced here: 15.2 us
  Pallas kernels  11.7 us (76%)
  starting transfers between devices  1.94 us (13%)
  local copies, waits for them, and re-layouts  1.52 us (10%)
    pallas_call x1, Pallas kernels, per_device(): pl.pallas_call(functools.partial(outer_kernel, count), out_shape=jax.Shap...  7.6 us
    pallas_call x1, Pallas kernels, per_device(): pl.pallas_call(inner_kernel, out_shape=jax.ShapeDtypeStruct((groups, rows...  2.59 us
    unnamed x4, local copies, waits for them, and re-layouts  1.52 us
    pallas_call x1, Pallas kernels, per_device(): pl.pallas_call(edges_kernel, out_shape=(jax.ShapeDtypeStruct((frames, cha...  1.46 us
    ppermute x1, starting transfers between devices, per_device(): from_far = lax.ppermute(to_far, ('grp', 'tm'), far)  1.2 us
    ppermute x1, starting transfers between devices, per_device(): from_chip = lax.ppermute(to_near, ('grp', 'tm'), near)  0.74 us
  transfers between devices with their start and end apart: 2, of which 0 were waited for; matrix products, arithmetic and copies ran while one was open for 0% of the time, Pallas kernels for 17%

profile of v2, /device:TPU:5, one launch (start us, length us, event | category | flops | bytes accessed | tf_op | source)
XLA Modules:
  0.0 15.2 jit_solution(6197220843725262330)
XLA Ops:
  0.0 0.0 copy-start.1
  0.0 0.0 copy-start
  0.0 1.5 %edges.1 = (bf16[384,512]{1,0:T(8,128)(2,1)S(1)}, bf16[48,512]{1,0:T(8,128)(2,1)S(1)}, bf16[48,512]{1,0:T(8,128)(2,1)S(1)}, f32[32,512]{1,0:T(8,128)S(1)}) custom-call(bf16[2,384,512]{2,1,0:T(8,128)(2,1)} %up_hbm.1, f32[3,512]{1,0:T(4,128)} %refs_0_.1, f32[3,512]{1,0:T(4,128)} %refs_1_.1, f32[3,512]{1,0:T(4,128)} %refs_2_.1, f32[3,512]{1,0:T(4,128)} %refs_3_.1, ...), custom_call_target="tpu_custom_call" | custom-call | flops 6000000000 | bytes 786432 | tf_op jit(solution)/shard_map/edges/pallas_call | solution.py:288
  1.5 0.7 %collective-permute-start = (bf16[48,512]{1,0:T(8,128)(2,1)S(1)}, bf16[48,512]{1,0:T(8,128)(2,1)S(1)}, u32[]{:S(2)}, u32[]{:S(2)}) collective-permute-start(bf16[48,512]{1,0:T(8,128)(2,1)S(1)} %get-tuple-element.11), channel_id=1, source_target_pairs={{0,1},{1,0},{2,3},{3,2},{4,5},{5,4},{6,7},{7,6},{8,9},{9,8},{10,11... | collective-permute-start | bytes 147464 | tf_op jit(solution)/shard_map/ppermute | solution.py:311
  2.2 1.2 %collective-permute-start.1 = (bf16[48,512]{1,0:T(8,128)(2,1)S(1)}, bf16[48,512]{1,0:T(8,128)(2,1)S(1)}, u32[]{:S(2)}, u32[]{:S(2)}) collective-permute-start(bf16[48,512]{1,0:T(8,128)(2,1)S(1)} %get-tuple-element.12), channel_id=1, source_target_pairs={{0,16},{1,2},{2,1},{3,4},{4,3},{5,6},{6,5},{7,8},{8,7},{9,10},{10,... | collective-permute-start | bytes 147464 | tf_op jit(solution)/shard_map/ppermute | solution.py:310
  3.4 0.0 copy-done.1
  3.4 1.5 %copy-done = bf16[3,7,512,512]{3,2,1,0:T(8,128)(2,1)S(1)} copy-done((bf16[3,7,512,512]{3,2,1,0:T(8,128)(2,1)S(1)}, bf16[3,7,512,512]{3,2,1,0:T(8,128)(2,1)}, u32[]{:S(2)}) %copy-start) | copy-done | bytes 11010072
  4.9 2.6 %inner.1.x_inner = f32[4,480,128]{2,1,0:T(8,128)S(1)} custom-call(bf16[384,512]{1,0:T(8,128)(2,1)S(1)} %get-tuple-element.9.x_own, f32[32,512]{1,0:T(8,128)S(1)} %get-tuple-element.10.table, bf16[3,7,512,512]{3,2,1,0:T(8,128)(2,1)S(1)} %copy-done, bf16[3,512,512]{2,1,0:T(8,128)(2,1)S(1)} %copy-done.1), custom_call_target="tpu_custom_call" | custom-call | flops 1543503872 | bytes 11010048 | tf_op jit(solution)/shard_map/inner/pallas_call | solution.py:315
  7.5 0.0 collective-permute-done.from_chip
  7.5 0.0 collective-permute-done.1.from_far
  7.6 7.6 %outer.1 = bf16[384,512]{1,0:T(8,128)(2,1)} custom-call(bf16[384,512]{1,0:T(8,128)(2,1)S(1)} %get-tuple-element.9.x_own, f32[4,480,128]{2,1,0:T(8,128)S(1)} %inner.1.x_inner, bf16[48,512]{1,0:T(8,128)(2,1)S(1)} %collective-permute-done.from_chip, bf16[48,512]{1,0:T(8,128)(2,1)S(1)} %collective-permute-done.1.from_far, ...), custom_call_target="tpu_custom_call" | custom-call | tf_op jit(solution)/shard_map/outer/pallas_call | solution.py:337
Async XLA Ops:
  0.0 3.4 %copy-start.1 = (bf16[3,512,512]{2,1,0:T(8,128)(2,1)S(1)}, bf16[3,512,512]{2,1,0:T(8,128)(2,1)}, u32[]{:S(2)}) copy-start(bf16[3,512,512]{2,1,0:T(8,128)(2,1)} %point.3) | copy-start | bytes 4718596
  0.0 4.9 %copy-start = (bf16[3,7,512,512]{3,2,1,0:T(8,128)(2,1)S(1)}, bf16[3,7,512,512]{3,2,1,0:T(8,128)(2,1)}, u32[]{:S(2)}) copy-start(bf16[3,7,512,512]{3,2,1,0:T(8,128)(2,1)} %taps.3) | copy-start | bytes 33030148
  1.5 6.1 %collective-permute-start = (bf16[48,512]{1,0:T(8,128)(2,1)S(1)}, bf16[48,512]{1,0:T(8,128)(2,1)S(1)}, u32[]{:S(2)}, u32[]{:S(2)}) collective-permute-start(bf16[48,512]{1,0:T(8,128)(2,1)S(1)} %get-tuple-element.11), channel_id=1, source_target_pairs={{0,1},{1,0},{2,3},{3,2},{4,5},{5,4},{6,7},{7,6},{8,9},{9,8},{10,11... | collective-permute-start | bytes 147464 | tf_op jit(solution)/shard_map/ppermute | solution.py:311
  2.2 5.3 %collective-permute-start.1 = (bf16[48,512]{1,0:T(8,128)(2,1)S(1)}, bf16[48,512]{1,0:T(8,128)(2,1)S(1)}, u32[]{:S(2)}, u32[]{:S(2)}) collective-permute-start(bf16[48,512]{1,0:T(8,128)(2,1)S(1)} %get-tuple-element.12), channel_id=1, source_target_pairs={{0,16},{1,2},{2,1},{3,4},{4,3},{5,6},{6,5},{7,8},{8,7},{9,10},{10,... | collective-permute-start | bytes 147464 | tf_op jit(solution)/shard_map/ppermute | solution.py:310

commit v3 on v2

v3 whole, which is shorter than its diff:
```python
import functools
import math

import jax
import jax.numpy as jnp
from jax import lax
from jax.experimental import pallas as pl
from jax.experimental.pallas import tpu as pltpu
from jax.sharding import PartitionSpec as P

KERNEL = 7
STRIDE = 8
UNITS = 3
DILATIONS = (1, 3, 9)
LANES = 128
LEFT = 48
SENT = 48
HALO = 40
SEGMENTS = 16
TABLE = 8
IN_RATE, IN_SCALE, MID_RATE, MID_SCALE, WIDE, POINT = range(6)

SINE = (9.86952481, -32.46513948, 42.64342537, -29.42627071, 10.5812946)


def snake(values, rate, scale):
    turns = values * rate
    rest = turns - jnp.round(turns)
    square = rest * rest
    sine = jnp.float32(SINE[4])
    for coefficient in SINE[3::-1]:
        sine = sine * square + jnp.float32(coefficient)
    return values + (sine * square) * scale


def rounded(values):
    return values.astype(jnp.bfloat16).astype(jnp.float32)


def lane(c):
    return slice(c * LANES, (c + 1) * LANES)


def entry(table, unit, which, lanes=slice(None)):
    row = unit * TABLE + which
    return table[row : row + 1, lanes]


class Part:
    def __init__(self, unit, pieces):
        self.unit = unit
        self.dilation = DILATIONS[unit]
        self.pieces = pieces
        self.rows = SEGMENTS * sum(length for _, length in pieces)
        self.tiles = sum(length + 6 * self.dilation for _, length in pieces)

    def gather(self, s_rows, tiles):
        steps = []

        def step(at, start, length):
            rows = slice(at * SEGMENTS, (at + 1) * SEGMENTS)
            for c in range(s_rows.shape[0]):
                low = s_rows[c, pl.ds(start, 8, stride=length), :]
                high = s_rows[c, pl.ds(start + 8 * length, 8, stride=length), :]
                tiles[rows, lane(c)] = jnp.concatenate([low, high], axis=0).astype(jnp.bfloat16)

        for first, length in self.pieces:
            start = LEFT + first - 3 * self.dilation
            for j in range(length + 6 * self.dilation):
                steps.append((10, functools.partial(step, len(steps), start + j, length)))
        return steps

    def window(self, tiles, k):
        at, found = 0, []
        for _, length in self.pieces:
            row = (at + k * self.dilation) * SEGMENTS
            found.append(tiles[row : row + length * SEGMENTS, :])
            at += length + 6 * self.dilation
        return found[0] if len(found) == 1 else jnp.concatenate(found, axis=0)

    def conv(self, tiles, taps, middle):
        channels = middle.shape[1]
        total = [None]

        def step(columns, k):
            product = jnp.dot(
                self.window(tiles, k),
                taps[self.unit, k, :, columns],
                preferred_element_type=jnp.float32,
            )
            total[0] = product if k == 0 else total[0] + product
            if k == KERNEL - 1:
                middle[: self.rows, columns] = total[0]

        return [
            (1, functools.partial(step, columns, k))
            for columns in halves(channels)
            for k in range(KERNEL)
        ]

    def gate(self, middle, gated, table, columns=slice(None)):
        def step(rows):
            gated[rows, columns] = snake(
                middle[rows, columns] + entry(table, self.unit, WIDE, columns),
                entry(table, self.unit, MID_RATE, columns),
                entry(table, self.unit, MID_SCALE, columns),
            ).astype(jnp.bfloat16)

        return [
            (40, functools.partial(step, slice(row, row + SEGMENTS)))
            for row in range(0, self.rows, SEGMENTS)
        ]

    def project(self, sources, point, update):
        total = [None]

        def step(i, gated, columns):
            product = jnp.dot(
                gated[: self.rows, columns],
                point[self.unit, columns, :],
                preferred_element_type=jnp.float32,
            )
            total[0] = product if i == 0 else total[0] + product
            if i == len(sources) - 1:
                update[: self.rows, :] = total[0]

        return [
            (20, functools.partial(step, i, gated, columns))
            for i, (gated, columns) in enumerate(sources)
        ]

    def finish(self, update, table, x_rows, x_next, s_next=None):
        steps = []

        def step(row, start, length):
            for half in range(2):
                where = pl.ds(start + half * 8 * length, 8, stride=length)
                rows = slice(row + half * 8, row + half * 8 + 8)
                for c in range(x_rows.shape[0]):
                    change = update[rows, lane(c)] + entry(table, self.unit, POINT, lane(c))
                    current = rounded(x_rows[c, where, :] + change)
                    x_next[c, where, :] = current
                    if s_next is not None:
                        s_next[c, where, :] = snake_in(table, self.unit + 1, c, current)

        for first, length in self.pieces:
            for j in range(length):
                steps.append(
                    (50, functools.partial(step, len(steps) * SEGMENTS, LEFT + first + j, length))
                )
        return steps


def snake_in(table, unit, c, values):
    return snake(
        values, entry(table, unit, IN_RATE, lane(c)), entry(table, unit, IN_SCALE, lane(c))
    )


def weave(main, others=()):
    whole = sum(cost for cost, _ in others)
    spent, at = 0, 0
    for i, (_, step) in enumerate(main):
        step()
        while at < len(others) and (i + 1 == len(main) or spent * len(main) < whole * (i + 1)):
            spent += others[at][0]
            others[at][1]()
            at += 1


def run(steps):
    for _, step in steps:
        step()


def halves(channels):
    return slice(0, channels // 2), slice(channels // 2, channels)


def parts(frames):
    inner = (
        Part(0, [(8, frames // SEGMENTS - 6)]),
        Part(1, [(20, frames // SEGMENTS - 7)]),
        Part(2, [(48, frames // SEGMENTS - 11)]),
    )
    outer = (
        Part(0, [(-36, 3), (frames - 88, 8)]),
        Part(1, [(-28, 3), (frames - 100, 8)]),
        Part(2, [(0, 3), (frames - 128, 8)]),
    )
    return inner, outer


def place():
    return lax.axis_index("tm")


def edges_kernel(up_hbm, *refs):
    params, (x_own, to_far, to_near, table), (up, held, sems) = refs[:6], refs[6:10], refs[10:]
    frames = up.shape[1]
    copies = [pltpu.make_async_copy(up_hbm, up, sems.at[6])]
    for i, param in enumerate(params):
        copies.append(pltpu.make_async_copy(param, held.at[i], sems.at[i]))
    for copy in copies:
        copy.start()
    for copy in copies:
        copy.wait()
    later = up[1].astype(jnp.float32)
    none = jnp.zeros((STRIDE, later.shape[1]), jnp.float32)
    later = jnp.concatenate([none, later], axis=0)
    own = up[0].astype(jnp.float32)
    x_own[...] = (own + later[:frames]).astype(jnp.bfloat16)
    to_next = jnp.concatenate([own[frames - HALO :], none], axis=0) + later[frames - HALO :]
    to_last = own[:SENT] + later[:SENT]
    odd = place() % 2 == 1
    to_far[...] = jnp.where(odd, to_next, to_last).astype(jnp.bfloat16)
    to_near[...] = jnp.where(odd, to_last, to_next).astype(jnp.bfloat16)
    table[UNITS * TABLE :, :] = later[frames:]
    wide, point, alpha_in, beta_in, alpha_mid, beta_mid = (held[i] for i in range(6))
    rows = (alpha_in / math.pi, 1 / beta_in, alpha_mid / math.pi, 1 / beta_mid, wide, point)
    for which, value in enumerate(rows):
        for unit in range(UNITS):
            row = unit * TABLE + which
            table[row : row + 1, :] = value[unit : unit + 1, :]


def first_kernel(x_own, table, x_rows, s_rows, tiles):
    frames = x_own.shape[0]
    for c in range(x_rows.shape[0]):
        current = x_own[:, lane(c)].astype(jnp.float32)
        x_rows[c, LEFT : LEFT + frames, :] = current
        s_rows[c, LEFT : LEFT + frames, :] = snake_in(table, 0, c, current)
    run(parts(frames)[0][0].gather(s_rows, tiles))


def inner_kernel(frames, tiles, table, taps, middle, gated):
    part = parts(frames)[0][0]
    first, _ = halves(middle.shape[1])
    steps = part.conv(tiles, taps, middle)
    weave(steps[:KERNEL])
    weave(steps[KERNEL:], part.gate(middle, gated, table, first))


def outer_kernel(
    tracks,
    x_own, x_first, s_first, first_middle, first_gated, from_chip, from_far, table, taps, point,
    out,
    x_0, x_1, x_2, s_0, s_1, s_2, inner_tiles, outer_tiles, inner_middle, outer_middle,
    gated, gated_2, update,
):
    frames, channels = x_own.shape
    groups = x_0.shape[0]
    end_row = LEFT + frames
    odd = place() % 2 == 1
    is_first = place() == 0
    is_last = place() == tracks - 1
    inner, outer = parts(frames)
    both = halves(channels)

    def clear_outside(s_rows):
        def step(c):
            s_rows[c, 0:LEFT, :] = jnp.where(is_first, 0.0, s_rows[c, 0:LEFT, :])
            s_rows[c, end_row:, :] = jnp.where(is_last, 0.0, s_rows[c, end_row:, :])

        return [(10, functools.partial(step, c)) for c in range(groups)]

    def store(begin, end):
        def step(c, row):
            rows = slice(LEFT + row, LEFT + row + SEGMENTS)
            out[row : row + SEGMENTS, lane(c)] = x_0[c, rows, :].astype(jnp.bfloat16)

        return [
            (2, functools.partial(step, c, row))
            for row in range(begin, end, SEGMENTS)
            for c in range(groups)
        ]

    def after(part, middle, x_rows, x_next, s_next):
        return (
            part.gate(middle, gated, table)
            + part.project([(gated, slice(None))], point, update)
            + part.finish(update, table, x_rows, x_next, s_next)
        )

    low_end = LEFT + 2 * STRIDE
    kept = LEFT + outer[0].pieces[1][0] - 8
    for c in range(groups):
        chip = from_chip[:, lane(c)].astype(jnp.float32)
        far = from_far[:, lane(c)].astype(jnp.float32)
        before = jnp.where(odd, chip, far)
        behind = jnp.where(odd, far, chip)
        carried = jnp.where(is_first, 0.0, before[HALO:SENT])
        own_low = x_own[: 2 * STRIDE, lane(c)].astype(jnp.float32)
        low = jnp.concatenate(
            [before[:HALO], rounded(own_low[:STRIDE] + carried), own_low[STRIDE:]], axis=0
        )
        joint = rounded(behind[:STRIDE] + table[UNITS * TABLE :, lane(c)])
        high = jnp.concatenate([joint, behind[STRIDE:HALO]], axis=0)
        x_0[c, LEFT - HALO : low_end, :] = low
        s_0[c, LEFT - HALO : low_end, :] = snake_in(table, 0, c, low)
        x_0[c, kept:end_row, :] = x_first[c, kept:end_row, :]
        s_0[c, kept:end_row, :] = s_first[c, kept:end_row, :]
        x_0[c, end_row : end_row + HALO, :] = high
        s_0[c, end_row : end_row + HALO, :] = snake_in(table, 0, c, high)
    run(clear_outside(s_0))
    run(outer[0].gather(s_0, outer_tiles))

    weave(
        outer[0].conv(outer_tiles, taps, outer_middle),
        inner[0].gate(first_middle, gated, table, both[1])
        + inner[0].project([(first_gated, both[0]), (gated, both[1])], point, update)
        + inner[0].finish(update, table, x_first, x_1, s_1)
        + inner[1].gather(s_1, inner_tiles),
    )
    weave(
        inner[1].conv(inner_tiles, taps, inner_middle),
        after(outer[0], outer_middle, x_0, x_1, s_1)
        + clear_outside(s_1)
        + outer[1].gather(s_1, outer_tiles),
    )
    weave(
        outer[1].conv(outer_tiles, taps, outer_middle),
        after(inner[1], inner_middle, x_1, x_2, s_2) + inner[2].gather(s_2, inner_tiles),
    )
    weave(
        inner[2].conv(inner_tiles, taps, inner_middle),
        after(outer[1], outer_middle, x_1, x_2, s_2)
        + clear_outside(s_2)
        + outer[2].gather(s_2, outer_tiles),
    )
    begin = inner[2].pieces[0][0]
    end = begin + inner[2].rows
    steps = outer[2].conv(outer_tiles, taps, outer_middle)
    finish = after(inner[2], inner_middle, x_2, x_0, None) + store(begin, end)
    cut = len(finish) // 2
    weave(steps[:KERNEL], finish[:cut])
    weave(steps[KERNEL:], finish[cut:] + outer[2].gate(outer_middle, gated_2, table, both[0]))
    run(outer[2].gate(outer_middle, gated_2, table, both[1]))
    run(outer[2].project([(gated_2, columns) for columns in both], point, update))
    run(outer[2].finish(update, table, x_2, x_0))
    run(store(0, begin) + store(end, frames))


def swaps(groups, count):
    near, far = [], []
    for group in range(groups):
        for index in range(count):
            me = group * count + index
            near.append((me, group * count + (index ^ 1)))
            if index == 0 or index == count - 1:
                far.append((me, (group ^ 1) * count + index))
            else:
                far.append((me, me + 1 if index % 2 else me - 1))
    return near, far


VMEM = pl.BlockSpec(memory_space=pltpu.VMEM)
HBM = pl.BlockSpec(memory_space=pltpu.HBM)


def in_hbm(value):
    return pltpu.with_memory_space_constraint(value, pltpu.HBM)


VMEM = pl.BlockSpec(memory_space=pltpu.VMEM)
HBM = pl.BlockSpec(memory_space=pltpu.HBM)


def in_hbm(value):
    return pltpu.with_memory_space_constraint(value, pltpu.HBM)


def per_device(
    upsampled, taps, bias_wide, pointwise, bias_point, alpha_in, beta_in, alpha_mid, beta_mid
):
    frames, channels = upsampled.shape[1:]
    count = lax.axis_size("tm")
    near, far = swaps(lax.axis_size("grp"), count)
    groups = channels // LANES
    rows = frames + 2 * LEFT
    half = jnp.bfloat16
    params = (bias_wide, bias_point, alpha_in, beta_in, alpha_mid, beta_mid)
    limit = pltpu.CompilerParams(vmem_limit_bytes=16 * 2**20)

    x_own, to_far, to_near, table = pl.pallas_call(
        edges_kernel,
        out_shape=(
            jax.ShapeDtypeStruct((frames, channels), half),
            jax.ShapeDtypeStruct((SENT, channels), half),
            jax.ShapeDtypeStruct((SENT, channels), half),
            jax.ShapeDtypeStruct((UNITS * TABLE + STRIDE, channels), jnp.float32),
        ),
        in_specs=[HBM] * 7,
        out_specs=(VMEM,) * 4,
        scratch_shapes=[
            pltpu.VMEM(upsampled.shape, half),
            pltpu.VMEM((6,) + bias_wide.shape, jnp.float32),
            pltpu.SemaphoreType.DMA((7,)),
        ],
        compiler_params=limit,
        cost_estimate=pl.CostEstimate(
            flops=6 * 10**9, bytes_accessed=upsampled.size * 2, transcendentals=0
        ),
        name="edges",
    )(in_hbm(upsampled), *(in_hbm(param) for param in params))

    from_far = lax.ppermute(to_far, ("grp", "tm"), far)
    from_chip = lax.ppermute(to_near, ("grp", "tm"), near)

    inner, outer = parts(frames)
    natural = (groups, rows, LANES)
    single = jnp.float32

    def tiles(*of):
        return max(part.tiles for part in of) * SEGMENTS, channels

    def most(*of):
        return max(part.rows for part in of), channels

    x_first, s_first, first_tiles = pl.pallas_call(
        first_kernel,
        out_shape=(
            jax.ShapeDtypeStruct(natural, single),
            jax.ShapeDtypeStruct(natural, single),
            jax.ShapeDtypeStruct(tiles(inner[0]), half),
        ),
        in_specs=[VMEM] * 2,
        out_specs=(VMEM,) * 3,
        compiler_params=limit,
        name="first",
    )(x_own, table)

    first_middle, first_gated = pl.pallas_call(
        functools.partial(inner_kernel, frames),
        out_shape=(
            jax.ShapeDtypeStruct(most(inner[0]), single),
            jax.ShapeDtypeStruct(most(inner[0]), half),
        ),
        in_specs=[VMEM] * 3,
        out_specs=(VMEM,) * 2,
        compiler_params=limit,
        cost_estimate=pl.CostEstimate(
            flops=2 * KERNEL * inner[0].rows * channels**2,
            bytes_accessed=taps.size * 2,
            transcendentals=0,
        ),
        name="inner",
    )(first_tiles, table, taps)

    return pl.pallas_call(
        functools.partial(outer_kernel, count),
        out_shape=jax.ShapeDtypeStruct((frames, channels), half),
        in_specs=[VMEM] * 10,
        out_specs=VMEM,
        scratch_shapes=[pltpu.VMEM(natural, single)] * 6
        + [
            pltpu.VMEM(tiles(*inner[1:]), half),
            pltpu.VMEM(tiles(*outer), half),
            pltpu.VMEM(most(*inner[1:]), single),
            pltpu.VMEM(most(*outer), single),
            pltpu.VMEM(most(*inner, *outer), half),
            pltpu.VMEM(most(outer[2]), half),
            pltpu.VMEM(most(*inner, *outer), single),
        ],
        compiler_params=pltpu.CompilerParams(vmem_limit_bytes=24 * 2**20),
        name="outer",
    )(
        x_own, x_first, s_first, first_middle, first_gated, from_chip, from_far,
        table, taps, pointwise,
    )


def solution(mesh):
    placed = (P(None, ("grp", "tm"), None), P(), P(), P(), P(), P(), P(), P(), P())
    return jax.shard_map(
        per_device, mesh=mesh, in_specs=placed, out_specs=P(("grp", "tm"), None), check_vma=False
    )
```

time: 15.3 us -> 14.2 us (0.928)
  local copies, waits for them, and re-layouts: 1.52 us -> 0.45 us
  Pallas kernels: 11.7 us -> 10.7 us
  waiting for transfers between devices: 0.01 us -> 0.85 us
    unnamed x4, local copies, waits for them, and re-layouts: 1.52 us -> 0.45 us
    ppermute x1, waiting for transfers between devices: 0.01 us -> 0.85 us  [per_device(): from_far = lax.ppermute(to_far, ('grp', 'tm'), far)]
    pallas_call x1 -> x2, Pallas kernels: 2.59 us -> 1.9 us  [the longest x1 1.32 us: per_device(): pl.pallas_call(functools.partial(inner_kernel, frames), out_shape=(jax.Sh...]
    pallas_call x1, Pallas kernels: 7.6 us -> 7.36 us  [per_device(): pl.pallas_call(functools.partial(outer_kernel, count), out_shape=jax.Shap...]
  transfers between devices with their start and end apart: 2 -> 2, of which waited for: 0 -> 1; matrix products, arithmetic and copies ran while one was open for 0% -> 0% of each run, Pallas kernels for 17% -> 14%
where the time goes in v3:
time: 14.2 us; the launch traced here: 14 us
  Pallas kernels  10.7 us (75%)
  starting transfers between devices  1.94 us (14%)
  waiting for transfers between devices  0.85 us (6%)
  local copies, waits for them, and re-layouts  0.45 us (3%)
    pallas_call x1, Pallas kernels, per_device(): pl.pallas_call(functools.partial(outer_kernel, count), out_shape=jax.Shap...  7.36 us
    pallas_call x1, Pallas kernels, per_device(): pl.pallas_call(edges_kernel, out_shape=(jax.ShapeDtypeStruct((frames, cha...  1.46 us
    pallas_call x1, Pallas kernels, per_device(): pl.pallas_call(functools.partial(inner_kernel, frames), out_shape=(jax.Sh...  1.32 us
    ppermute x1, starting transfers between devices, per_device(): from_far = lax.ppermute(to_far, ('grp', 'tm'), far)  1.2 us
    ppermute x1, waiting for transfers between devices, per_device(): from_far = lax.ppermute(to_far, ('grp', 'tm'), far)  0.85 us
    ppermute x1, starting transfers between devices, per_device(): from_chip = lax.ppermute(to_near, ('grp', 'tm'), near)  0.74 us
    pallas_call x1, Pallas kernels, per_device(): pl.pallas_call(first_kernel, out_shape=(jax.ShapeDtypeStruct(natural, sin...  0.59 us
    unnamed x4, local copies, waits for them, and re-layouts  0.45 us
  transfers between devices with their start and end apart: 2, of which 1 were waited for; matrix products, arithmetic and copies ran while one was open for 0% of the time, Pallas kernels for 14%

profile of v3, /device:TPU:5, one launch (start us, length us, event | category | flops | bytes accessed | tf_op | source)
XLA Modules:
  0.0 14.0 jit_solution(16654940639179912359)
XLA Ops:
  0.0 0.0 copy-start
  0.0 1.5 %edges.1 = (bf16[384,512]{1,0:T(8,128)(2,1)S(1)}, bf16[48,512]{1,0:T(8,128)(2,1)S(1)}, bf16[48,512]{1,0:T(8,128)(2,1)S(1)}, f32[32,512]{1,0:T(8,128)S(1)}) custom-call(bf16[2,384,512]{2,1,0:T(8,128)(2,1)} %up_hbm.1, f32[3,512]{1,0:T(4,128)} %refs_0_.1, f32[3,512]{1,0:T(4,128)} %refs_1_.1, f32[3,512]{1,0:T(4,128)} %refs_2_.1, f32[3,512]{1,0:T(4,128)} %refs_3_.1, ...), custom_call_target="tpu_custom_call" | custom-call | flops 6000000000 | bytes 786432 | tf_op jit(solution)/shard_map/edges/pallas_call | solution.py:385
  1.5 0.0 copy-start.1
  1.5 0.7 %collective-permute-start = (bf16[48,512]{1,0:T(8,128)(2,1)S(1)}, bf16[48,512]{1,0:T(8,128)(2,1)S(1)}, u32[]{:S(2)}, u32[]{:S(2)}) collective-permute-start(bf16[48,512]{1,0:T(8,128)(2,1)S(1)} %get-tuple-element.21), channel_id=1, source_target_pairs={{0,1},{1,0},{2,3},{3,2},{4,5},{5,4},{6,7},{7,6},{8,9},{9,8},{10,11... | collective-permute-start | bytes 147464 | tf_op jit(solution)/shard_map/ppermute | solution.py:408
  2.2 1.2 %collective-permute-start.1 = (bf16[48,512]{1,0:T(8,128)(2,1)S(1)}, bf16[48,512]{1,0:T(8,128)(2,1)S(1)}, u32[]{:S(2)}, u32[]{:S(2)}) collective-permute-start(bf16[48,512]{1,0:T(8,128)(2,1)S(1)} %get-tuple-element.22), channel_id=1, source_target_pairs={{0,16},{1,2},{2,1},{3,4},{4,3},{5,6},{6,5},{7,8},{8,7},{9,10},{10,... | collective-permute-start | bytes 147464 | tf_op jit(solution)/shard_map/ppermute | solution.py:407
  3.4 0.6 %first.1 = (f32[4,480,128]{2,1,0:T(8,128)S(1)}, f32[4,480,128]{2,1,0:T(8,128)S(1)}, bf16[384,512]{1,0:T(8,128)(2,1)S(1)}) custom-call(bf16[384,512]{1,0:T(8,128)(2,1)S(1)} %get-tuple-element.14.x_own, f32[32,512]{1,0:T(8,128)S(1)} %get-tuple-element.15.table), custom_call_target="tpu_custom_call" | custom-call | tf_op jit(solution)/shard_map/first/pallas_call | solution.py:420
  4.0 0.4 %copy-done = bf16[3,7,512,512]{3,2,1,0:T(8,128)(2,1)S(1)} copy-done((bf16[3,7,512,512]{3,2,1,0:T(8,128)(2,1)S(1)}, bf16[3,7,512,512]{3,2,1,0:T(8,128)(2,1)}, u32[]{:S(2)}) %copy-start) | copy-done | bytes 11010072
  4.5 1.3 %inner.1 = (f32[288,512]{1,0:T(8,128)S(1)}, bf16[288,512]{1,0:T(8,128)(2,1)S(1)}) custom-call(bf16[384,512]{1,0:T(8,128)(2,1)S(1)} %get-tuple-element.18.tiles, f32[32,512]{1,0:T(8,128)S(1)} %get-tuple-element.15.table, bf16[3,7,512,512]{3,2,1,0:T(8,128)(2,1)S(1)} %copy-done), custom_call_target="tpu_custom_call" | custom-call | flops 1056964608 | bytes 11010048 | tf_op jit(solution)/shard_map/inner/pallas_call | solution.py:433
  5.8 0.0 collective-permute-done.from_chip
  5.8 0.8 %collective-permute-done.1.from_far = bf16[48,512]{1,0:T(8,128)(2,1)S(1)} collective-permute-done((bf16[48,512]{1,0:T(8,128)(2,1)S(1)}, bf16[48,512]{1,0:T(8,128)(2,1)S(1)}, u32[]{:S(2)}, u32[]{:S(2)}) %collective-permute-start.1) | collective-permute-done | bytes 49184 | tf_op jit(solution)/shard_map/ppermute | solution.py:407
  6.6 0.0 copy-done.1
  6.6 7.4 %outer.1 = bf16[384,512]{1,0:T(8,128)(2,1)} custom-call(bf16[384,512]{1,0:T(8,128)(2,1)S(1)} %get-tuple-element.14.x_own, f32[4,480,128]{2,1,0:T(8,128)S(1)} %get-tuple-element.16.x_first, f32[4,480,128]{2,1,0:T(8,128)S(1)} %get-tuple-element.17.s_first, f32[288,512]{1,0:T(8,128)S(1)} %get-tuple-element.19.first_middle, ...), custom_call_target="tpu_custom_call" | custom-call | tf_op jit(solution)/shard_map/outer/pallas_call | solution.py:450
Async XLA Ops:
  0.0 4.5 %copy-start = (bf16[3,7,512,512]{3,2,1,0:T(8,128)(2,1)S(1)}, bf16[3,7,512,512]{3,2,1,0:T(8,128)(2,1)}, u32[]{:S(2)}) copy-start(bf16[3,7,512,512]{3,2,1,0:T(8,128)(2,1)} %taps.3) | copy-start | bytes 33030148
  1.5 5.2 %copy-start.1 = (bf16[3,512,512]{2,1,0:T(8,128)(2,1)S(1)}, bf16[3,512,512]{2,1,0:T(8,128)(2,1)}, u32[]{:S(2)}) copy-start(bf16[3,512,512]{2,1,0:T(8,128)(2,1)} %point.1) | copy-start | bytes 4718596
  1.5 4.3 %collective-permute-start = (bf16[48,512]{1,0:T(8,128)(2,1)S(1)}, bf16[48,512]{1,0:T(8,128)(2,1)S(1)}, u32[]{:S(2)}, u32[]{:S(2)}) collective-permute-start(bf16[48,512]{1,0:T(8,128)(2,1)S(1)} %get-tuple-element.21), channel_id=1, source_target_pairs={{0,1},{1,0},{2,3},{3,2},{4,5},{5,4},{6,7},{7,6},{8,9},{9,8},{10,11... | collective-permute-start | bytes 147464 | tf_op jit(solution)/shard_map/ppermute | solution.py:408
  2.2 4.4 %collective-permute-start.1 = (bf16[48,512]{1,0:T(8,128)(2,1)S(1)}, bf16[48,512]{1,0:T(8,128)(2,1)S(1)}, u32[]{:S(2)}, u32[]{:S(2)}) collective-permute-start(bf16[48,512]{1,0:T(8,128)(2,1)S(1)} %get-tuple-element.22), channel_id=1, source_target_pairs={{0,16},{1,2},{2,1},{3,4},{4,3},{5,6},{6,5},{7,8},{8,7},{9,10},{10,... | collective-permute-start | bytes 147464 | tf_op jit(solution)/shard_map/ppermute | solution.py:407

commit v4 on v3

v4 whole, which is shorter than its diff:
```python
import functools
import math

import jax
import jax.numpy as jnp
from jax import lax
from jax.experimental import pallas as pl
from jax.experimental.pallas import tpu as pltpu
from jax.sharding import PartitionSpec as P

KERNEL = 7
STRIDE = 8
UNITS = 3
DILATIONS = (1, 3, 9)
LANES = 128
LEFT = 48
SENT = 48
HALO = 40
SEGMENTS = 16
TABLE = 8
IN_RATE, IN_SCALE, MID_RATE, MID_SCALE, WIDE, POINT = range(6)

SINE = (9.86952481, -32.46513948, 42.64342537, -29.42627071, 10.5812946)


def snake(values, rate, scale):
    turns = values * rate
    rest = turns - jnp.round(turns)
    square = rest * rest
    sine = jnp.float32(SINE[4])
    for coefficient in SINE[3::-1]:
        sine = sine * square + jnp.float32(coefficient)
    return values + (sine * square) * scale


def rounded(values):
    return values.astype(jnp.bfloat16).astype(jnp.float32)


def lane(c):
    return slice(c * LANES, (c + 1) * LANES)


def entry(table, unit, which, lanes=slice(None)):
    row = unit * TABLE + which
    return table[row : row + 1, lanes]


WIDTH = 256


class Matrix:
    def __init__(self):
        self.count = 0
        self.staged = None

    def tile(self, weights, rows, sums):
        register = self.count % 2
        self.count += 1
        for unit, columns in enumerate(halves(2 * WIDTH)):
            pltpu.matmul_push_rhs(weights(columns), register, unit)
        self.flush()
        self.staged = register, rows, sums

    def flush(self):
        if self.staged is None:
            return
        register, rows, sums = self.staged
        self.staged = None
        for i, pair in enumerate(sums):
            value = rows(i)
            for unit in range(2):
                load = register if i == 0 else None
                pltpu.matmul_acc_lhs(pair[unit], value, load_staged_rhs=load)


class Part:
    def __init__(self, unit, pieces, plain=False):
        self.unit = unit
        self.plain = plain
        self.dilation = DILATIONS[unit]
        self.pieces = pieces
        self.rows = SEGMENTS * sum(length for _, length in pieces)
        if plain:
            self.tiles = KERNEL * self.rows // SEGMENTS
        else:
            self.tiles = sum(length + 6 * self.dilation for _, length in pieces)

    def starts(self, first, j, length):
        if self.plain:
            start = LEFT + first + SEGMENTS * j
            return (start, start + 8), 1
        start = LEFT + first + j
        return (start, start + 8 * length), length

    def gather(self, s_rows, tiles):
        steps = []

        def step(at, first, j, length):
            rows = slice(at * SEGMENTS, (at + 1) * SEGMENTS)
            starts, stride = self.starts(first, j, length)
            for c in range(s_rows.shape[0]):
                both = [s_rows[c, run_of(start, stride), :] for start in starts]
                tiles[rows, lane(c)] = jnp.concatenate(both, axis=0).astype(jnp.bfloat16)

        reach = 3 * self.dilation
        if self.plain:
            for k in range(KERNEL):
                for first, length in self.pieces:
                    first += (k - 3) * self.dilation
                    for j in range(length):
                        steps.append((10, functools.partial(step, len(steps), first, j, length)))
            return steps
        for first, length in self.pieces:
            for j in range(length + 2 * reach):
                steps.append(
                    (10, functools.partial(step, len(steps), first - reach, j, length))
                )
        return steps

    def window(self, tiles, k):
        at, found = 0, []
        for _, length in self.pieces:
            row = (at + k * self.dilation) * SEGMENTS
            found.append(tiles[row : row + length * SEGMENTS, :])
            at += length + 6 * self.dilation
        return found[0] if len(found) == 1 else jnp.concatenate(found, axis=0)

    def conv(self, tiles, taps, middle):
        channels = middle.shape[1]
        total = [None]

        def step(columns, k):
            product = jnp.dot(
                self.window(tiles, k),
                taps[self.unit, k, :, columns],
                preferred_element_type=jnp.float32,
            )
            total[0] = product if k == 0 else total[0] + product
            if k == KERNEL - 1:
                middle[: self.rows, columns] = total[0]

        return [
            (1, functools.partial(step, columns, k))
            for columns in halves(channels)
            for k in range(KERNEL)
        ]

    def conv_sums(self, matrix, tiles, taps, sums):
        places, at = [], 0
        for _, length in self.pieces:
            places += range(at, at + length)
            at += length + (0 if self.plain else 6 * self.dilation)
        away = len(places) if self.plain else self.dilation

        def rows(k, inputs, i):
            row = (places[i] + k * away) * SEGMENTS
            return tiles[row : row + SEGMENTS, inputs]

        def step(k, inputs):
            matrix.tile(
                lambda columns: taps[self.unit, k, inputs, columns],
                functools.partial(rows, k, inputs),
                sums[: len(places)],
            )

        steps = [
            (1, functools.partial(step, k, inputs))
            for k in range(KERNEL)
            for inputs in halves(taps.shape[2])
        ]
        return steps + [(1, matrix.flush)]

    def gate_values(self, values, gated, table, columns):
        gated_values = snake(
            values + entry(table, self.unit, WIDE, columns),
            entry(table, self.unit, MID_RATE, columns),
            entry(table, self.unit, MID_SCALE, columns),
        )
        return gated_values.astype(jnp.bfloat16)

    def gate(self, middle, gated, table, columns):
        def step(rows):
            gated[rows, columns] = self.gate_values(middle[rows, columns], gated, table, columns)

        return [
            (20, functools.partial(step, slice(row, row + SEGMENTS)))
            for row in range(0, self.rows, SEGMENTS)
        ]

    def gate_sums(self, sums, gated, table):
        def step(i):
            rows = slice(i * SEGMENTS, (i + 1) * SEGMENTS)
            for unit, columns in enumerate(halves(gated.shape[1])):
                values = pltpu.matmul_pop(sums[i][unit])
                gated[rows, columns] = self.gate_values(values, gated, table, columns)

        return [(40, functools.partial(step, i)) for i in range(self.rows // SEGMENTS)]

    def project(self, matrix, sources, point, sums):
        def rows(gated, columns, i):
            return gated[i * SEGMENTS : (i + 1) * SEGMENTS, columns]

        def step(gated, inputs):
            matrix.tile(
                lambda columns: point[self.unit, inputs, columns],
                functools.partial(rows, gated, inputs),
                sums[: self.rows // SEGMENTS],
            )

        steps = [(5, functools.partial(step, gated, columns)) for gated, columns in sources]
        return steps + [(5, matrix.flush)]

    def finish(self, sums, table, x_rows, x_next, s_next=None):
        steps = []

        def step(i, first, j, length):
            starts, stride = self.starts(first, j, length)
            update = [pltpu.matmul_pop(sums[i][unit]) for unit in range(2)]
            for half in range(2):
                where = run_of(starts[half], stride)
                rows = slice(half * 8, half * 8 + 8)
                for c in range(x_rows.shape[0]):
                    unit, group = divmod(c, WIDTH // LANES)
                    change = update[unit][rows, lane(group)] + entry(
                        table, self.unit, POINT, lane(c)
                    )
                    current = rounded(x_rows[c, where, :] + change)
                    x_next[c, where, :] = current
                    if s_next is not None:
                        s_next[c, where, :] = snake_in(table, self.unit + 1, c, current)

        for first, length in self.pieces:
            for j in range(length):
                cost = 25 if s_next is None else 50
                steps.append(
                    (cost, functools.partial(step, len(steps), first, j, length))
                )
        return steps


def run_of(start, stride):
    return pl.ds(start, 8) if stride == 1 else pl.ds(start, 8, stride=stride)


def snake_in(table, unit, c, values):
    return snake(
        values, entry(table, unit, IN_RATE, lane(c)), entry(table, unit, IN_SCALE, lane(c))
    )


def weave(main, others=()):
    whole = sum(cost for cost, _ in others)
    spent, at = 0, 0
    for i, (_, step) in enumerate(main):
        step()
        while at < len(others) and (i + 1 == len(main) or spent * len(main) < whole * (i + 1)):
            spent += others[at][0]
            others[at][1]()
            at += 1


def run(steps):
    for _, step in steps:
        step()


def halves(channels):
    return slice(0, channels // 2), slice(channels // 2, channels)


def parts(frames):
    inner = (
        Part(0, [(8, frames // SEGMENTS - 6)]),
        Part(1, [(20, frames // SEGMENTS - 7)]),
        Part(2, [(48, frames // SEGMENTS - 11)]),
    )
    outer = (
        Part(0, [(-36, 3), (frames - 88, 8)]),
        Part(1, [(-28, 3), (frames - 100, 8)], plain=True),
        Part(2, [(0, 3), (frames - 128, 8)], plain=True),
    )
    return inner, outer


def place():
    return lax.axis_index("tm")


def edges_kernel(up_hbm, to_far, to_near, held, sems):
    frames = up_hbm.shape[1]
    copies = []
    for part in range(2):
        for end, row in enumerate((0, frames - SENT)):
            copies.append(
                pltpu.make_async_copy(
                    up_hbm.at[part, pl.ds(row, SENT)], held.at[part, end], sems.at[part, end]
                )
            )
    for copy in copies:
        copy.start()
    for copy in copies:
        copy.wait()
    odd = place() % 2 == 1
    for c in range(up_hbm.shape[2] // LANES):
        own_low, own_high = (held[0, end, :, lane(c)].astype(jnp.float32) for end in range(2))
        low, high = (held[1, end, :, lane(c)].astype(jnp.float32) for end in range(2))
        none = jnp.zeros((STRIDE, LANES), jnp.float32)
        to_next = jnp.concatenate([own_high[STRIDE:], none], axis=0) + high
        to_last = own_low + jnp.concatenate([none, low[:HALO]], axis=0)
        to_far[:, lane(c)] = jnp.where(odd, to_next, to_last).astype(jnp.bfloat16)
        to_near[:, lane(c)] = jnp.where(odd, to_last, to_next).astype(jnp.bfloat16)


def first_kernel(
    up, wide, point, alpha_in, beta_in, alpha_mid, beta_mid, x_rows, s_rows, tiles, table
):
    frames = up.shape[1]
    rows = (
        alpha_in[...] / math.pi, 1 / beta_in[...], alpha_mid[...] / math.pi, 1 / beta_mid[...],
        wide[...], point[...],
    )
    for which, value in enumerate(rows):
        for unit in range(UNITS):
            row = unit * TABLE + which
            table[row : row + 1, :] = value[unit : unit + 1, :]
    for c in range(x_rows.shape[0]):
        later = up[1, :, lane(c)].astype(jnp.float32)
        none = jnp.zeros((STRIDE, LANES), jnp.float32)
        own = up[0, :, lane(c)].astype(jnp.float32)
        current = rounded(own + jnp.concatenate([none, later[: frames - STRIDE]], axis=0))
        table[UNITS * TABLE :, lane(c)] = later[frames - STRIDE :]
        x_rows[c, LEFT : LEFT + frames, :] = current
        s_rows[c, LEFT : LEFT + frames, :] = snake_in(table, 0, c, current)
    run(parts(frames)[0][0].gather(s_rows, tiles))


def inner_kernel(frames, tiles, table, taps, middle, gated):
    part = parts(frames)[0][0]
    first, _ = halves(middle.shape[1])
    steps = part.conv(tiles, taps, middle)
    weave(steps[:KERNEL])
    weave(steps[KERNEL:], part.gate(middle, gated, table, first))


def outer_kernel(
    tracks,
    x_first, s_first, first_middle, first_gated, from_chip, from_far, table, taps, point,
    out,
    x_0, x_1, x_2, s_0, s_1, s_2, inner_tiles, outer_tiles, gated,
):
    inner, outer = parts(out.shape[0])

    def sums(*of):
        one = [pltpu.ACC(unit)((SEGMENTS, WIDTH), jnp.float32) for unit in range(2)]
        return [one] * (max(part.rows for part in of) // SEGMENTS)

    def scoped(inner_sums, outer_sums, update_sums):
        outer_body(
            tracks,
            x_first, s_first, first_middle, first_gated, from_chip, from_far, table, taps,
            point, out,
            x_0, x_1, x_2, s_0, s_1, s_2, inner_tiles, outer_tiles, gated,
            inner_sums, outer_sums, update_sums,
        )

    pl.run_scoped(scoped, sums(*inner[1:]), sums(*outer), sums(*inner, *outer))


def outer_body(
    tracks,
    x_first, s_first, first_middle, first_gated, from_chip, from_far, table, taps, point,
    out,
    x_0, x_1, x_2, s_0, s_1, s_2, inner_tiles, outer_tiles, gated,
    inner_sums, outer_sums, update_sums,
):
    frames, channels = out.shape
    groups = x_0.shape[0]
    end_row = LEFT + frames
    odd = place() % 2 == 1
    is_first = place() == 0
    is_last = place() == tracks - 1
    inner, outer = parts(frames)
    both = halves(channels)

    def clear_outside(s_rows):
        def step(c):
            s_rows[c, 0:LEFT, :] = jnp.where(is_first, 0.0, s_rows[c, 0:LEFT, :])
            s_rows[c, end_row:, :] = jnp.where(is_last, 0.0, s_rows[c, end_row:, :])

        return [(10, functools.partial(step, c)) for c in range(groups)]

    def store(begin, end):
        def step(c, row):
            rows = slice(LEFT + row, LEFT + row + SEGMENTS)
            out[row : row + SEGMENTS, lane(c)] = x_0[c, rows, :].astype(jnp.bfloat16)

        return [
            (2, functools.partial(step, c, row))
            for row in range(begin, end, SEGMENTS)
            for c in range(groups)
        ]

    matrix = Matrix()

    def after(part, sums, x_rows, x_next, s_next):
        return (
            part.gate_sums(sums, gated, table)
            + part.project(matrix, [(gated, columns) for columns in both], point, update_sums)
            + part.finish(update_sums, table, x_rows, x_next, s_next)
        )

    low_end = LEFT + 2 * STRIDE
    kept = LEFT + outer[0].pieces[1][0] - 8
    for c in range(groups):
        chip = from_chip[:, lane(c)].astype(jnp.float32)
        far = from_far[:, lane(c)].astype(jnp.float32)
        before = jnp.where(odd, chip, far)
        behind = jnp.where(odd, far, chip)
        carried = jnp.where(is_first, 0.0, before[HALO:SENT])
        own_low = x_first[c, LEFT:low_end, :]
        low = jnp.concatenate(
            [before[:HALO], rounded(own_low[:STRIDE] + carried), own_low[STRIDE:]], axis=0
        )
        joint = rounded(behind[:STRIDE] + table[UNITS * TABLE :, lane(c)])
        high = jnp.concatenate([joint, behind[STRIDE:HALO]], axis=0)
        x_0[c, LEFT - HALO : low_end, :] = low
        s_0[c, LEFT - HALO : low_end, :] = snake_in(table, 0, c, low)
        x_0[c, kept:end_row, :] = x_first[c, kept:end_row, :]
        s_0[c, kept:end_row, :] = s_first[c, kept:end_row, :]
        x_0[c, end_row : end_row + HALO, :] = high
        s_0[c, end_row : end_row + HALO, :] = snake_in(table, 0, c, high)
    run(clear_outside(s_0))
    run(outer[0].gather(s_0, outer_tiles))

    weave(
        outer[0].conv_sums(matrix, outer_tiles, taps, outer_sums),
        inner[0].gate(first_middle, gated, table, both[1])
        + inner[0].project(
            matrix, [(first_gated, both[0]), (gated, both[1])], point, update_sums
        )
        + inner[0].finish(update_sums, table, x_first, x_1, s_1)
        + inner[1].gather(s_1, inner_tiles),
    )
    weave(
        inner[1].conv_sums(matrix, inner_tiles, taps, inner_sums),
        after(outer[0], outer_sums, x_0, x_1, s_1)
        + clear_outside(s_1)
        + outer[1].gather(s_1, outer_tiles),
    )
    weave(
        outer[1].conv_sums(matrix, outer_tiles, taps, outer_sums),
        after(inner[1], inner_sums, x_1, x_2, s_2) + inner[2].gather(s_2, inner_tiles),
    )
    weave(
        inner[2].conv_sums(matrix, inner_tiles, taps, inner_sums),
        after(outer[1], outer_sums, x_1, x_2, s_2)
        + clear_outside(s_2)
        + outer[2].gather(s_2, outer_tiles),
    )
    begin = inner[2].pieces[0][0]
    end = begin + inner[2].rows
    weave(
        outer[2].conv_sums(matrix, outer_tiles, taps, outer_sums),
        after(inner[2], inner_sums, x_2, x_0, None) + store(begin, end),
    )
    run(after(outer[2], outer_sums, x_2, x_0, None))
    run(store(0, begin) + store(end, frames))


def swaps(groups, count):
    near, far = [], []
    for group in range(groups):
        for index in range(count):
            me = group * count + index
            near.append((me, group * count + (index ^ 1)))
            if index == 0 or index == count - 1:
                far.append((me, (group ^ 1) * count + index))
            else:
                far.append((me, me + 1 if index % 2 else me - 1))
    return near, far


VMEM = pl.BlockSpec(memory_space=pltpu.VMEM)
HBM = pl.BlockSpec(memory_space=pltpu.HBM)


def in_hbm(value):
    return pltpu.with_memory_space_constraint(value, pltpu.HBM)


VMEM = pl.BlockSpec(memory_space=pltpu.VMEM)
HBM = pl.BlockSpec(memory_space=pltpu.HBM)


def in_hbm(value):
    return pltpu.with_memory_space_constraint(value, pltpu.HBM)


def per_device(
    upsampled, taps, bias_wide, pointwise, bias_point, alpha_in, beta_in, alpha_mid, beta_mid
):
    frames, channels = upsampled.shape[1:]
    count = lax.axis_size("tm")
    near, far = swaps(lax.axis_size("grp"), count)
    groups = channels // LANES
    rows = frames + 2 * LEFT
    half = jnp.bfloat16
    params = (bias_wide, bias_point, alpha_in, beta_in, alpha_mid, beta_mid)
    limit = pltpu.CompilerParams(vmem_limit_bytes=16 * 2**20)

    sent = jax.ShapeDtypeStruct((SENT, channels), half)
    to_far, to_near = pl.pallas_call(
        edges_kernel,
        out_shape=(sent, sent),
        in_specs=[HBM],
        out_specs=(VMEM,) * 2,
        scratch_shapes=[
            pltpu.VMEM((2, 2, SENT, channels), half),
            pltpu.SemaphoreType.DMA((2, 2)),
        ],
        compiler_params=limit,
        cost_estimate=pl.CostEstimate(
            flops=6 * 10**9, bytes_accessed=upsampled.size * 2, transcendentals=0
        ),
        name="edges",
    )(in_hbm(upsampled))

    from_far = lax.ppermute(to_far, ("grp", "tm"), far)
    from_chip = lax.ppermute(to_near, ("grp", "tm"), near)

    inner, outer = parts(frames)
    natural = (groups, rows, LANES)
    single = jnp.float32

    def tiles(*of):
        return max(part.tiles for part in of) * SEGMENTS, channels

    def most(*of):
        return max(part.rows for part in of), channels

    x_first, s_first, first_tiles, table = pl.pallas_call(
        first_kernel,
        out_shape=(
            jax.ShapeDtypeStruct(natural, single),
            jax.ShapeDtypeStruct(natural, single),
            jax.ShapeDtypeStruct(tiles(inner[0]), half),
            jax.ShapeDtypeStruct((UNITS * TABLE + STRIDE, channels), single),
        ),
        in_specs=[VMEM] * 7,
        out_specs=(VMEM,) * 4,
        compiler_params=limit,
        name="first",
    )(upsampled, *params)

    first_middle, first_gated = pl.pallas_call(
        functools.partial(inner_kernel, frames),
        out_shape=(
            jax.ShapeDtypeStruct(most(inner[0]), single),
            jax.ShapeDtypeStruct(most(inner[0]), half),
        ),
        in_specs=[VMEM] * 3,
        out_specs=(VMEM,) * 2,
        compiler_params=limit,
        cost_estimate=pl.CostEstimate(
            flops=2 * KERNEL * inner[0].rows * channels**2,
            bytes_accessed=taps.size * 2,
            transcendentals=0,
        ),
        name="inner",
    )(first_tiles, table, taps)

    return pl.pallas_call(
        functools.partial(outer_kernel, count),
        out_shape=jax.ShapeDtypeStruct((frames, channels), half),
        in_specs=[VMEM] * 9,
        out_specs=VMEM,
        scratch_shapes=[pltpu.VMEM(natural, single)] * 6
        + [
            pltpu.VMEM(tiles(*inner[1:]), half),
            pltpu.VMEM(tiles(*outer), half),
            pltpu.VMEM(most(*inner, *outer), half),
        ],
        compiler_params=pltpu.CompilerParams(vmem_limit_bytes=24 * 2**20),
        name="outer",
    )(
        x_first, s_first, first_middle, first_gated, from_chip, from_far,
        table, taps, pointwise,
    )


def solution(mesh):
    placed = (P(None, ("grp", "tm"), None), P(), P(), P(), P(), P(), P(), P(), P())
    return jax.shard_map(
        per_device, mesh=mesh, in_specs=placed, out_specs=P(("grp", "tm"), None), check_vma=False
    )
```

time: 14.2 us -> 13.7 us (0.965)
  waiting for transfers between devices: 0.85 us -> 0.4 us
  Pallas kernels: 10.7 us -> 10.4 us
  local copies, waits for them, and re-layouts: 0.45 us -> 0.73 us
    ppermute x1, waiting for transfers between devices: 0.85 us -> 0.4 us  [per_device(): from_far = lax.ppermute(to_far, ('grp', 'tm'), far)]
    pallas_call x1, Pallas kernels: 1.46 us -> 1.09 us  [per_device(): pl.pallas_call(edges_kernel, out_shape=(sent, sent), in_specs=[HBM], out_...]
    unnamed x4 -> x18, local copies, waits for them, and re-layouts: 0.45 us -> 0.73 us
    pallas_call x1, Pallas kernels: 0.59 us -> 0.73 us  [per_device(): pl.pallas_call(first_kernel, out_shape=(jax.ShapeDtypeStruct(natural, sin...]
    pallas_call x1, Pallas kernels: 7.36 us -> 7.22 us  [per_device(): pl.pallas_call(functools.partial(outer_kernel, count), out_shape=jax.Shap...]
  transfers between devices with their start and end apart: 2 -> 2, of which waited for: 1 -> 1; matrix products, arithmetic and copies ran while one was open for 0% -> 0% of each run, Pallas kernels for 14% -> 15%
where the time goes in v4:
time: 13.7 us; the launch traced here: 13.5 us
  Pallas kernels  10.4 us (76%)
  starting transfers between devices  1.94 us (14%)
  local copies, waits for them, and re-layouts  0.73 us (5%)
  waiting for transfers between devices  0.4 us (3%)
    pallas_call x1, Pallas kernels, per_device(): pl.pallas_call(functools.partial(outer_kernel, count), out_shape=jax.Shap...  7.22 us
    pallas_call x1, Pallas kernels, per_device(): pl.pallas_call(functools.partial(inner_kernel, frames), out_shape=(jax.Sh...  1.32 us
    ppermute x1, starting transfers between devices, per_device(): from_far = lax.ppermute(to_far, ('grp', 'tm'), far)  1.2 us
    pallas_call x1, Pallas kernels, per_device(): pl.pallas_call(edges_kernel, out_shape=(sent, sent), in_specs=[HBM], out_...  1.09 us
    ppermute x1, starting transfers between devices, per_device(): from_chip = lax.ppermute(to_near, ('grp', 'tm'), near)  0.74 us
    unnamed x18, local copies, waits for them, and re-layouts  0.73 us
    pallas_call x1, Pallas kernels, per_device(): pl.pallas_call(first_kernel, out_shape=(jax.ShapeDtypeStruct(natural, sin...  0.73 us
    ppermute x1, waiting for transfers between devices, per_device(): from_far = lax.ppermute(to_far, ('grp', 'tm'), far)  0.4 us
  transfers between devices with their start and end apart: 2, of which 1 were waited for; matrix products, arithmetic and copies ran while one was open for 0% of the time, Pallas kernels for 15%

profile of v4, /device:TPU:5, one launch (start us, length us, event | category | flops | bytes accessed | tf_op | source)
XLA Modules:
  0.0 13.5 jit_solution(9710634432955785755)
XLA Ops:
  0.0 0.0 copy-start.2
  0.0 0.0 copy-start.3
  0.0 0.0 copy-start.4
  0.0 0.0 copy-start.5
  0.0 0.0 copy-start.6
  0.0 0.0 copy-start.7
  0.0 0.0 copy-start.8
  0.0 0.0 copy-start
  0.1 1.1 %edges.1 = (bf16[48,512]{1,0:T(8,128)(2,1)S(1)}, bf16[48,512]{1,0:T(8,128)(2,1)S(1)}) custom-call(bf16[2,384,512]{2,1,0:T(8,128)(2,1)} %up_hbm.1), custom_call_target="tpu_custom_call" | custom-call | flops 6000000000 | bytes 786432 | tf_op jit(solution)/shard_map/edges/pallas_call | solution.py:513
  1.2 0.0 copy-start.1
  1.2 0.7 %collective-permute-start = (bf16[48,512]{1,0:T(8,128)(2,1)S(1)}, bf16[48,512]{1,0:T(8,128)(2,1)S(1)}, u32[]{:S(2)}, u32[]{:S(2)}) collective-permute-start(bf16[48,512]{1,0:T(8,128)(2,1)S(1)} %get-tuple-element.19), channel_id=1, source_target_pairs={{0,1},{1,0},{2,3},{3,2},{4,5},{5,4},{6,7},{7,6},{8,9},{9,8},{10,11... | collective-permute-start | bytes 147464 | tf_op jit(solution)/shard_map/ppermute | solution.py:530
  1.9 1.2 %collective-permute-start.1 = (bf16[48,512]{1,0:T(8,128)(2,1)S(1)}, bf16[48,512]{1,0:T(8,128)(2,1)S(1)}, u32[]{:S(2)}, u32[]{:S(2)}) collective-permute-start(bf16[48,512]{1,0:T(8,128)(2,1)S(1)} %get-tuple-element.20), channel_id=1, source_target_pairs={{0,16},{1,2},{2,1},{3,4},{4,3},{5,6},{6,5},{7,8},{8,7},{9,10},{10,... | collective-permute-start | bytes 147464 | tf_op jit(solution)/shard_map/ppermute | solution.py:529
  3.1 0.0 copy-done.2
  3.1 0.0 copy-done.3
  3.1 0.0 copy-done.4
  3.1 0.0 copy-done.5
  3.1 0.0 copy-done.6
  3.1 0.0 copy-done.7
  3.1 0.0 copy-done.8
  3.2 0.7 %first.1 = (f32[4,480,128]{2,1,0:T(8,128)S(1)}, f32[4,480,128]{2,1,0:T(8,128)S(1)}, bf16[384,512]{1,0:T(8,128)(2,1)S(1)}, f32[32,512]{1,0:T(8,128)S(1)}) custom-call(bf16[2,384,512]{2,1,0:T(8,128)(2,1)S(1)} %copy-done.2, f32[3,512]{1,0:T(4,128)S(1)} %copy-done.3, f32[3,512]{1,0:T(4,128)S(1)} %copy-done.4, f32[3,512]{1,0:T(4,128)S(1)} %copy-done.5, ...), custom_call_target="tpu_custom_call" | custom-call | tf_op jit(solution)/shard_map/first/pallas_call | solution.py:542
  3.9 0.7 %copy-done = bf16[3,7,512,512]{3,2,1,0:T(8,128)(2,1)S(1)} copy-done((bf16[3,7,512,512]{3,2,1,0:T(8,128)(2,1)S(1)}, bf16[3,7,512,512]{3,2,1,0:T(8,128)(2,1)}, u32[]{:S(2)}) %copy-start) | copy-done | bytes 11010072
  4.6 1.3 %inner.1 = (f32[288,512]{1,0:T(8,128)S(1)}, bf16[288,512]{1,0:T(8,128)(2,1)S(1)}) custom-call(bf16[384,512]{1,0:T(8,128)(2,1)S(1)} %get-tuple-element.15.tiles, f32[32,512]{1,0:T(8,128)S(1)} %get-tuple-element.16.table, bf16[3,7,512,512]{3,2,1,0:T(8,128)(2,1)S(1)} %copy-done), custom_call_target="tpu_custom_call" | custom-call | flops 1056964608 | bytes 11010048 | tf_op jit(solution)/shard_map/inner/pallas_call | solution.py:556
  5.9 0.0 collective-permute-done.from_chip
  5.9 0.4 %collective-permute-done.1.from_far = bf16[48,512]{1,0:T(8,128)(2,1)S(1)} collective-permute-done((bf16[48,512]{1,0:T(8,128)(2,1)S(1)}, bf16[48,512]{1,0:T(8,128)(2,1)S(1)}, u32[]{:S(2)}, u32[]{:S(2)}) %collective-permute-start.1) | collective-permute-done | bytes 49184 | tf_op jit(solution)/shard_map/ppermute | solution.py:529
  6.3 0.0 copy-done.1
  6.3 7.2 %outer.1 = bf16[384,512]{1,0:T(8,128)(2,1)} custom-call(f32[4,480,128]{2,1,0:T(8,128)S(1)} %get-tuple-element.13.x_first, f32[4,480,128]{2,1,0:T(8,128)S(1)} %get-tuple-element.14.s_first, f32[288,512]{1,0:T(8,128)S(1)} %get-tuple-element.17.first_middle, bf16[288,512]{1,0:T(8,128)(2,1)S(1)} %get-tuple-element.18.first_gated, ...), custom_call_target="tpu_custom_call" | custom-call | tf_op jit(solution)/shard_map/outer/pallas_call | solution.py:573
Async XLA Ops:
  0.0 3.1 %copy-start.2 = (bf16[2,384,512]{2,1,0:T(8,128)(2,1)S(1)}, bf16[2,384,512]{2,1,0:T(8,128)(2,1)}, u32[]{:S(2)}) copy-start(bf16[2,384,512]{2,1,0:T(8,128)(2,1)} %up_hbm.1) | copy-start | bytes 2359300
  0.0 3.1 %copy-start.3 = (f32[3,512]{1,0:T(4,128)S(1)}, f32[3,512]{1,0:T(4,128)}, u32[]{:S(2)}) copy-start(f32[3,512]{1,0:T(4,128)} %wide.1) | copy-start | bytes 18436
  0.0 3.1 %copy-start.4 = (f32[3,512]{1,0:T(4,128)S(1)}, f32[3,512]{1,0:T(4,128)}, u32[]{:S(2)}) copy-start(f32[3,512]{1,0:T(4,128)} %point.2) | copy-start | bytes 18436
  0.0 3.1 %copy-start.5 = (f32[3,512]{1,0:T(4,128)S(1)}, f32[3,512]{1,0:T(4,128)}, u32[]{:S(2)}) copy-start(f32[3,512]{1,0:T(4,128)} %alpha_in.1) | copy-start | bytes 18436
  0.0 3.1 %copy-start.6 = (f32[3,512]{1,0:T(4,128)S(1)}, f32[3,512]{1,0:T(4,128)}, u32[]{:S(2)}) copy-start(f32[3,512]{1,0:T(4,128)} %beta_in.1) | copy-start | bytes 18436
  0.0 3.1 %copy-start.7 = (f32[3,512]{1,0:T(4,128)S(1)}, f32[3,512]{1,0:T(4,128)}, u32[]{:S(2)}) copy-start(f32[3,512]{1,0:T(4,128)} %alpha_mid.1) | copy-start | bytes 18436
  0.0 3.1 %copy-start.8 = (f32[3,512]{1,0:T(4,128)S(1)}, f32[3,512]{1,0:T(4,128)}, u32[]{:S(2)}) copy-start(f32[3,512]{1,0:T(4,128)} %beta_mid.1) | copy-start | bytes 18436
  0.0 4.5 %copy-start = (bf16[3,7,512,512]{3,2,1,0:T(8,128)(2,1)S(1)}, bf16[3,7,512,512]{3,2,1,0:T(8,128)(2,1)}, u32[]{:S(2)}) copy-start(bf16[3,7,512,512]{3,2,1,0:T(8,128)(2,1)} %taps.3) | copy-start | bytes 33030148
  1.2 5.2 %copy-start.1 = (bf16[3,512,512]{2,1,0:T(8,128)(2,1)S(1)}, bf16[3,512,512]{2,1,0:T(8,128)(2,1)}, u32[]{:S(2)}) copy-start(bf16[3,512,512]{2,1,0:T(8,128)(2,1)} %point.3) | copy-start | bytes 4718596
  1.2 4.8 %collective-permute-start = (bf16[48,512]{1,0:T(8,128)(2,1)S(1)}, bf16[48,512]{1,0:T(8,128)(2,1)S(1)}, u32[]{:S(2)}, u32[]{:S(2)}) collective-permute-start(bf16[48,512]{1,0:T(8,128)(2,1)S(1)} %get-tuple-element.19), channel_id=1, source_target_pairs={{0,1},{1,0},{2,3},{3,2},{4,5},{5,4},{6,7},{7,6},{8,9},{9,8},{10,11... | collective-permute-start | bytes 147464 | tf_op jit(solution)/shard_map/ppermute | solution.py:530
  1.9 4.4 %collective-permute-start.1 = (bf16[48,512]{1,0:T(8,128)(2,1)S(1)}, bf16[48,512]{1,0:T(8,128)(2,1)S(1)}, u32[]{:S(2)}, u32[]{:S(2)}) collective-permute-start(bf16[48,512]{1,0:T(8,128)(2,1)S(1)} %get-tuple-element.20), channel_id=1, source_target_pairs={{0,16},{1,2},{2,1},{3,4},{4,3},{5,6},{6,5},{7,8},{8,7},{9,10},{10,... | collective-permute-start | bytes 147464 | tf_op jit(solution)/shard_map/ppermute | solution.py:529

commit v5 on v4

--- a/solution.py
+++ b/solution.py
@@ -17,20 +17,21 @@
 SENT = 48
 HALO = 40
 SEGMENTS = 16
-TABLE = 8
-IN_RATE, IN_SCALE, MID_RATE, MID_SCALE, WIDE, POINT = range(6)
-
-SINE = (9.86952481, -32.46513948, 42.64342537, -29.42627071, 10.5812946)
-
-
-def snake(values, rate, scale):
-    turns = values * rate
+TABLE = 16
+IN, MID, WIDE, POINT = 0, 5, 10, 11
+
+SINE = (3.141582022, -5.167142795, 2.541899018, -0.5546361724)
+
+
+def snake(values, rates):
+    turns = values * rates[0]
     rest = turns - jnp.round(turns)
     square = rest * rest
-    sine = jnp.float32(SINE[4])
-    for coefficient in SINE[3::-1]:
-        sine = sine * square + jnp.float32(coefficient)
-    return values + (sine * square) * scale
+    sine = rates[-1]
+    for coefficient in rates[-2:0:-1]:
+        sine = sine * square + coefficient
+    sine = sine * rest
+    return values + sine * sine
 
 
 def rounded(values):
@@ -47,6 +48,10 @@
 
 
 WIDTH = 256
+
+
+def rates(table, unit, which, lanes):
+    return [entry(table, unit, which + i, lanes) for i in range(5)]
 
 
 class Matrix:
@@ -94,7 +99,7 @@
         return (start, start + 8 * length), length
 
     def gather(self, s_rows, tiles):
-        steps = []
+        steps = [[] for _ in range(KERNEL)]
 
         def step(at, first, j, length):
             rows = slice(at * SEGMENTS, (at + 1) * SEGMENTS)
@@ -104,18 +109,20 @@
                 tiles[rows, lane(c)] = jnp.concatenate(both, axis=0).astype(jnp.bfloat16)
 
         reach = 3 * self.dilation
-        if self.plain:
-            for k in range(KERNEL):
-                for first, length in self.pieces:
-                    first += (k - 3) * self.dilation
-                    for j in range(length):
-                        steps.append((10, functools.partial(step, len(steps), first, j, length)))
-            return steps
-        for first, length in self.pieces:
-            for j in range(length + 2 * reach):
-                steps.append(
-                    (10, functools.partial(step, len(steps), first - reach, j, length))
-                )
+        for k in range(KERNEL):
+            at = 0
+            for first, length in self.pieces:
+                if self.plain:
+                    away = first + (k - 3) * self.dilation
+                    new = [(k * self.rows // SEGMENTS + at + j, away, j) for j in range(length)]
+                    at += length
+                else:
+                    begin = length + (k - 1) * self.dilation if k else 0
+                    end = length + k * self.dilation
+                    new = [(at + j, first - reach, j) for j in range(begin, end)]
+                    at += length + 2 * reach
+                for tile, start, j in new:
+                    steps[k].append((10, functools.partial(step, tile, start, j, length)))
         return steps
 
     def window(self, tiles, k):
@@ -174,8 +181,7 @@
     def gate_values(self, values, gated, table, columns):
         gated_values = snake(
             values + entry(table, self.unit, WIDE, columns),
-            entry(table, self.unit, MID_RATE, columns),
-            entry(table, self.unit, MID_SCALE, columns),
+            rates(table, self.unit, MID, columns),
         )
         return gated_values.astype(jnp.bfloat16)
 
@@ -195,7 +201,7 @@
                 values = pltpu.matmul_pop(sums[i][unit])
                 gated[rows, columns] = self.gate_values(values, gated, table, columns)
 
-        return [(40, functools.partial(step, i)) for i in range(self.rows // SEGMENTS)]
+        return [(20, functools.partial(step, i)) for i in range(self.rows // SEGMENTS)]
 
     def project(self, matrix, sources, point, sums):
         def rows(gated, columns, i):
@@ -244,17 +250,19 @@
 
 
 def snake_in(table, unit, c, values):
-    return snake(
-        values, entry(table, unit, IN_RATE, lane(c)), entry(table, unit, IN_SCALE, lane(c))
-    )
-
-
-def weave(main, others=()):
+    return snake(values, rates(table, unit, IN, lane(c)))
+
+
+def weave(main, others=(), own=(), lead=0):
     whole = sum(cost for cost, _ in others)
     spent, at = 0, 0
     for i, (_, step) in enumerate(main):
         step()
-        while at < len(others) and (i + 1 == len(main) or spent * len(main) < whole * (i + 1)):
+        if i // 2 + 1 < len(own):
+            late = own[i // 2 + 1]
+            run(late[: len(late) // 2] if i % 2 == 0 else late[len(late) // 2 :])
+        share = max(0, i + 1 - lead) / (len(main) - lead)
+        while at < len(others) and (i + 1 == len(main) or spent < whole * share):
             spent += others[at][0]
             others[at][1]()
             at += 1
@@ -316,11 +324,11 @@
     up, wide, point, alpha_in, beta_in, alpha_mid, beta_mid, x_rows, s_rows, tiles, table
 ):
     frames = up.shape[1]
-    rows = (
-        alpha_in[...] / math.pi, 1 / beta_in[...], alpha_mid[...] / math.pi, 1 / beta_mid[...],
-        wide[...], point[...],
-    )
-    for which, value in enumerate(rows):
+    rows = []
+    for alpha, beta in ((alpha_in, beta_in), (alpha_mid, beta_mid)):
+        root = jnp.sqrt(1 / beta[...])
+        rows += [alpha[...] / math.pi] + [root * coefficient for coefficient in SINE]
+    for which, value in enumerate(rows + [wide[...], point[...]]):
         for unit in range(UNITS):
             row = unit * TABLE + which
             table[row : row + 1, :] = value[unit : unit + 1, :]
@@ -332,7 +340,7 @@
         table[UNITS * TABLE :, lane(c)] = later[frames - STRIDE :]
         x_rows[c, LEFT : LEFT + frames, :] = current
         s_rows[c, LEFT : LEFT + frames, :] = snake_in(table, 0, c, current)
-    run(parts(frames)[0][0].gather(s_rows, tiles))
+    run(sum(parts(frames)[0][0].gather(s_rows, tiles), []))
 
 
 def inner_kernel(frames, tiles, table, taps, middle, gated):
@@ -431,8 +439,10 @@
         x_0[c, end_row : end_row + HALO, :] = high
         s_0[c, end_row : end_row + HALO, :] = snake_in(table, 0, c, high)
     run(clear_outside(s_0))
-    run(outer[0].gather(s_0, outer_tiles))
-
+    lead = 1
+    own = outer[0].gather(s_0, outer_tiles)
+    run(own[0])
+    coming = inner[1].gather(s_1, inner_tiles)
     weave(
         outer[0].conv_sums(matrix, outer_tiles, taps, outer_sums),
         inner[0].gate(first_middle, gated, table, both[1])
@@ -440,29 +450,37 @@
             matrix, [(first_gated, both[0]), (gated, both[1])], point, update_sums
         )
         + inner[0].finish(update_sums, table, x_first, x_1, s_1)
-        + inner[1].gather(s_1, inner_tiles),
-    )
+        + coming[0],
+        own,
+    )
+    own, coming = coming, outer[1].gather(s_1, outer_tiles)
     weave(
         inner[1].conv_sums(matrix, inner_tiles, taps, inner_sums),
-        after(outer[0], outer_sums, x_0, x_1, s_1)
-        + clear_outside(s_1)
-        + outer[1].gather(s_1, outer_tiles),
-    )
+        after(outer[0], outer_sums, x_0, x_1, s_1) + clear_outside(s_1) + coming[0],
+        own,
+        lead,
+    )
+    own, coming = coming, inner[2].gather(s_2, inner_tiles)
     weave(
         outer[1].conv_sums(matrix, outer_tiles, taps, outer_sums),
-        after(inner[1], inner_sums, x_1, x_2, s_2) + inner[2].gather(s_2, inner_tiles),
-    )
+        after(inner[1], inner_sums, x_1, x_2, s_2) + coming[0],
+        own,
+        lead,
+    )
+    own, coming = coming, outer[2].gather(s_2, outer_tiles)
     weave(
         inner[2].conv_sums(matrix, inner_tiles, taps, inner_sums),
-        after(outer[1], outer_sums, x_1, x_2, s_2)
-        + clear_outside(s_2)
-        + outer[2].gather(s_2, outer_tiles),
+        after(outer[1], outer_sums, x_1, x_2, s_2) + clear_outside(s_2) + coming[0],
+        own,
+        lead,
     )
     begin = inner[2].pieces[0][0]
     end = begin + inner[2].rows
     weave(
         outer[2].conv_sums(matrix, outer_tiles, taps, outer_sums),
         after(inner[2], inner_sums, x_2, x_0, None) + store(begin, end),
+        coming,
+        lead,
     )
     run(after(outer[2], outer_sums, x_2, x_0, None))
     run(store(0, begin) + store(end, frames))

time: 13.7 us -> 13.3 us (0.971)
  Pallas kernels: 10.4 us -> 9.91 us
    pallas_call x1, Pallas kernels: 7.22 us -> 6.85 us  [per_device(): pl.pallas_call(functools.partial(outer_kernel, count), out_shape=jax.Shap...]
where the time goes in v5:
time: 13.3 us; the launch traced here: 13.2 us
  Pallas kernels  9.91 us (75%)
  starting transfers between devices  1.94 us (15%)
  local copies, waits for them, and re-layouts  0.8 us (6%)
  waiting for transfers between devices  0.42 us (3%)
    pallas_call x1, Pallas kernels, per_device(): pl.pallas_call(functools.partial(outer_kernel, count), out_shape=jax.Shap...  6.85 us
    pallas_call x1, Pallas kernels, per_device(): pl.pallas_call(functools.partial(inner_kernel, frames), out_shape=(jax.Sh...  1.3 us
    ppermute x1, starting transfers between devices, per_device(): from_far = lax.ppermute(to_far, ('grp', 'tm'), far)  1.2 us
    pallas_call x1, Pallas kernels, per_device(): pl.pallas_call(edges_kernel, out_shape=(sent, sent), in_specs=[HBM], out_...  1.09 us
    unnamed x18, local copies, waits for them, and re-layouts  0.8 us
    ppermute x1, starting transfers between devices, per_device(): from_chip = lax.ppermute(to_near, ('grp', 'tm'), near)  0.74 us
    pallas_call x1, Pallas kernels, per_device(): pl.pallas_call(first_kernel, out_shape=(jax.ShapeDtypeStruct(natural, sin...  0.67 us
    ppermute x1, waiting for transfers between devices, per_device(): from_far = lax.ppermute(to_far, ('grp', 'tm'), far)  0.41 us
  transfers between devices with their start and end apart: 2, of which 1 were waited for; matrix products, arithmetic and copies ran while one was open for 0% of the time, Pallas kernels for 15%

profile of v5, /device:TPU:5, one launch (start us, length us, event | category | flops | bytes accessed | tf_op | source)
XLA Modules:
  0.0 13.2 jit_solution(16165032522140829769)
XLA Ops:
  0.0 0.0 copy-start.2
  0.0 0.0 copy-start.3
  0.0 0.0 copy-start.4
  0.0 0.0 copy-start.5
  0.0 0.0 copy-start.6
  0.0 0.0 copy-start.7
  0.0 0.0 copy-start.8
  0.0 0.0 copy-start
  0.1 1.1 %edges.1 = (bf16[48,512]{1,0:T(8,128)(2,1)S(1)}, bf16[48,512]{1,0:T(8,128)(2,1)S(1)}) custom-call(bf16[2,384,512]{2,1,0:T(8,128)(2,1)} %up_hbm.1), custom_call_target="tpu_custom_call" | custom-call | flops 6000000000 | bytes 786432 | tf_op jit(solution)/shard_map/edges/pallas_call | solution.py:531
  1.2 0.0 copy-start.1
  1.2 0.7 %collective-permute-start = (bf16[48,512]{1,0:T(8,128)(2,1)S(1)}, bf16[48,512]{1,0:T(8,128)(2,1)S(1)}, u32[]{:S(2)}, u32[]{:S(2)}) collective-permute-start(bf16[48,512]{1,0:T(8,128)(2,1)S(1)} %get-tuple-element.19), channel_id=1, source_target_pairs={{0,1},{1,0},{2,3},{3,2},{4,5},{5,4},{6,7},{7,6},{8,9},{9,8},{10,11... | collective-permute-start | bytes 147464 | tf_op jit(solution)/shard_map/ppermute | solution.py:548
  1.9 1.2 %collective-permute-start.1 = (bf16[48,512]{1,0:T(8,128)(2,1)S(1)}, bf16[48,512]{1,0:T(8,128)(2,1)S(1)}, u32[]{:S(2)}, u32[]{:S(2)}) collective-permute-start(bf16[48,512]{1,0:T(8,128)(2,1)S(1)} %get-tuple-element.20), channel_id=1, source_target_pairs={{0,16},{1,2},{2,1},{3,4},{4,3},{5,6},{6,5},{7,8},{8,7},{9,10},{10,... | collective-permute-start | bytes 147464 | tf_op jit(solution)/shard_map/ppermute | solution.py:547
  3.1 0.0 copy-done.2
  3.1 0.0 copy-done.3
  3.1 0.0 copy-done.4
  3.1 0.0 copy-done.5
  3.1 0.0 copy-done.6
  3.1 0.0 copy-done.7
  3.1 0.0 copy-done.8
  3.2 0.7 %first.1 = (f32[4,480,128]{2,1,0:T(8,128)S(1)}, f32[4,480,128]{2,1,0:T(8,128)S(1)}, bf16[384,512]{1,0:T(8,128)(2,1)S(1)}, f32[56,512]{1,0:T(8,128)S(1)}) custom-call(bf16[2,384,512]{2,1,0:T(8,128)(2,1)S(1)} %copy-done.2, f32[3,512]{1,0:T(4,128)S(1)} %copy-done.3, f32[3,512]{1,0:T(4,128)S(1)} %copy-done.4, f32[3,512]{1,0:T(4,128)S(1)} %copy-done.5, ...), custom_call_target="tpu_custom_call" | custom-call | tf_op jit(solution)/shard_map/first/pallas_call | solution.py:560
  3.8 0.8 %copy-done = bf16[3,7,512,512]{3,2,1,0:T(8,128)(2,1)S(1)} copy-done((bf16[3,7,512,512]{3,2,1,0:T(8,128)(2,1)S(1)}, bf16[3,7,512,512]{3,2,1,0:T(8,128)(2,1)}, u32[]{:S(2)}) %copy-start) | copy-done | bytes 11010072
  4.6 1.3 %inner.1 = (f32[288,512]{1,0:T(8,128)S(1)}, bf16[288,512]{1,0:T(8,128)(2,1)S(1)}) custom-call(bf16[384,512]{1,0:T(8,128)(2,1)S(1)} %get-tuple-element.15.tiles, f32[56,512]{1,0:T(8,128)S(1)} %get-tuple-element.16.table, bf16[3,7,512,512]{3,2,1,0:T(8,128)(2,1)S(1)} %copy-done), custom_call_target="tpu_custom_call" | custom-call | flops 1056964608 | bytes 11010048 | tf_op jit(solution)/shard_map/inner/pallas_call | solution.py:574
  5.9 0.0 collective-permute-done.from_chip
  5.9 0.4 %collective-permute-done.1.from_far = bf16[48,512]{1,0:T(8,128)(2,1)S(1)} collective-permute-done((bf16[48,512]{1,0:T(8,128)(2,1)S(1)}, bf16[48,512]{1,0:T(8,128)(2,1)S(1)}, u32[]{:S(2)}, u32[]{:S(2)}) %collective-permute-start.1) | collective-permute-done | bytes 49184 | tf_op jit(solution)/shard_map/ppermute | solution.py:547
  6.3 0.0 copy-done.1
  6.3 6.9 %outer.1 = bf16[384,512]{1,0:T(8,128)(2,1)} custom-call(f32[4,480,128]{2,1,0:T(8,128)S(1)} %get-tuple-element.13.x_first, f32[4,480,128]{2,1,0:T(8,128)S(1)} %get-tuple-element.14.s_first, f32[288,512]{1,0:T(8,128)S(1)} %get-tuple-element.17.first_middle, bf16[288,512]{1,0:T(8,128)(2,1)S(1)} %get-tuple-element.18.first_gated, ...), custom_call_target="tpu_custom_call" | custom-call | tf_op jit(solution)/shard_map/outer/pallas_call | solution.py:591
Async XLA Ops:
  0.0 3.1 %copy-start.2 = (bf16[2,384,512]{2,1,0:T(8,128)(2,1)S(1)}, bf16[2,384,512]{2,1,0:T(8,128)(2,1)}, u32[]{:S(2)}) copy-start(bf16[2,384,512]{2,1,0:T(8,128)(2,1)} %up_hbm.1) | copy-start | bytes 2359300
  0.0 3.1 %copy-start.3 = (f32[3,512]{1,0:T(4,128)S(1)}, f32[3,512]{1,0:T(4,128)}, u32[]{:S(2)}) copy-start(f32[3,512]{1,0:T(4,128)} %wide.1) | copy-start | bytes 18436
  0.0 3.1 %copy-start.4 = (f32[3,512]{1,0:T(4,128)S(1)}, f32[3,512]{1,0:T(4,128)}, u32[]{:S(2)}) copy-start(f32[3,512]{1,0:T(4,128)} %point.2) | copy-start | bytes 18436
  0.0 3.1 %copy-start.5 = (f32[3,512]{1,0:T(4,128)S(1)}, f32[3,512]{1,0:T(4,128)}, u32[]{:S(2)}) copy-start(f32[3,512]{1,0:T(4,128)} %alpha_in.1) | copy-start | bytes 18436
  0.0 3.1 %copy-start.6 = (f32[3,512]{1,0:T(4,128)S(1)}, f32[3,512]{1,0:T(4,128)}, u32[]{:S(2)}) copy-start(f32[3,512]{1,0:T(4,128)} %beta_in.1) | copy-start | bytes 18436
  0.0 3.1 %copy-start.7 = (f32[3,512]{1,0:T(4,128)S(1)}, f32[3,512]{1,0:T(4,128)}, u32[]{:S(2)}) copy-start(f32[3,512]{1,0:T(4,128)} %alpha_mid.1) | copy-start | bytes 18436
  0.0 3.1 %copy-start.8 = (f32[3,512]{1,0:T(4,128)S(1)}, f32[3,512]{1,0:T(4,128)}, u32[]{:S(2)}) copy-start(f32[3,512]{1,0:T(4,128)} %beta_mid.1) | copy-start | bytes 18436
  0.0 4.5 %copy-start = (bf16[3,7,512,512]{3,2,1,0:T(8,128)(2,1)S(1)}, bf16[3,7,512,512]{3,2,1,0:T(8,128)(2,1)}, u32[]{:S(2)}) copy-start(bf16[3,7,512,512]{3,2,1,0:T(8,128)(2,1)} %taps.3) | copy-start | bytes 33030148
  1.2 5.2 %copy-start.1 = (bf16[3,512,512]{2,1,0:T(8,128)(2,1)S(1)}, bf16[3,512,512]{2,1,0:T(8,128)(2,1)}, u32[]{:S(2)}) copy-start(bf16[3,512,512]{2,1,0:T(8,128)(2,1)} %point.3) | copy-start | bytes 4718596
  1.2 4.7 %collective-permute-start = (bf16[48,512]{1,0:T(8,128)(2,1)S(1)}, bf16[48,512]{1,0:T(8,128)(2,1)S(1)}, u32[]{:S(2)}, u32[]{:S(2)}) collective-permute-start(bf16[48,512]{1,0:T(8,128)(2,1)S(1)} %get-tuple-element.19), channel_id=1, source_target_pairs={{0,1},{1,0},{2,3},{3,2},{4,5},{5,4},{6,7},{7,6},{8,9},{9,8},{10,11... | collective-permute-start | bytes 147464 | tf_op jit(solution)/shard_map/ppermute | solution.py:548
  1.9 4.4 %collective-permute-start.1 = (bf16[48,512]{1,0:T(8,128)(2,1)S(1)}, bf16[48,512]{1,0:T(8,128)(2,1)S(1)}, u32[]{:S(2)}, u32[]{:S(2)}) collective-permute-start(bf16[48,512]{1,0:T(8,128)(2,1)S(1)} %get-tuple-element.20), channel_id=1, source_target_pairs={{0,16},{1,2},{2,1},{3,4},{4,3},{5,6},{6,5},{7,8},{8,7},{9,10},{10,... | collective-permute-start | bytes 147464 | tf_op jit(solution)/shard_map/ppermute | solution.py:547

commit v6 on v5

--- a/solution.py
+++ b/solution.py
@@ -62,8 +62,8 @@
     def tile(self, weights, rows, sums):
         register = self.count % 2
         self.count += 1
-        for unit, columns in enumerate(halves(2 * WIDTH)):
-            pltpu.matmul_push_rhs(weights(columns), register, unit)
+        for unit in range(2):
+            pltpu.matmul_push_rhs(weights(unit), register, unit)
         self.flush()
         self.staged = register, rows, sums
 
@@ -73,10 +73,9 @@
         register, rows, sums = self.staged
         self.staged = None
         for i, pair in enumerate(sums):
-            value = rows(i)
             for unit in range(2):
                 load = register if i == 0 else None
-                pltpu.matmul_acc_lhs(pair[unit], value, load_staged_rhs=load)
+                pltpu.matmul_acc_lhs(pair[unit], rows(unit, i), load_staged_rhs=load)
 
 
 class Part:
@@ -153,28 +152,37 @@
             for k in range(KERNEL)
         ]
 
-    def conv_sums(self, matrix, tiles, taps, sums):
+    def conv_sums(self, matrix, tiles, taps, sums, columns=None):
         places, at = [], 0
         for _, length in self.pieces:
             places += range(at, at + length)
             at += length + (0 if self.plain else 6 * self.dilation)
         away = len(places) if self.plain else self.dilation
 
+        both = halves(taps.shape[2])
+
         def rows(k, inputs, i):
             row = (places[i] + k * away) * SEGMENTS
             return tiles[row : row + SEGMENTS, inputs]
 
         def step(k, inputs):
             matrix.tile(
-                lambda columns: taps[self.unit, k, inputs, columns],
-                functools.partial(rows, k, inputs),
+                lambda unit: taps[self.unit, k, inputs, both[unit]],
+                lambda unit, i: rows(k, inputs, i),
                 sums[: len(places)],
             )
 
+        def column_step(k):
+            matrix.tile(
+                lambda unit: taps[self.unit, k, both[unit], columns],
+                lambda unit, i: rows(k, both[unit], i),
+                sums[: len(places)],
+            )
+
+        if columns is not None:
+            return [(1, functools.partial(column_step, k)) for k in range(KERNEL)]
         steps = [
-            (1, functools.partial(step, k, inputs))
-            for k in range(KERNEL)
-            for inputs in halves(taps.shape[2])
+            (1, functools.partial(step, k, inputs)) for k in range(KERNEL) for inputs in both
         ]
         return steps + [(1, matrix.flush)]
 
@@ -203,14 +211,24 @@
 
         return [(20, functools.partial(step, i)) for i in range(self.rows // SEGMENTS)]
 
+    def gate_columns(self, sums, gated, table, columns):
+        def step(i):
+            rows = slice(i * SEGMENTS, (i + 1) * SEGMENTS)
+            values = pltpu.matmul_pop(sums[i][0]) + pltpu.matmul_pop(sums[i][1])
+            gated[rows, columns] = self.gate_values(values, gated, table, columns)
+
+        return [(20, functools.partial(step, i)) for i in range(self.rows // SEGMENTS)]
+
     def project(self, matrix, sources, point, sums):
         def rows(gated, columns, i):
             return gated[i * SEGMENTS : (i + 1) * SEGMENTS, columns]
 
+        both = halves(point.shape[2])
+
         def step(gated, inputs):
             matrix.tile(
-                lambda columns: point[self.unit, inputs, columns],
-                functools.partial(rows, gated, inputs),
+                lambda unit: point[self.unit, inputs, both[unit]],
+                lambda unit, i: rows(gated, inputs, i),
                 sums[: self.rows // SEGMENTS],
             )
 
@@ -254,13 +272,14 @@
 
 
 def weave(main, others=(), own=(), lead=0):
+    pace = 1 if len(main) == KERNEL else 2
     whole = sum(cost for cost, _ in others)
     spent, at = 0, 0
     for i, (_, step) in enumerate(main):
         step()
-        if i // 2 + 1 < len(own):
-            late = own[i // 2 + 1]
-            run(late[: len(late) // 2] if i % 2 == 0 else late[len(late) // 2 :])
+        if i // pace + 1 < len(own):
+            late = own[i // pace + 1]
+            run(late[i % pace :: pace])
         share = max(0, i + 1 - lead) / (len(main) - lead)
         while at < len(others) and (i + 1 == len(main) or spent < whole * share):
             spent += others[at][0]
@@ -355,7 +374,7 @@
     tracks,
     x_first, s_first, first_middle, first_gated, from_chip, from_far, table, taps, point,
     out,
-    x_0, x_1, x_2, s_0, s_1, s_2, inner_tiles, outer_tiles, gated,
+    x_0, x_1, x_2, s_0, s_1, s_2, inner_tiles, outer_tiles, gated, gated_2, held, sems,
 ):
     inner, outer = parts(out.shape[0])
 
@@ -363,24 +382,26 @@
         one = [pltpu.ACC(unit)((SEGMENTS, WIDTH), jnp.float32) for unit in range(2)]
         return [one] * (max(part.rows for part in of) // SEGMENTS)
 
-    def scoped(inner_sums, outer_sums, update_sums):
+    def scoped(inner_sums, outer_sums, last_sums, update_sums):
         outer_body(
             tracks,
             x_first, s_first, first_middle, first_gated, from_chip, from_far, table, taps,
             point, out,
-            x_0, x_1, x_2, s_0, s_1, s_2, inner_tiles, outer_tiles, gated,
-            inner_sums, outer_sums, update_sums,
+            x_0, x_1, x_2, s_0, s_1, s_2, inner_tiles, outer_tiles, gated, gated_2, held, sems,
+            inner_sums, outer_sums, last_sums, update_sums,
         )
 
-    pl.run_scoped(scoped, sums(*inner[1:]), sums(*outer), sums(*inner, *outer))
+    pl.run_scoped(
+        scoped, sums(*inner[1:]), sums(*outer), sums(outer[2]), sums(*inner, *outer)
+    )
 
 
 def outer_body(
     tracks,
     x_first, s_first, first_middle, first_gated, from_chip, from_far, table, taps, point,
     out,
-    x_0, x_1, x_2, s_0, s_1, s_2, inner_tiles, outer_tiles, gated,
-    inner_sums, outer_sums, update_sums,
+    x_0, x_1, x_2, s_0, s_1, s_2, inner_tiles, outer_tiles, gated, gated_2, held, sems,
+    inner_sums, outer_sums, last_sums, update_sums,
 ):
     frames, channels = out.shape
     groups = x_0.shape[0]
@@ -398,10 +419,21 @@
 
         return [(10, functools.partial(step, c)) for c in range(groups)]
 
+    copies = []
+
+    def send(begin, end):
+        def step():
+            rows = pl.ds(begin, end - begin)
+            copy = pltpu.make_async_copy(held.at[rows], out.at[rows], sems.at[len(copies)])
+            copies.append(copy)
+            copy.start()
+
+        return step
+
     def store(begin, end):
         def step(c, row):
             rows = slice(LEFT + row, LEFT + row + SEGMENTS)
-            out[row : row + SEGMENTS, lane(c)] = x_0[c, rows, :].astype(jnp.bfloat16)
+            held[row : row + SEGMENTS, lane(c)] = x_0[c, rows, :].astype(jnp.bfloat16)
 
         return [
             (2, functools.partial(step, c, row))
@@ -476,14 +508,25 @@
     )
     begin = inner[2].pieces[0][0]
     end = begin + inner[2].rows
-    weave(
-        outer[2].conv_sums(matrix, outer_tiles, taps, outer_sums),
-        after(inner[2], inner_sums, x_2, x_0, None) + store(begin, end),
-        coming,
-        lead,
-    )
-    run(after(outer[2], outer_sums, x_2, x_0, None))
-    run(store(0, begin) + store(end, frames))
+    last = outer[2]
+    finish = after(inner[2], inner_sums, x_2, x_0, None) + store(begin, end)
+    finish.append((2, send(begin, end)))
+    cut = len(finish) // 2
+    sums = outer_sums, last_sums
+    conv = [
+        last.conv_sums(matrix, outer_tiles, taps, sums[n], columns)
+        for n, columns in enumerate(both)
+    ]
+    point_steps = last.project(matrix, [(gated_2, columns) for columns in both], point, update_sums)
+    weave(conv[0], finish[:cut], coming, lead)
+    weave(conv[1], finish[cut:] + last.gate_columns(sums[0], gated_2, table, both[0]))
+    run(point_steps[:1])
+    run(last.gate_columns(sums[1], gated_2, table, both[1]))
+    run(point_steps[1:])
+    run(last.finish(update_sums, table, x_2, x_0))
+    run(store(0, begin) + [(2, send(0, begin))] + store(end, frames) + [(2, send(end, frames))])
+    for copy in copies:
+        copy.wait()
 
 
 def swaps(groups, count):
@@ -592,12 +635,15 @@
         functools.partial(outer_kernel, count),
         out_shape=jax.ShapeDtypeStruct((frames, channels), half),
         in_specs=[VMEM] * 9,
-        out_specs=VMEM,
+        out_specs=HBM,
         scratch_shapes=[pltpu.VMEM(natural, single)] * 6
         + [
             pltpu.VMEM(tiles(*inner[1:]), half),
             pltpu.VMEM(tiles(*outer), half),
             pltpu.VMEM(most(*inner, *outer), half),
+            pltpu.VMEM(most(outer[2]), half),
+            pltpu.VMEM((frames, channels), half),
+            pltpu.SemaphoreType.DMA((3,)),
         ],
         compiler_params=pltpu.CompilerParams(vmem_limit_bytes=24 * 2**20),
         name="outer",

time: 13.3 us -> 13.2 us (level)
  no operation moved by 1% of the time
where the time goes in v6:
time: 13.2 us; the launch traced here: 13.1 us
  Pallas kernels  9.81 us (74%)
  starting transfers between devices  1.94 us (15%)
  local copies, waits for them, and re-layouts  0.8 us (6%)
  waiting for transfers between devices  0.42 us (3%)
    pallas_call x1, Pallas kernels, per_device(): pl.pallas_call(functools.partial(outer_kernel, count), out_shape=jax.Shap...  6.76 us
    pallas_call x1, Pallas kernels, per_device(): pl.pallas_call(functools.partial(inner_kernel, frames), out_shape=(jax.Sh...  1.3 us
    ppermute x1, starting transfers between devices, per_device(): from_far = lax.ppermute(to_far, ('grp', 'tm'), far)  1.2 us
    pallas_call x1, Pallas kernels, per_device(): pl.pallas_call(edges_kernel, out_shape=(sent, sent), in_specs=[HBM], out_...  1.09 us
    unnamed x18, local copies, waits for them, and re-layouts  0.8 us
    ppermute x1, starting transfers between devices, per_device(): from_chip = lax.ppermute(to_near, ('grp', 'tm'), near)  0.74 us
    pallas_call x1, Pallas kernels, per_device(): pl.pallas_call(first_kernel, out_shape=(jax.ShapeDtypeStruct(natural, sin...  0.67 us
    ppermute x1, waiting for transfers between devices, per_device(): from_far = lax.ppermute(to_far, ('grp', 'tm'), far)  0.41 us
  transfers between devices with their start and end apart: 2, of which 1 were waited for; matrix products, arithmetic and copies ran while one was open for 0% of the time, Pallas kernels for 15%

profile of v6, /device:TPU:5, one launch (start us, length us, event | category | flops | bytes accessed | tf_op | source)
XLA Modules:
  0.0 13.1 jit_solution(10752060351382550242)
XLA Ops:
  0.0 0.0 copy-start.2
  0.0 0.0 copy-start.3
  0.0 0.0 copy-start.4
  0.0 0.0 copy-start.5
  0.0 0.0 copy-start.6
  0.0 0.0 copy-start.7
  0.0 0.0 copy-start.8
  0.0 0.0 copy-start
  0.1 1.1 %edges.1 = (bf16[48,512]{1,0:T(8,128)(2,1)S(1)}, bf16[48,512]{1,0:T(8,128)(2,1)S(1)}) custom-call(bf16[2,384,512]{2,1,0:T(8,128)(2,1)} %up_hbm.1), custom_call_target="tpu_custom_call" | custom-call | flops 6000000000 | bytes 786432 | tf_op jit(solution)/shard_map/edges/pallas_call | solution.py:574
  1.2 0.0 copy-start.1
  1.2 0.7 %collective-permute-start = (bf16[48,512]{1,0:T(8,128)(2,1)S(1)}, bf16[48,512]{1,0:T(8,128)(2,1)S(1)}, u32[]{:S(2)}, u32[]{:S(2)}) collective-permute-start(bf16[48,512]{1,0:T(8,128)(2,1)S(1)} %get-tuple-element.19), channel_id=1, source_target_pairs={{0,1},{1,0},{2,3},{3,2},{4,5},{5,4},{6,7},{7,6},{8,9},{9,8},{10,11... | collective-permute-start | bytes 147464 | tf_op jit(solution)/shard_map/ppermute | solution.py:591
  1.9 1.2 %collective-permute-start.1 = (bf16[48,512]{1,0:T(8,128)(2,1)S(1)}, bf16[48,512]{1,0:T(8,128)(2,1)S(1)}, u32[]{:S(2)}, u32[]{:S(2)}) collective-permute-start(bf16[48,512]{1,0:T(8,128)(2,1)S(1)} %get-tuple-element.20), channel_id=1, source_target_pairs={{0,16},{1,2},{2,1},{3,4},{4,3},{5,6},{6,5},{7,8},{8,7},{9,10},{10,... | collective-permute-start | bytes 147464 | tf_op jit(solution)/shard_map/ppermute | solution.py:590
  3.1 0.0 copy-done.2
  3.1 0.0 copy-done.3
  3.1 0.0 copy-done.4
  3.1 0.0 copy-done.5
  3.1 0.0 copy-done.6
  3.1 0.0 copy-done.7
  3.1 0.0 copy-done.8
  3.2 0.7 %first.1 = (f32[4,480,128]{2,1,0:T(8,128)S(1)}, f32[4,480,128]{2,1,0:T(8,128)S(1)}, bf16[384,512]{1,0:T(8,128)(2,1)S(1)}, f32[56,512]{1,0:T(8,128)S(1)}) custom-call(bf16[2,384,512]{2,1,0:T(8,128)(2,1)S(1)} %copy-done.2, f32[3,512]{1,0:T(4,128)S(1)} %copy-done.3, f32[3,512]{1,0:T(4,128)S(1)} %copy-done.4, f32[3,512]{1,0:T(4,128)S(1)} %copy-done.5, ...), custom_call_target="tpu_custom_call" | custom-call | tf_op jit(solution)/shard_map/first/pallas_call | solution.py:603
  3.8 0.8 %copy-done = bf16[3,7,512,512]{3,2,1,0:T(8,128)(2,1)S(1)} copy-done((bf16[3,7,512,512]{3,2,1,0:T(8,128)(2,1)S(1)}, bf16[3,7,512,512]{3,2,1,0:T(8,128)(2,1)}, u32[]{:S(2)}) %copy-start) | copy-done | bytes 11010072
  4.6 1.3 %inner.1 = (f32[288,512]{1,0:T(8,128)S(1)}, bf16[288,512]{1,0:T(8,128)(2,1)S(1)}) custom-call(bf16[384,512]{1,0:T(8,128)(2,1)S(1)} %get-tuple-element.15.tiles, f32[56,512]{1,0:T(8,128)S(1)} %get-tuple-element.16.table, bf16[3,7,512,512]{3,2,1,0:T(8,128)(2,1)S(1)} %copy-done), custom_call_target="tpu_custom_call" | custom-call | flops 1056964608 | bytes 11010048 | tf_op jit(solution)/shard_map/inner/pallas_call | solution.py:617
  5.9 0.0 collective-permute-done.from_chip
  5.9 0.4 %collective-permute-done.1.from_far = bf16[48,512]{1,0:T(8,128)(2,1)S(1)} collective-permute-done((bf16[48,512]{1,0:T(8,128)(2,1)S(1)}, bf16[48,512]{1,0:T(8,128)(2,1)S(1)}, u32[]{:S(2)}, u32[]{:S(2)}) %collective-permute-start.1) | collective-permute-done | bytes 49184 | tf_op jit(solution)/shard_map/ppermute | solution.py:590
  6.3 0.0 copy-done.1
  6.3 6.8 %outer.1 = bf16[384,512]{1,0:T(8,128)(2,1)} custom-call(f32[4,480,128]{2,1,0:T(8,128)S(1)} %get-tuple-element.13.x_first, f32[4,480,128]{2,1,0:T(8,128)S(1)} %get-tuple-element.14.s_first, f32[288,512]{1,0:T(8,128)S(1)} %get-tuple-element.17.first_middle, bf16[288,512]{1,0:T(8,128)(2,1)S(1)} %get-tuple-element.18.first_gated, ...), custom_call_target="tpu_custom_call" | custom-call | tf_op jit(solution)/shard_map/outer/pallas_call | solution.py:634
Async XLA Ops:
  0.0 3.1 %copy-start.2 = (bf16[2,384,512]{2,1,0:T(8,128)(2,1)S(1)}, bf16[2,384,512]{2,1,0:T(8,128)(2,1)}, u32[]{:S(2)}) copy-start(bf16[2,384,512]{2,1,0:T(8,128)(2,1)} %up_hbm.1) | copy-start | bytes 2359300
  0.0 3.1 %copy-start.3 = (f32[3,512]{1,0:T(4,128)S(1)}, f32[3,512]{1,0:T(4,128)}, u32[]{:S(2)}) copy-start(f32[3,512]{1,0:T(4,128)} %wide.1) | copy-start | bytes 18436
  0.0 3.1 %copy-start.4 = (f32[3,512]{1,0:T(4,128)S(1)}, f32[3,512]{1,0:T(4,128)}, u32[]{:S(2)}) copy-start(f32[3,512]{1,0:T(4,128)} %point.2) | copy-start | bytes 18436
  0.0 3.1 %copy-start.5 = (f32[3,512]{1,0:T(4,128)S(1)}, f32[3,512]{1,0:T(4,128)}, u32[]{:S(2)}) copy-start(f32[3,512]{1,0:T(4,128)} %alpha_in.1) | copy-start | bytes 18436
  0.0 3.1 %copy-start.6 = (f32[3,512]{1,0:T(4,128)S(1)}, f32[3,512]{1,0:T(4,128)}, u32[]{:S(2)}) copy-start(f32[3,512]{1,0:T(4,128)} %beta_in.1) | copy-start | bytes 18436
  0.0 3.1 %copy-start.7 = (f32[3,512]{1,0:T(4,128)S(1)}, f32[3,512]{1,0:T(4,128)}, u32[]{:S(2)}) copy-start(f32[3,512]{1,0:T(4,128)} %alpha_mid.1) | copy-start | bytes 18436
  0.0 3.1 %copy-start.8 = (f32[3,512]{1,0:T(4,128)S(1)}, f32[3,512]{1,0:T(4,128)}, u32[]{:S(2)}) copy-start(f32[3,512]{1,0:T(4,128)} %beta_mid.1) | copy-start | bytes 18436
  0.0 4.5 %copy-start = (bf16[3,7,512,512]{3,2,1,0:T(8,128)(2,1)S(1)}, bf16[3,7,512,512]{3,2,1,0:T(8,128)(2,1)}, u32[]{:S(2)}) copy-start(bf16[3,7,512,512]{3,2,1,0:T(8,128)(2,1)} %taps.3) | copy-start | bytes 33030148
  1.2 5.2 %copy-start.1 = (bf16[3,512,512]{2,1,0:T(8,128)(2,1)S(1)}, bf16[3,512,512]{2,1,0:T(8,128)(2,1)}, u32[]{:S(2)}) copy-start(bf16[3,512,512]{2,1,0:T(8,128)(2,1)} %point.3) | copy-start | bytes 4718596
  1.2 4.7 %collective-permute-start = (bf16[48,512]{1,0:T(8,128)(2,1)S(1)}, bf16[48,512]{1,0:T(8,128)(2,1)S(1)}, u32[]{:S(2)}, u32[]{:S(2)}) collective-permute-start(bf16[48,512]{1,0:T(8,128)(2,1)S(1)} %get-tuple-element.19), channel_id=1, source_target_pairs={{0,1},{1,0},{2,3},{3,2},{4,5},{5,4},{6,7},{7,6},{8,9},{9,8},{10,11... | collective-permute-start | bytes 147464 | tf_op jit(solution)/shard_map/ppermute | solution.py:591
  1.9 4.4 %collective-permute-start.1 = (bf16[48,512]{1,0:T(8,128)(2,1)S(1)}, bf16[48,512]{1,0:T(8,128)(2,1)S(1)}, u32[]{:S(2)}, u32[]{:S(2)}) collective-permute-start(bf16[48,512]{1,0:T(8,128)(2,1)S(1)} %get-tuple-element.20), channel_id=1, source_target_pairs={{0,16},{1,2},{2,1},{3,4},{4,3},{5,6},{6,5},{7,8},{8,7},{9,10},{10,... | collective-permute-start | bytes 147464 | tf_op jit(solution)/shard_map/ppermute | solution.py:590

commit v7 on v6

--- a/solution.py
+++ b/solution.py
@@ -16,6 +16,7 @@
 LEFT = 48
 SENT = 48
 HALO = 40
+LATE = 64
 SEGMENTS = 16
 TABLE = 16
 IN, MID, WIDE, POINT = 0, 5, 10, 11
@@ -211,6 +212,24 @@
 
         return [(20, functools.partial(step, i)) for i in range(self.rows // SEGMENTS)]
 
+    def finish_plain(self, sums, table, x_rows, out):
+        steps = []
+
+        def step(i, first, j):
+            row = first + SEGMENTS * j
+            for c in range(x_rows.shape[0]):
+                unit, group = divmod(c, WIDTH // LANES)
+                if group == 0:
+                    update = pltpu.matmul_pop(sums[i][unit])
+                change = update[:, lane(group)] + entry(table, self.unit, POINT, lane(c))
+                current = x_rows[c, LEFT + row : LEFT + row + SEGMENTS, :] + change
+                out[row : row + SEGMENTS, lane(c)] = current.astype(jnp.bfloat16)
+
+        for first, length in self.pieces:
+            for j in range(length):
+                steps.append((20, functools.partial(step, len(steps), first, j)))
+        return steps
+
     def gate_columns(self, sums, gated, table, columns):
         def step(i):
             rows = slice(i * SEGMENTS, (i + 1) * SEGMENTS)
@@ -298,12 +317,12 @@
 
 def parts(frames):
     inner = (
-        Part(0, [(8, frames // SEGMENTS - 6)]),
+        Part(0, [(8, frames // SEGMENTS - 5)]),
         Part(1, [(20, frames // SEGMENTS - 7)]),
         Part(2, [(48, frames // SEGMENTS - 11)]),
     )
     outer = (
-        Part(0, [(-36, 3), (frames - 88, 8)]),
+        Part(0, [(-36, 3), (frames - 72, 7)]),
         Part(1, [(-28, 3), (frames - 100, 8)], plain=True),
         Part(2, [(0, 3), (frames - 128, 8)], plain=True),
     )
@@ -358,21 +377,33 @@
         current = rounded(own + jnp.concatenate([none, later[: frames - STRIDE]], axis=0))
         table[UNITS * TABLE :, lane(c)] = later[frames - STRIDE :]
         x_rows[c, LEFT : LEFT + frames, :] = current
-        s_rows[c, LEFT : LEFT + frames, :] = snake_in(table, 0, c, current)
+        early = frames - LATE
+        s_rows[c, LEFT : LEFT + early, :] = snake_in(table, 0, c, current[:early])
     run(sum(parts(frames)[0][0].gather(s_rows, tiles), []))
 
 
-def inner_kernel(frames, tiles, table, taps, middle, gated):
+def inner_kernel(frames, x_first, tiles, table, taps, middle, gated, s_late):
     part = parts(frames)[0][0]
     first, _ = halves(middle.shape[1])
     steps = part.conv(tiles, taps, middle)
-    weave(steps[:KERNEL])
+
+    def late(c, row):
+        start = LEFT + frames - LATE + row
+        values = x_first[c, start : start + SEGMENTS, :]
+        s_late[c, row : row + SEGMENTS, :] = snake_in(table, 0, c, values)
+
+    late_steps = [
+        (1, functools.partial(late, c, row))
+        for c in range(x_first.shape[0])
+        for row in range(0, LATE, SEGMENTS)
+    ]
+    weave(steps[:KERNEL], late_steps)
     weave(steps[KERNEL:], part.gate(middle, gated, table, first))
 
 
 def outer_kernel(
     tracks,
-    x_first, s_first, first_middle, first_gated, from_chip, from_far, table, taps, point,
+    x_first, s_first, s_late, first_middle, first_gated, from_chip, from_far, table, taps, point,
     out,
     x_0, x_1, x_2, s_0, s_1, s_2, inner_tiles, outer_tiles, gated, gated_2, held, sems,
 ):
@@ -385,7 +416,7 @@
     def scoped(inner_sums, outer_sums, last_sums, update_sums):
         outer_body(
             tracks,
-            x_first, s_first, first_middle, first_gated, from_chip, from_far, table, taps,
+            x_first, s_first, s_late, first_middle, first_gated, from_chip, from_far, table, taps,
             point, out,
             x_0, x_1, x_2, s_0, s_1, s_2, inner_tiles, outer_tiles, gated, gated_2, held, sems,
             inner_sums, outer_sums, last_sums, update_sums,
@@ -398,7 +429,7 @@
 
 def outer_body(
     tracks,
-    x_first, s_first, first_middle, first_gated, from_chip, from_far, table, taps, point,
+    x_first, s_first, s_late, first_middle, first_gated, from_chip, from_far, table, taps, point,
     out,
     x_0, x_1, x_2, s_0, s_1, s_2, inner_tiles, outer_tiles, gated, gated_2, held, sems,
     inner_sums, outer_sums, last_sums, update_sums,
@@ -449,6 +480,12 @@
             + part.project(matrix, [(gated, columns) for columns in both], point, update_sums)
             + part.finish(update_sums, table, x_rows, x_next, s_next)
         )
+
+    first_point = inner[0].project(
+        matrix, [(first_gated, both[0]), (gated, both[1])], point, update_sums
+    )
+    run(first_point[:1])
+    matrix.flush()
 
     low_end = LEFT + 2 * STRIDE
     kept = LEFT + outer[0].pieces[1][0] - 8
@@ -467,7 +504,8 @@
         x_0[c, LEFT - HALO : low_end, :] = low
         s_0[c, LEFT - HALO : low_end, :] = snake_in(table, 0, c, low)
         x_0[c, kept:end_row, :] = x_first[c, kept:end_row, :]
-        s_0[c, kept:end_row, :] = s_first[c, kept:end_row, :]
+        s_0[c, kept : end_row - LATE, :] = s_first[c, kept : end_row - LATE, :]
+        s_0[c, end_row - LATE : end_row, :] = s_late[c]
         x_0[c, end_row : end_row + HALO, :] = high
         s_0[c, end_row : end_row + HALO, :] = snake_in(table, 0, c, high)
     run(clear_outside(s_0))
@@ -478,9 +516,7 @@
     weave(
         outer[0].conv_sums(matrix, outer_tiles, taps, outer_sums),
         inner[0].gate(first_middle, gated, table, both[1])
-        + inner[0].project(
-            matrix, [(first_gated, both[0]), (gated, both[1])], point, update_sums
-        )
+        + first_point[1:]
         + inner[0].finish(update_sums, table, x_first, x_1, s_1)
         + coming[0],
         own,
@@ -523,8 +559,10 @@
     run(point_steps[:1])
     run(last.gate_columns(sums[1], gated_2, table, both[1]))
     run(point_steps[1:])
-    run(last.finish(update_sums, table, x_2, x_0))
-    run(store(0, begin) + [(2, send(0, begin))] + store(end, frames) + [(2, send(end, frames))])
+    finish = last.finish_plain(update_sums, table, x_2, held)
+    low_tiles = last.pieces[0][1]
+    run(finish[:low_tiles] + [(2, send(0, begin))])
+    run(finish[low_tiles:] + [(2, send(end, frames))])
     for copy in copies:
         copy.wait()
 
@@ -614,14 +652,15 @@
         name="first",
     )(upsampled, *params)
 
-    first_middle, first_gated = pl.pallas_call(
+    first_middle, first_gated, s_late = pl.pallas_call(
         functools.partial(inner_kernel, frames),
         out_shape=(
             jax.ShapeDtypeStruct(most(inner[0]), single),
             jax.ShapeDtypeStruct(most(inner[0]), half),
+            jax.ShapeDtypeStruct((groups, LATE, LANES), single),
         ),
-        in_specs=[VMEM] * 3,
-        out_specs=(VMEM,) * 2,
+        in_specs=[VMEM] * 4,
+        out_specs=(VMEM,) * 3,
         compiler_params=limit,
         cost_estimate=pl.CostEstimate(
             flops=2 * KERNEL * inner[0].rows * channels**2,
@@ -629,12 +668,12 @@
             transcendentals=0,
         ),
         name="inner",
-    )(first_tiles, table, taps)
+    )(x_first, first_tiles, table, taps)
 
     return pl.pallas_call(
         functools.partial(outer_kernel, count),
         out_shape=jax.ShapeDtypeStruct((frames, channels), half),
-        in_specs=[VMEM] * 9,
+        in_specs=[VMEM] * 10,
         out_specs=HBM,
         scratch_shapes=[pltpu.VMEM(natural, single)] * 6
         + [
@@ -648,7 +687,7 @@
         compiler_params=pltpu.CompilerParams(vmem_limit_bytes=24 * 2**20),
         name="outer",
     )(
-        x_first, s_first, first_middle, first_gated, from_chip, from_far,
+        x_first, s_first, s_late, first_middle, first_gated, from_chip, from_far,
         table, taps, pointwise,
     )
 

time: 13.2 us -> 13.2 us (level)
  no operation moved by 1% of the time
where the time goes in v7:
time: 13.2 us; the launch traced here: 13 us
  Pallas kernels  9.72 us (74%)
  starting transfers between devices  1.94 us (15%)
  local copies, waits for them, and re-layouts  0.88 us (7%)
  waiting for transfers between devices  0.35 us (3%)
    pallas_call x1, Pallas kernels, per_device(): pl.pallas_call(functools.partial(outer_kernel, count), out_shape=jax.Shap...  6.68 us
    pallas_call x1, Pallas kernels, per_device(): pl.pallas_call(functools.partial(inner_kernel, frames), out_shape=(jax.Sh...  1.36 us
    ppermute x1, starting transfers between devices, per_device(): from_far = lax.ppermute(to_far, ('grp', 'tm'), far)  1.2 us
    pallas_call x1, Pallas kernels, per_device(): pl.pallas_call(edges_kernel, out_shape=(sent, sent), in_specs=[HBM], out_...  1.09 us
    unnamed x18, local copies, waits for them, and re-layouts  0.88 us
    ppermute x1, starting transfers between devices, per_device(): from_chip = lax.ppermute(to_near, ('grp', 'tm'), near)  0.74 us
    pallas_call x1, Pallas kernels, per_device(): pl.pallas_call(first_kernel, out_shape=(jax.ShapeDtypeStruct(natural, sin...  0.59 us
    ppermute x1, waiting for transfers between devices, per_device(): from_far = lax.ppermute(to_far, ('grp', 'tm'), far)  0.35 us
  transfers between devices with their start and end apart: 2, of which 1 were waited for; matrix products, arithmetic and copies ran while one was open for 0% of the time, Pallas kernels for 15%

profile of v7, /device:TPU:5, one launch (start us, length us, event | category | flops | bytes accessed | tf_op | source)
XLA Modules:
  0.0 13.0 jit_solution(1377271124404717738)
XLA Ops:
  0.0 0.0 copy-start.2
  0.0 0.0 copy-start.3
  0.0 0.0 copy-start.4
  0.0 0.0 copy-start.5
  0.0 0.0 copy-start.6
  0.0 0.0 copy-start.7
  0.0 0.0 copy-start.8
  0.0 0.0 copy-start
  0.1 1.1 %edges.1 = (bf16[48,512]{1,0:T(8,128)(2,1)S(1)}, bf16[48,512]{1,0:T(8,128)(2,1)S(1)}) custom-call(bf16[2,384,512]{2,1,0:T(8,128)(2,1)} %up_hbm.1), custom_call_target="tpu_custom_call" | custom-call | flops 6000000000 | bytes 786432 | tf_op jit(solution)/shard_map/edges/pallas_call | solution.py:612
  1.2 0.0 copy-start.1
  1.2 0.7 %collective-permute-start = (bf16[48,512]{1,0:T(8,128)(2,1)S(1)}, bf16[48,512]{1,0:T(8,128)(2,1)S(1)}, u32[]{:S(2)}, u32[]{:S(2)}) collective-permute-start(bf16[48,512]{1,0:T(8,128)(2,1)S(1)} %get-tuple-element.21), channel_id=1, source_target_pairs={{0,1},{1,0},{2,3},{3,2},{4,5},{5,4},{6,7},{7,6},{8,9},{9,8},{10,11... | collective-permute-start | bytes 147464 | tf_op jit(solution)/shard_map/ppermute | solution.py:629
  1.9 1.2 %collective-permute-start.1 = (bf16[48,512]{1,0:T(8,128)(2,1)S(1)}, bf16[48,512]{1,0:T(8,128)(2,1)S(1)}, u32[]{:S(2)}, u32[]{:S(2)}) collective-permute-start(bf16[48,512]{1,0:T(8,128)(2,1)S(1)} %get-tuple-element.22), channel_id=1, source_target_pairs={{0,16},{1,2},{2,1},{3,4},{4,3},{5,6},{6,5},{7,8},{8,7},{9,10},{10,... | collective-permute-start | bytes 147464 | tf_op jit(solution)/shard_map/ppermute | solution.py:628
  3.1 0.0 copy-done.2
  3.1 0.0 copy-done.3
  3.1 0.0 copy-done.4
  3.1 0.0 copy-done.5
  3.1 0.0 copy-done.6
  3.1 0.0 copy-done.7
  3.1 0.0 copy-done.8
  3.2 0.6 %first.1 = (f32[4,480,128]{2,1,0:T(8,128)S(1)}, f32[4,480,128]{2,1,0:T(8,128)S(1)}, bf16[400,512]{1,0:T(8,128)(2,1)S(1)}, f32[56,512]{1,0:T(8,128)S(1)}) custom-call(bf16[2,384,512]{2,1,0:T(8,128)(2,1)S(1)} %copy-done.2, f32[3,512]{1,0:T(4,128)S(1)} %copy-done.3, f32[3,512]{1,0:T(4,128)S(1)} %copy-done.4, f32[3,512]{1,0:T(4,128)S(1)} %copy-done.5, ...), custom_call_target="tpu_custom_call" | custom-call | tf_op jit(solution)/shard_map/first/pallas_call | solution.py:641
  3.7 0.8 %copy-done = bf16[3,7,512,512]{3,2,1,0:T(8,128)(2,1)S(1)} copy-done((bf16[3,7,512,512]{3,2,1,0:T(8,128)(2,1)S(1)}, bf16[3,7,512,512]{3,2,1,0:T(8,128)(2,1)}, u32[]{:S(2)}) %copy-start) | copy-done | bytes 11010072
  4.6 1.4 %inner.1 = (f32[304,512]{1,0:T(8,128)S(1)}, bf16[304,512]{1,0:T(8,128)(2,1)S(1)}, f32[4,64,128]{2,1,0:T(8,128)S(1)}) custom-call(f32[4,480,128]{2,1,0:T(8,128)S(1)} %get-tuple-element.14.x_first, bf16[400,512]{1,0:T(8,128)(2,1)S(1)} %get-tuple-element.16.tiles, f32[56,512]{1,0:T(8,128)S(1)} %get-tuple-element.17.table, bf16[3,7,512,512]{3,2,1,0:T(8,128)(2,1)S(1)} %copy-done), custom_call_target="tpu_custom_call" | custom-call | flops 1115684864 | bytes 11010048 | tf_op jit(solution)/shard_map/inner/pallas_call | solution.py:655
  6.0 0.0 collective-permute-done.from_chip
  6.0 0.3 %collective-permute-done.1.from_far = bf16[48,512]{1,0:T(8,128)(2,1)S(1)} collective-permute-done((bf16[48,512]{1,0:T(8,128)(2,1)S(1)}, bf16[48,512]{1,0:T(8,128)(2,1)S(1)}, u32[]{:S(2)}, u32[]{:S(2)}) %collective-permute-start.1) | collective-permute-done | bytes 49184 | tf_op jit(solution)/shard_map/ppermute | solution.py:628
  6.3 0.0 copy-done.1
  6.3 6.7 %outer.1 = bf16[384,512]{1,0:T(8,128)(2,1)} custom-call(f32[4,480,128]{2,1,0:T(8,128)S(1)} %get-tuple-element.14.x_first, f32[4,480,128]{2,1,0:T(8,128)S(1)} %get-tuple-element.15.s_first, f32[4,64,128]{2,1,0:T(8,128)S(1)} %get-tuple-element.18.s_late, f32[304,512]{1,0:T(8,128)S(1)} %get-tuple-element.19.first_middle, ...), custom_call_target="tpu_custom_call" | custom-call | tf_op jit(solution)/shard_map/outer/pallas_call | solution.py:673
Async XLA Ops:
  0.0 3.1 %copy-start.2 = (bf16[2,384,512]{2,1,0:T(8,128)(2,1)S(1)}, bf16[2,384,512]{2,1,0:T(8,128)(2,1)}, u32[]{:S(2)}) copy-start(bf16[2,384,512]{2,1,0:T(8,128)(2,1)} %up_hbm.1) | copy-start | bytes 2359300
  0.0 3.1 %copy-start.3 = (f32[3,512]{1,0:T(4,128)S(1)}, f32[3,512]{1,0:T(4,128)}, u32[]{:S(2)}) copy-start(f32[3,512]{1,0:T(4,128)} %wide.1) | copy-start | bytes 18436
  0.0 3.1 %copy-start.4 = (f32[3,512]{1,0:T(4,128)S(1)}, f32[3,512]{1,0:T(4,128)}, u32[]{:S(2)}) copy-start(f32[3,512]{1,0:T(4,128)} %point.2) | copy-start | bytes 18436
  0.0 3.1 %copy-start.5 = (f32[3,512]{1,0:T(4,128)S(1)}, f32[3,512]{1,0:T(4,128)}, u32[]{:S(2)}) copy-start(f32[3,512]{1,0:T(4,128)} %alpha_in.1) | copy-start | bytes 18436
  0.0 3.1 %copy-start.6 = (f32[3,512]{1,0:T(4,128)S(1)}, f32[3,512]{1,0:T(4,128)}, u32[]{:S(2)}) copy-start(f32[3,512]{1,0:T(4,128)} %beta_in.1) | copy-start | bytes 18436
  0.0 3.1 %copy-start.7 = (f32[3,512]{1,0:T(4,128)S(1)}, f32[3,512]{1,0:T(4,128)}, u32[]{:S(2)}) copy-start(f32[3,512]{1,0:T(4,128)} %alpha_mid.1) | copy-start | bytes 18436
  0.0 3.1 %copy-start.8 = (f32[3,512]{1,0:T(4,128)S(1)}, f32[3,512]{1,0:T(4,128)}, u32[]{:S(2)}) copy-start(f32[3,512]{1,0:T(4,128)} %beta_mid.1) | copy-start | bytes 18436
  0.0 4.5 %copy-start = (bf16[3,7,512,512]{3,2,1,0:T(8,128)(2,1)S(1)}, bf16[3,7,512,512]{3,2,1,0:T(8,128)(2,1)}, u32[]{:S(2)}) copy-start(bf16[3,7,512,512]{3,2,1,0:T(8,128)(2,1)} %taps.3) | copy-start | bytes 33030148
  1.2 5.2 %copy-start.1 = (bf16[3,512,512]{2,1,0:T(8,128)(2,1)S(1)}, bf16[3,512,512]{2,1,0:T(8,128)(2,1)}, u32[]{:S(2)}) copy-start(bf16[3,512,512]{2,1,0:T(8,128)(2,1)} %point.3) | copy-start | bytes 4718596
  1.2 4.8 %collective-permute-start = (bf16[48,512]{1,0:T(8,128)(2,1)S(1)}, bf16[48,512]{1,0:T(8,128)(2,1)S(1)}, u32[]{:S(2)}, u32[]{:S(2)}) collective-permute-start(bf16[48,512]{1,0:T(8,128)(2,1)S(1)} %get-tuple-element.21), channel_id=1, source_target_pairs={{0,1},{1,0},{2,3},{3,2},{4,5},{5,4},{6,7},{7,6},{8,9},{9,8},{10,11... | collective-permute-start | bytes 147464 | tf_op jit(solution)/shard_map/ppermute | solution.py:629
  1.9 4.4 %collective-permute-start.1 = (bf16[48,512]{1,0:T(8,128)(2,1)S(1)}, bf16[48,512]{1,0:T(8,128)(2,1)S(1)}, u32[]{:S(2)}, u32[]{:S(2)}) collective-permute-start(bf16[48,512]{1,0:T(8,128)(2,1)S(1)} %get-tuple-element.22), channel_id=1, source_target_pairs={{0,16},{1,2},{2,1},{3,4},{4,3},{5,6},{6,5},{7,8},{8,7},{9,10},{10,... | collective-permute-start | bytes 147464 | tf_op jit(solution)/shard_map/ppermute | solution.py:628

commit v8 on v7

--- a/solution.py
+++ b/solution.py
@@ -275,7 +275,7 @@
 
         for first, length in self.pieces:
             for j in range(length):
-                cost = 25 if s_next is None else 50
+                cost = 25 if s_next is None else 35
                 steps.append(
                     (cost, functools.partial(step, len(steps), first, j, length))
                 )
@@ -562,7 +562,10 @@
     finish = last.finish_plain(update_sums, table, x_2, held)
     low_tiles = last.pieces[0][1]
     run(finish[:low_tiles] + [(2, send(0, begin))])
-    run(finish[low_tiles:] + [(2, send(end, frames))])
+    middle_tiles = low_tiles + last.pieces[1][1] // 2
+    middle_row = end + last.pieces[1][1] // 2 * SEGMENTS
+    run(finish[low_tiles:middle_tiles] + [(2, send(end, middle_row))])
+    run(finish[middle_tiles:] + [(2, send(middle_row, frames))])
     for copy in copies:
         copy.wait()
 
@@ -682,7 +685,7 @@
             pltpu.VMEM(most(*inner, *outer), half),
             pltpu.VMEM(most(outer[2]), half),
             pltpu.VMEM((frames, channels), half),
-            pltpu.SemaphoreType.DMA((3,)),
+            pltpu.SemaphoreType.DMA((4,)),
         ],
         compiler_params=pltpu.CompilerParams(vmem_limit_bytes=24 * 2**20),
         name="outer",

time: 13.2 us -> 13.2 us (level)
  no operation moved by 1% of the time
where the time goes in v8:
time: 13.2 us; the launch traced here: 13 us
  Pallas kernels  9.74 us (74%)
  starting transfers between devices  1.94 us (15%)
  local copies, waits for them, and re-layouts  0.88 us (7%)
  waiting for transfers between devices  0.35 us (3%)
    pallas_call x1, Pallas kernels, per_device(): pl.pallas_call(functools.partial(outer_kernel, count), out_shape=jax.Shap...  6.7 us
    pallas_call x1, Pallas kernels, per_device(): pl.pallas_call(functools.partial(inner_kernel, frames), out_shape=(jax.Sh...  1.36 us
    ppermute x1, starting transfers between devices, per_device(): from_far = lax.ppermute(to_far, ('grp', 'tm'), far)  1.2 us
    pallas_call x1, Pallas kernels, per_device(): pl.pallas_call(edges_kernel, out_shape=(sent, sent), in_specs=[HBM], out_...  1.09 us
    unnamed x18, local copies, waits for them, and re-layouts  0.88 us
    ppermute x1, starting transfers between devices, per_device(): from_chip = lax.ppermute(to_near, ('grp', 'tm'), near)  0.74 us
    pallas_call x1, Pallas kernels, per_device(): pl.pallas_call(first_kernel, out_shape=(jax.ShapeDtypeStruct(natural, sin...  0.59 us
    ppermute x1, waiting for transfers between devices, per_device(): from_far = lax.ppermute(to_far, ('grp', 'tm'), far)  0.35 us
  transfers between devices with their start and end apart: 2, of which 1 were waited for; matrix products, arithmetic and copies ran while one was open for 0% of the time, Pallas kernels for 15%

profile of v8, /device:TPU:5, one launch (start us, length us, event | category | flops | bytes accessed | tf_op | source)
XLA Modules:
  0.0 13.0 jit_solution(12973951849677906785)
XLA Ops:
  0.0 0.0 copy-start.2
  0.0 0.0 copy-start.3
  0.0 0.0 copy-start.4
  0.0 0.0 copy-start.5
  0.0 0.0 copy-start.6
  0.0 0.0 copy-start.7
  0.0 0.0 copy-start.8
  0.0 0.0 copy-start
  0.1 1.1 %edges.1 = (bf16[48,512]{1,0:T(8,128)(2,1)S(1)}, bf16[48,512]{1,0:T(8,128)(2,1)S(1)}) custom-call(bf16[2,384,512]{2,1,0:T(8,128)(2,1)} %up_hbm.1), custom_call_target="tpu_custom_call" | custom-call | flops 6000000000 | bytes 786432 | tf_op jit(solution)/shard_map/edges/pallas_call | solution.py:615
  1.2 0.0 copy-start.1
  1.2 0.7 %collective-permute-start = (bf16[48,512]{1,0:T(8,128)(2,1)S(1)}, bf16[48,512]{1,0:T(8,128)(2,1)S(1)}, u32[]{:S(2)}, u32[]{:S(2)}) collective-permute-start(bf16[48,512]{1,0:T(8,128)(2,1)S(1)} %get-tuple-element.21), channel_id=1, source_target_pairs={{0,1},{1,0},{2,3},{3,2},{4,5},{5,4},{6,7},{7,6},{8,9},{9,8},{10,11... | collective-permute-start | bytes 147464 | tf_op jit(solution)/shard_map/ppermute | solution.py:632
  1.9 1.2 %collective-permute-start.1 = (bf16[48,512]{1,0:T(8,128)(2,1)S(1)}, bf16[48,512]{1,0:T(8,128)(2,1)S(1)}, u32[]{:S(2)}, u32[]{:S(2)}) collective-permute-start(bf16[48,512]{1,0:T(8,128)(2,1)S(1)} %get-tuple-element.22), channel_id=1, source_target_pairs={{0,16},{1,2},{2,1},{3,4},{4,3},{5,6},{6,5},{7,8},{8,7},{9,10},{10,... | collective-permute-start | bytes 147464 | tf_op jit(solution)/shard_map/ppermute | solution.py:631
  3.1 0.0 copy-done.2
  3.1 0.0 copy-done.3
  3.1 0.0 copy-done.4
  3.1 0.0 copy-done.5
  3.1 0.0 copy-done.6
  3.1 0.0 copy-done.7
  3.1 0.0 copy-done.8
  3.2 0.6 %first.1 = (f32[4,480,128]{2,1,0:T(8,128)S(1)}, f32[4,480,128]{2,1,0:T(8,128)S(1)}, bf16[400,512]{1,0:T(8,128)(2,1)S(1)}, f32[56,512]{1,0:T(8,128)S(1)}) custom-call(bf16[2,384,512]{2,1,0:T(8,128)(2,1)S(1)} %copy-done.2, f32[3,512]{1,0:T(4,128)S(1)} %copy-done.3, f32[3,512]{1,0:T(4,128)S(1)} %copy-done.4, f32[3,512]{1,0:T(4,128)S(1)} %copy-done.5, ...), custom_call_target="tpu_custom_call" | custom-call | tf_op jit(solution)/shard_map/first/pallas_call | solution.py:644
  3.7 0.8 %copy-done = bf16[3,7,512,512]{3,2,1,0:T(8,128)(2,1)S(1)} copy-done((bf16[3,7,512,512]{3,2,1,0:T(8,128)(2,1)S(1)}, bf16[3,7,512,512]{3,2,1,0:T(8,128)(2,1)}, u32[]{:S(2)}) %copy-start) | copy-done | bytes 11010072
  4.6 1.4 %inner.1 = (f32[304,512]{1,0:T(8,128)S(1)}, bf16[304,512]{1,0:T(8,128)(2,1)S(1)}, f32[4,64,128]{2,1,0:T(8,128)S(1)}) custom-call(f32[4,480,128]{2,1,0:T(8,128)S(1)} %get-tuple-element.14.x_first, bf16[400,512]{1,0:T(8,128)(2,1)S(1)} %get-tuple-element.16.tiles, f32[56,512]{1,0:T(8,128)S(1)} %get-tuple-element.17.table, bf16[3,7,512,512]{3,2,1,0:T(8,128)(2,1)S(1)} %copy-done), custom_call_target="tpu_custom_call" | custom-call | flops 1115684864 | bytes 11010048 | tf_op jit(solution)/shard_map/inner/pallas_call | solution.py:658
  6.0 0.0 collective-permute-done.from_chip
  6.0 0.3 %collective-permute-done.1.from_far = bf16[48,512]{1,0:T(8,128)(2,1)S(1)} collective-permute-done((bf16[48,512]{1,0:T(8,128)(2,1)S(1)}, bf16[48,512]{1,0:T(8,128)(2,1)S(1)}, u32[]{:S(2)}, u32[]{:S(2)}) %collective-permute-start.1) | collective-permute-done | bytes 49184 | tf_op jit(solution)/shard_map/ppermute | solution.py:631
  6.3 0.0 copy-done.1
  6.3 6.7 %outer.1 = bf16[384,512]{1,0:T(8,128)(2,1)} custom-call(f32[4,480,128]{2,1,0:T(8,128)S(1)} %get-tuple-element.14.x_first, f32[4,480,128]{2,1,0:T(8,128)S(1)} %get-tuple-element.15.s_first, f32[4,64,128]{2,1,0:T(8,128)S(1)} %get-tuple-element.18.s_late, f32[304,512]{1,0:T(8,128)S(1)} %get-tuple-element.19.first_middle, ...), custom_call_target="tpu_custom_call" | custom-call | tf_op jit(solution)/shard_map/outer/pallas_call | solution.py:676
Async XLA Ops:
  0.0 3.1 %copy-start.2 = (bf16[2,384,512]{2,1,0:T(8,128)(2,1)S(1)}, bf16[2,384,512]{2,1,0:T(8,128)(2,1)}, u32[]{:S(2)}) copy-start(bf16[2,384,512]{2,1,0:T(8,128)(2,1)} %up_hbm.1) | copy-start | bytes 2359300
  0.0 3.1 %copy-start.3 = (f32[3,512]{1,0:T(4,128)S(1)}, f32[3,512]{1,0:T(4,128)}, u32[]{:S(2)}) copy-start(f32[3,512]{1,0:T(4,128)} %wide.1) | copy-start | bytes 18436
  0.0 3.1 %copy-start.4 = (f32[3,512]{1,0:T(4,128)S(1)}, f32[3,512]{1,0:T(4,128)}, u32[]{:S(2)}) copy-start(f32[3,512]{1,0:T(4,128)} %point.2) | copy-start | bytes 18436
  0.0 3.1 %copy-start.5 = (f32[3,512]{1,0:T(4,128)S(1)}, f32[3,512]{1,0:T(4,128)}, u32[]{:S(2)}) copy-start(f32[3,512]{1,0:T(4,128)} %alpha_in.1) | copy-start | bytes 18436
  0.0 3.1 %copy-start.6 = (f32[3,512]{1,0:T(4,128)S(1)}, f32[3,512]{1,0:T(4,128)}, u32[]{:S(2)}) copy-start(f32[3,512]{1,0:T(4,128)} %beta_in.1) | copy-start | bytes 18436
  0.0 3.1 %copy-start.7 = (f32[3,512]{1,0:T(4,128)S(1)}, f32[3,512]{1,0:T(4,128)}, u32[]{:S(2)}) copy-start(f32[3,512]{1,0:T(4,128)} %alpha_mid.1) | copy-start | bytes 18436
  0.0 3.1 %copy-start.8 = (f32[3,512]{1,0:T(4,128)S(1)}, f32[3,512]{1,0:T(4,128)}, u32[]{:S(2)}) copy-start(f32[3,512]{1,0:T(4,128)} %beta_mid.1) | copy-start | bytes 18436
  0.0 4.5 %copy-start = (bf16[3,7,512,512]{3,2,1,0:T(8,128)(2,1)S(1)}, bf16[3,7,512,512]{3,2,1,0:T(8,128)(2,1)}, u32[]{:S(2)}) copy-start(bf16[3,7,512,512]{3,2,1,0:T(8,128)(2,1)} %taps.3) | copy-start | bytes 33030148
  1.2 5.2 %copy-start.1 = (bf16[3,512,512]{2,1,0:T(8,128)(2,1)S(1)}, bf16[3,512,512]{2,1,0:T(8,128)(2,1)}, u32[]{:S(2)}) copy-start(bf16[3,512,512]{2,1,0:T(8,128)(2,1)} %point.3) | copy-start | bytes 4718596
  1.2 4.8 %collective-permute-start = (bf16[48,512]{1,0:T(8,128)(2,1)S(1)}, bf16[48,512]{1,0:T(8,128)(2,1)S(1)}, u32[]{:S(2)}, u32[]{:S(2)}) collective-permute-start(bf16[48,512]{1,0:T(8,128)(2,1)S(1)} %get-tuple-element.21), channel_id=1, source_target_pairs={{0,1},{1,0},{2,3},{3,2},{4,5},{5,4},{6,7},{7,6},{8,9},{9,8},{10,11... | collective-permute-start | bytes 147464 | tf_op jit(solution)/shard_map/ppermute | solution.py:632
  1.9 4.4 %collective-permute-start.1 = (bf16[48,512]{1,0:T(8,128)(2,1)S(1)}, bf16[48,512]{1,0:T(8,128)(2,1)S(1)}, u32[]{:S(2)}, u32[]{:S(2)}) collective-permute-start(bf16[48,512]{1,0:T(8,128)(2,1)S(1)} %get-tuple-element.22), channel_id=1, source_target_pairs={{0,16},{1,2},{2,1},{3,4},{4,3},{5,6},{6,5},{7,8},{8,7},{9,10},{10,... | collective-permute-start | bytes 147464 | tf_op jit(solution)/shard_map/ppermute | solution.py:631
